TPU v7x, 32 devices: a whole 2x2x4 slice. The times are simulated.
32 devices in a mesh: groups: 2 (over x), seq: 16 (over z, y, core).
Axes of the slice: x: 2, y: 2, z: 4, core: 2. Of those that a mesh axis runs over, the one named last changes fastest.
Arguments:
- dec_query: bfloat16 [512, 4096], P(('groups', 'seq')), parts along dimension 0, may hold values from -55 to 55
- ctx_grad: bfloat16 [512, 4096], P(('groups', 'seq')), parts along dimension 0, may hold values from -6 to 6
- dec_segments: int32 [512], P(('groups', 'seq')), parts along dimension 0, may hold values from 0 to 255
- enc_kv: bfloat16 [4096, 2, 4096], P(('groups', 'seq')), parts along dimension 0, may hold values from -6 to 6
- enc_segments: int32 [4096], P(('groups', 'seq')), parts along dimension 0, may hold values from 0 to 255, as said below
- moe_input: bfloat16 [512, 4096], P(('groups', 'seq')), parts along dimension 0, may hold values from -6 to 6
- moe_grad: bfloat16 [512, 4096], P(('groups', 'seq')), parts along dimension 0, may hold values from -6 to 6
- gate_prob: bfloat16 [512], P(('groups', 'seq')), parts along dimension 0, may hold values from 0.19921875 to 1
- expert_ids: int32 [512], P(('groups', 'seq')), parts along dimension 0, may hold values from 0 to 1
- keep_mask: int32 [512], P(('groups', 'seq')), parts along dimension 0, may hold values from 0 to 1
- w_input: bfloat16 [4096, 16384], P(None, 'seq'), may hold values from -0.09375 to 0.09375
- w_output: bfloat16 [16384, 4096], P('seq'), may hold values from -0.0625 to 0.0625
Outputs:
- query_grad: bfloat16 [512, 4096], P(('groups', 'seq')), parts along dimension 0
- kv_grad: bfloat16 [4096, 2, 4096], P(('groups', 'seq')), parts along dimension 0
- moe_input_grad: bfloat16 [512, 4096], P(('groups', 'seq')), parts along dimension 0
- gate_grad: float32 [512], P(('groups', 'seq')), parts along dimension 0
- w_input_grad: bfloat16 [8192, 16384], P('groups', 'seq'), parts along dimension 0
- w_output_grad: bfloat16 [16384, 8192], P('seq', 'groups'), parts along dimension 1
There are 2 independent parts, one for each index of `groups`. A program takes and returns all parts, laid end to end along the dimension named above; an argument that names none is the same for every part. Nothing has to cross between parts.
Inputs may be any that keep to these rules, and one draw needn't show every extreme that they name: `enc_segments`: segment ids never fall along the rows; the encoder rows of a decoder token's document lie within 64 rows beyond the encoder rows of the token's device on either side, and every decoder token's document has two or more encoder rows.
All inputs are finite; a program needn't handle non-finite values.
Results may differ from a plain program's by a relative error of at most 0.0091.
Values may be sent and summed in bfloat16 or wider, within the bound.
No kernel may reach another device: no remote copies, remote signals or barrier semaphores. Data moves between devices by JAX's collectives and lax.ppermute only.
A program may use at most 192 MiB of HBM per device.

v0:
```python
import jax
import jax.numpy as jnp
from jax import lax
from jax.sharding import PartitionSpec as P

D = 4096
HEADS = 32
HEAD_DIM = 128
EXPERTS = 2
ENC_DEV = 128
HALO = 64
CAP = 10


SCALE = 0.125


def with_halo(cells, sides, width):
    for axis, dim in sides:
        count = lax.axis_size(axis)
        ends = count - 1
        head = lax.slice_in_dim(cells, 0, width, axis=dim)
        tail = lax.slice_in_dim(cells, cells.shape[dim] - width, cells.shape[dim], axis=dim)
        cells = jnp.concatenate(
            [
                lax.ppermute(tail, axis, [(i, (i + 1) % count) for i in range(ends)]),
                cells,
                lax.ppermute(head, axis, [((i + 1) % count, i) for i in range(ends)]),
            ],
            axis=dim,
        )
    return cells


def shifted(block, axis, distance):
    devices = range(lax.axis_size(axis))
    route = [(i - distance, i) for i in devices if i - distance in devices]
    return lax.ppermute(block, axis, route)


def attention_grads(dec_query, ctx_grad, dec_segments, ext_kv, ext_rows):
    query_rows = dec_query.shape[0]
    key_rows = ext_kv.shape[0]
    queries = dec_query.reshape(query_rows, HEADS, HEAD_DIM)
    upstream = ctx_grad.reshape(query_rows, HEADS, HEAD_DIM)
    ext_keys = ext_kv[:, 0].reshape(key_rows, HEADS, HEAD_DIM)
    ext_values = ext_kv[:, 1].reshape(key_rows, HEADS, HEAD_DIM)
    allowed = (dec_segments + 1)[:, None] == ext_rows[None, :]
    scores = SCALE * jnp.einsum(
        "qhd,khd->hqk", queries, ext_keys, preferred_element_type=jnp.float32
    )
    scores = jnp.where(allowed[None], scores, -1e30)
    row_peak = jnp.max(scores, axis=2, keepdims=True)
    exp_scores = jnp.exp(scores - row_peak)
    attn_probs = exp_scores / jnp.sum(exp_scores, axis=2, keepdims=True)
    probs_low = attn_probs.astype(jnp.bfloat16)
    context = jnp.einsum("hqk,khd->qhd", probs_low, ext_values, preferred_element_type=jnp.float32)
    row_delta = jnp.sum(upstream.astype(jnp.float32) * context, axis=2)
    prob_grad = jnp.einsum("qhd,khd->hqk", upstream, ext_values, preferred_element_type=jnp.float32)
    score_grad = (attn_probs * (prob_grad - row_delta.T[:, :, None])).astype(jnp.bfloat16)
    query_grad = (
        SCALE * jnp.einsum("hqk,khd->qhd", score_grad, ext_keys, preferred_element_type=jnp.float32)
    ).astype(jnp.bfloat16)
    key_grad = SCALE * jnp.einsum(
        "hqk,qhd->khd", score_grad, queries, preferred_element_type=jnp.float32
    )
    value_grad = jnp.einsum("hqk,qhd->khd", probs_low, upstream, preferred_element_type=jnp.float32)
    ext_grad = jnp.stack(
        [
            key_grad.reshape(key_rows, HEADS * HEAD_DIM),
            value_grad.reshape(key_rows, HEADS * HEAD_DIM),
        ],
        axis=1,
    )
    return (query_grad.reshape(query_rows, HEADS * HEAD_DIM), ext_grad)


def local(
    dec_query,
    ctx_grad,
    dec_segments,
    enc_kv,
    enc_segments,
    moe_input,
    moe_grad,
    gate_prob,
    expert_ids,
    keep_mask,
    w_input,
    w_output,
):
    ext_kv, ext_rows = (
        with_halo(enc_kv, (("seq", 0),), HALO),
        with_halo(enc_segments + 1, (("seq", 0),), HALO),
    )
    query_grad, ext_grad = attention_grads(dec_query, ctx_grad, dec_segments, ext_kv, ext_rows)
    own_grad = ext_grad[HALO : HALO + ENC_DEV]
    from_right = shifted(ext_grad[:HALO].astype(jnp.bfloat16), "seq", -1).astype(jnp.float32)
    from_left = shifted(ext_grad[HALO + ENC_DEV :].astype(jnp.bfloat16), "seq", 1).astype(
        jnp.float32
    )
    own_grad = own_grad.at[ENC_DEV - HALO :].add(from_right).at[:HALO].add(from_left)
    kv_grad = own_grad.astype(jnp.bfloat16)
    devices = lax.axis_size("seq")
    shards = devices // EXPERTS
    choose = (expert_ids[:, None] == jnp.arange(EXPERTS, dtype=jnp.int32)[None, :]) & (
        keep_mask[:, None] == 1
    )
    counts = jnp.cumsum(choose.astype(jnp.int32), axis=0) - 1
    slot_index = jnp.sum(jnp.where(choose, counts, 0), axis=1)
    routed = jnp.any(choose, axis=1) & (slot_index < CAP)
    target = jnp.where(routed, expert_ids * CAP + slot_index, -1)
    dispatch = jnp.arange(EXPERTS * CAP, dtype=jnp.int32)[:, None] == target[None, :]
    dispatch_low = dispatch.astype(jnp.bfloat16)
    sent_input = (
        jnp.dot(dispatch_low, moe_input, preferred_element_type=jnp.float32)
        .astype(jnp.bfloat16)
        .reshape(EXPERTS, CAP, D)
    )
    sent_grad = (
        jnp.dot(dispatch_low, moe_grad, preferred_element_type=jnp.float32)
        .astype(jnp.bfloat16)
        .reshape(EXPERTS, CAP, D)
    )
    sent_gate = (
        jnp.dot(dispatch_low, gate_prob, preferred_element_type=jnp.float32)
        .astype(jnp.bfloat16)
        .reshape(EXPERTS, CAP)
    )
    slot_input, slot_grad, slot_gate = (
        lax.all_to_all(
            jnp.repeat(sent_input, shards, axis=0), "seq", split_axis=0, concat_axis=0, tiled=True
        ),
        lax.all_to_all(
            jnp.repeat(sent_grad, shards, axis=0), "seq", split_axis=0, concat_axis=0, tiled=True
        ),
        lax.all_to_all(
            jnp.repeat(sent_gate, shards, axis=0), "seq", split_axis=0, concat_axis=0, tiled=True
        ),
    )
    slot_rows = devices * CAP
    slot_input = slot_input.reshape(slot_rows, D)
    slot_grad = slot_grad.reshape(slot_rows, D)
    slot_gate = slot_gate.reshape(slot_rows).astype(jnp.float32)
    pre_act = jnp.dot(slot_input, w_input, preferred_element_type=jnp.float32)
    back_hidden = lax.dot_general(
        slot_grad, w_output, (((1,), (1,)), ((), ())), preferred_element_type=jnp.float32
    )
    active = jnp.maximum(pre_act, 0.0)
    hidden_grad = (slot_gate[:, None] * back_hidden * (pre_act > 0)).astype(jnp.bfloat16)
    scaled_hidden = (slot_gate[:, None] * active).astype(jnp.bfloat16)
    w_output_grad = lax.dot_general(
        scaled_hidden, slot_grad, (((0,), (0,)), ((), ())), preferred_element_type=jnp.float32
    ).astype(jnp.bfloat16)
    w_input_grad = lax.dot_general(
        slot_input, hidden_grad, (((0,), (0,)), ((), ())), preferred_element_type=jnp.float32
    ).astype(jnp.bfloat16)
    input_part = lax.dot_general(
        hidden_grad, w_input, (((1,), (1,)), ((), ())), preferred_element_type=jnp.float32
    )
    gate_part = jnp.sum(active * back_hidden, axis=1)
    parts_input, parts_gate = (
        lax.all_to_all(
            input_part.reshape(devices, CAP, D).astype(jnp.bfloat16),
            "seq",
            split_axis=0,
            concat_axis=0,
            tiled=True,
        ).astype(jnp.float32),
        lax.all_to_all(
            gate_part.reshape(devices, CAP).astype(jnp.bfloat16),
            "seq",
            split_axis=0,
            concat_axis=0,
            tiled=True,
        ).astype(jnp.float32),
    )
    back_input = jnp.sum(parts_input.reshape(EXPERTS, shards, CAP, D), axis=1).reshape(
        EXPERTS * CAP, D
    )
    back_gate = jnp.sum(parts_gate.reshape(EXPERTS, shards, CAP), axis=1).reshape(EXPERTS * CAP)
    dispatch_wide = dispatch.astype(jnp.float32)
    moe_input_grad = jnp.dot(dispatch_wide.T, back_input, precision=lax.Precision.HIGHEST).astype(
        jnp.bfloat16
    )
    gate_grad = jnp.dot(dispatch_wide.T, back_gate, precision=lax.Precision.HIGHEST)
    return (query_grad, kv_grad, moe_input_grad, gate_grad, w_input_grad, w_output_grad)


def solution(mesh):
    return jax.shard_map(
        local,
        mesh=mesh,
        in_specs=(
            P(("groups", "seq"), None),
            P(("groups", "seq"), None),
            P(("groups", "seq")),
            P(("groups", "seq"), None, None),
            P(("groups", "seq")),
            P(("groups", "seq"), None),
            P(("groups", "seq"), None),
            P(("groups", "seq")),
            P(("groups", "seq")),
            P(("groups", "seq")),
            P(None, "seq"),
            P("seq", None),
        ),
        out_specs=(
            P(("groups", "seq"), None),
            P(("groups", "seq"), None, None),
            P(("groups", "seq"), None),
            P(("groups", "seq")),
            P("groups", "seq"),
            P("seq", "groups"),
        ),
        check_vma=False,
    )
```

profile of v0, /device:TPU:13, one launch (start us, length us, event | category | flops | bytes accessed | tf_op | source)
XLA Modules:
  0.0 226.4 jit_solution(1328943585046562567)
XLA Ops:
  0.7 3.1 %fusion.56 = (bf16[64,2,4096]{2,1,0:T(2,128)(2,1)S(1)}, bf16[64,2,4096]{2,1,0:T(2,128)(2,1)S(1)}) fusion(bf16[128,2,4096]{2,1,0:T(2,128)(2,1)} %param.19), kind=kLoop, calls=%fused_computation.86 | loop fusion | bytes 4194304 | tf_op jit(solution)/shard_map/slice | solution.py:23
  5.4 2.6 %collective-permute-start.1 = (bf16[64,2,4096]{2,0,1:T(8,128)(2,1)}, bf16[64,2,4096]{2,0,1:T(8,128)(2,1)S(1)}, u32[]{:S(2)}, u32[]{:S(2)}) collective-permute-start(bf16[64,2,4096]{2,0,1:T(8,128)(2,1)} %copy.79), channel_id=1, source_target_pairs={{1,0},{2,1},{3,2},{4,3},{5,4},{6,5},{7,6},{8,7},{9,8},{10,9},{11,1... | collective-permute-start | bytes 3145736 | tf_op jit(solution)/shard_map/ppermute | solution.py:28
  9.6 3.9 %collective-permute-start = (bf16[64,2,4096]{2,0,1:T(8,128)(2,1)}, bf16[64,2,4096]{2,0,1:T(8,128)(2,1)}, u32[]{:S(2)}, u32[]{:S(2)}) collective-permute-start(bf16[64,2,4096]{2,0,1:T(8,128)(2,1)} %copy.78), channel_id=1, source_target_pairs={{0,1},{1,2},{2,3},{3,4},{4,5},{5,6},{6,7},{7,8},{8,9},{9,10},{10,1... | collective-permute-start | bytes 3145736 | tf_op jit(solution)/shard_map/ppermute | solution.py:26
  16.0 4.5 %collective-permute-start.2 = (s32[64]{0:T(128)}, s32[64]{0:T(128)}, u32[]{:S(2)}, u32[]{:S(2)}) collective-permute-start(s32[64]{0:T(128)} %get-tuple-element.40), channel_id=1, source_target_pairs={{0,1},{1,2},{2,3},{3,4},{4,5},{5,6},{6,7},{7,8},{8,9},{9,10},{10,1... | collective-permute-start | bytes 776 | tf_op jit(solution)/shard_map/ppermute | solution.py:26
  21.8 5.0 %all-to-all-start.1 = ((bf16[16,1,10]{2,1,0:T(2,128)(2,1)}), bf16[16,1,10]{2,1,0:T(2,128)(2,1)S(1)}, u32[]{:S(2)}, u32[]{:S(2)}) async-start(bf16[16,1,10]{2,1,0:T(2,128)(2,1)} %copy.72), calls=%async_computation.1 | async-start | bytes 16384 | tf_op jit(solution)/shard_map/all_to_all | solution.py:137
  28.4 4.9 %copy.58 = bf16[128,2,4096]{0,2,1:T(8,128)(2,1)S(1)} copy(bf16[128,2,4096]{2,1,0:T(2,128)(2,1)} %param.19) | data formatting | bytes 4194304 | tf_op args[3]
  39.6 6.0 %all-to-all-start = ((bf16[16,10,4096]{2,1,0:T(8,128)(2,1)}), bf16[16,10,4096]{2,1,0:T(8,128)(2,1)}, u32[]{:S(2)}, u32[]{:S(2)}) async-start(bf16[16,10,4096]{2,1,0:T(8,128)(2,1)} %bitcast.98), calls=%async_computation | async-start | bytes 4194304 | tf_op jit(solution)/shard_map/all_to_all | solution.py:131
  47.5 2.7 %copy.57 = bf16[64,2,4096]{0,2,1:T(8,128)(2,1)} copy(bf16[64,2,4096]{2,0,1:T(8,128)(2,1)} %collective-permute-done) | data formatting | bytes 2097152 | tf_op jit(solution)/shard_map/ppermute | solution.py:26
  50.3 4.2 %pad_maximum_fusion.1 = bf16[256,2,4096]{0,2,1:T(8,128)(2,1)S(1)} fusion(bf16[64,2,4096]{0,2,1:T(8,128)(2,1)} %copy.59, bf16[128,2,4096]{0,2,1:T(8,128)(2,1)S(1)} %copy.58, bf16[64,2,4096]{0,2,1:T(8,128)(2,1)} %copy.57), kind=kLoop, calls=%fused_computation.14 | loop fusion | flops 12582912 | bytes 8388608 | tf_op jit(solution)/shard_map/concatenate | solution.py:24
  57.5 2.6 %fusion.15 = f32[16,32]{0,1:T(8,128)S(1)} fusion(bf16[256,32,128]{0,2,1:T(8,128)(2,1)} %bitcast.100, f32[32,16]{1,0:T(8,128)S(1)} %get-tuple-element.42, f32[32,16,256]{2,1,0:T(8,128)S(1)} %fusion.10, pred[16,256]{1,0:T(8,128)(4,1)S(1)} %copy-done.12, bf16[16,4096]{1,0:T(8,128)(2,1)S(1)} %copy-done), kind=kOutput, calls=%fused_computation.34 | convolution fusion | flops 34275584 | bytes 2760704 | tf_op jit(solution)/shard_map/hqk,khd->qhd/dot_general | solution.py:57
  62.2 2.8 %convolution_multiply_fusion = f32[32,256,128]{1,2,0:T(8,128)} fusion(bf16[32,16,256]{2,1,0:T(8,128)(2,1)S(1)} %fusion.12, bf16[16,4096]{1,0:T(8,128)(2,1)S(1)} %copy-done.9), kind=kOutput, calls=%fused_computation.16 | convolution fusion | flops 34603008 | bytes 4587520 | tf_op jit(solution)/shard_map/hqk,qhd->khd/dot_general | solution.py:64
  64.9 10.1 %copy.70 = f32[256,1,4096]{2,1,0:T(1,128)} copy(f32[256,1,4096]{0,2,1:T(8,128)} %bitcast.97) | data formatting | bytes 8388608 | tf_op jit(solution)/shard_map/stack;reshape | solution.py:68
  75.1 3.3 %fusion.24 = f32[32,256,128]{1,2,0:T(8,128)} fusion(f32[32,16]{1,0:T(8,128)S(1)} %get-tuple-element.42, f32[32,16,256]{2,1,0:T(8,128)S(1)} %fusion.10, pred[16,256]{1,0:T(8,128)(4,1)S(1)} %copy-done.12, bf16[16,4096]{1,0:T(8,128)(2,1)S(1)} %copy-done), kind=kOutput, calls=%fused_computation.51 | convolution fusion | flops 34079488 | bytes 4855808 | tf_op jit(solution)/shard_map/hqk,qhd->khd/dot_general | solution.py:67
  78.4 10.2 %copy.71 = f32[256,1,4096]{2,1,0:T(1,128)} copy(f32[256,1,4096]{0,2,1:T(8,128)} %bitcast.96) | data formatting | bytes 8388608 | tf_op jit(solution)/shard_map/stack;reshape | solution.py:68
  88.6 4.5 %all-to-all-done = bf16[16,10,4096]{2,1,0:T(8,128)(2,1)} async-done(((bf16[16,10,4096]{2,1,0:T(8,128)(2,1)}), bf16[16,10,4096]{2,1,0:T(8,128)(2,1)}, u32[]{:S(2)}, u32[]{:S(2)}) %all-to-all-start) | async-done | bytes 1310752 | tf_op jit(solution)/shard_map/all_to_all | solution.py:131
  94.7 4.9 %all-to-all-start.2 = ((bf16[16,10,4096]{2,1,0:T(8,128)(2,1)}), bf16[16,10,4096]{2,1,0:T(8,128)(2,1)}, u32[]{:S(2)}, u32[]{:S(2)}) async-start(bf16[16,10,4096]{2,1,0:T(8,128)(2,1)} %bitcast.99), calls=%async_computation.2 | async-start | bytes 4194304 | tf_op jit(solution)/shard_map/all_to_all | solution.py:134
  99.6 9.3 %fusion.1 = bf16[256,2,4096]{2,1,0:T(2,128)(2,1)S(1)} fusion(f32[256,1,4096]{2,1,0:T(1,128)} %copy.71, f32[256,1,4096]{2,1,0:T(1,128)} %copy.70), kind=kLoop, calls=%fused_computation.6 | loop fusion | flops 8388608 | bytes 12582912 | tf_op jit(solution)/shard_map/convert.4
  110.3 2.9 %fusion.54 = (bf16[64,2,4096]{2,1,0:T(2,128)(2,1)}, bf16[64,2,4096]{2,1,0:T(2,128)(2,1)}) fusion(bf16[256,2,4096]{2,1,0:T(2,128)(2,1)S(1)} %fusion.1), kind=kLoop, calls=%fused_computation.84 | loop fusion | bytes 4194304 | tf_op jit(solution)/shard_map/slice | solution.py:99
  115.4 4.2 %collective-permute-start.5 = (bf16[64,2,4096]{2,1,0:T(2,128)(2,1)}, bf16[64,2,4096]{2,1,0:T(2,128)(2,1)}, u32[]{:S(2)}, u32[]{:S(2)}) collective-permute-start(bf16[64,2,4096]{2,1,0:T(2,128)(2,1)} %get-tuple-element.30), channel_id=1, source_target_pairs={{0,1},{1,2},{2,3},{3,4},{4,5},{5,6},{6,7},{7,8},{8,9},{9,10},{10,1... | collective-permute-start | bytes 3145736 | tf_op jit(solution)/shard_map/ppermute | solution.py:38
  119.7 5.1 %fusion.2 = f32[128,2,4096]{2,1,0:T(2,128)} fusion(f32[256,1,4096]{2,1,0:T(1,128)S(1)} %copy-done.2, f32[256,1,4096]{2,1,0:T(1,128)S(1)} %copy-done.3), kind=kLoop, calls=%fused_computation.13 | loop fusion | flops 1048576 | bytes 12582912 | tf_op jit(solution)/shard_map/stack | solution.py:68
  126.6 4.9 %fusion.59 = f32[160,1024]{1,0:T(8,128)S(1)} fusion(bf16[160,4096]{1,0:T(8,128)(2,1)S(1)} %reshape.186, bf16[4096,1024]{1,0:T(8,128)(2,1)} %param.26), kind=kOutput, calls=%fused_computation.89 | convolution fusion | flops 1342177280 | bytes 10354688 | tf_op jit(solution)/shard_map/dot_general | solution.py:145
  131.5 17.1 %all-to-all-done.2 = bf16[16,10,4096]{2,1,0:T(8,128)(2,1)} async-done(((bf16[16,10,4096]{2,1,0:T(8,128)(2,1)}), bf16[16,10,4096]{2,1,0:T(8,128)(2,1)}, u32[]{:S(2)}, u32[]{:S(2)}) %all-to-all-start.2) | async-done | bytes 1310752 | tf_op jit(solution)/shard_map/all_to_all | solution.py:134
  150.4 7.7 %multiply_reduce_fusion = (bf16[160]{0:T(256)(128)(2,1)S(1)}, bf16[160,1024]{1,0:T(8,128)(2,1)}) fusion(f32[160,1024]{1,0:T(8,128)S(1)} %fusion.59, f32[160]{0:T(256)S(1)} %reshape.195, bf16[160,4096]{1,0:T(8,128)(2,1)S(1)} %reshape.190, bf16[1024,4096]{1,0:T(8,128)(2,1)} %param.27), kind=kOutput, calls=%fused_computation.40 | convolution fusion | flops 1343324032 | bytes 10683328 | tf_op jit(solution)/shard_map/dot_general | solution.py:146
  158.8 4.9 %all-to-all-start.4 = ((bf16[16,1,10]{2,1,0:T(2,128)(2,1)}), bf16[16,1,10]{2,1,0:T(2,128)(2,1)S(1)}, u32[]{:S(2)}, u32[]{:S(2)}) async-start(bf16[16,1,10]{2,1,0:T(2,128)(2,1)} %convert_element_type.124), calls=%async_computation.4 | async-start | bytes 16384 | tf_op jit(solution)/shard_map/all_to_all | solution.py:170
  163.6 6.4 %convolution_convert_fusion.2 = bf16[160,4096]{1,0:T(8,128)(2,1)S(1)} fusion(bf16[160,1024]{1,0:T(8,128)(2,1)} %get-tuple-element.37, bf16[4096,1024]{1,0:T(8,128)(2,1)} %param.26), kind=kOutput, calls=%fused_computation.9 | convolution fusion | flops 1342832640 | bytes 10027008 | tf_op jit(solution)/shard_map/dot_general | solution.py:158
  171.6 6.0 %all-to-all-start.3 = ((bf16[16,10,4096]{2,1,0:T(8,128)(2,1)}), bf16[16,10,4096]{2,1,0:T(8,128)(2,1)S(1)}, u32[]{:S(2)}, u32[]{:S(2)}) async-start(bf16[16,10,4096]{2,1,0:T(8,128)(2,1)} %convert_element_type.113), calls=%async_computation.3 | async-start | bytes 4194304 | tf_op jit(solution)/shard_map/all_to_all | solution.py:163
  177.6 5.3 %fusion.6 = f32[128,2,4096]{2,1,0:T(2,128)} fusion(f32[128,2,4096]{2,1,0:T(2,128)} %fusion.2, bf16[64,2,4096]{2,1,0:T(2,128)(2,1)} %collective-permute-done.4, f32[256,1,4096]{2,1,0:T(1,128)} %copy.71, f32[256,1,4096]{2,1,0:T(1,128)} %copy.70), kind=kLoop, calls=%fused_computation.21 | loop fusion | flops 1572864 | bytes 11534336 | tf_op jit(solution)/shard_map/scatter-add | solution.py:102
  182.9 5.1 %fusion.5 = f32[128,2,4096]{2,1,0:T(2,128)} fusion(f32[128,2,4096]{2,1,0:T(2,128)} %fusion.6, bf16[64,2,4096]{2,1,0:T(2,128)(2,1)} %collective-permute-done.5), kind=kLoop, calls=%fused_computation.20 | loop fusion | flops 1048576 | bytes 5242880 | tf_op jit(solution)/shard_map/scatter-add | solution.py:102
  188.0 5.5 %convert_element_type.104 = bf16[128,2,4096]{2,1,0:T(2,128)(2,1)} convert(f32[128,2,4096]{2,1,0:T(2,128)} %fusion.5) | non-fusion elementwise | flops 1048576 | bytes 6291456 | tf_op jit(solution)/shard_map/convert_element_type | solution.py:103
  193.6 5.8 %convolution_convert_fusion.1 = bf16[4096,1024]{1,0:T(8,128)(2,1)} fusion(bf16[160,4096]{1,0:T(8,128)(2,1)S(1)} %reshape.186, bf16[160,1024]{1,0:T(8,128)(2,1)S(1)} %copy-done.8), kind=kOutput, calls=%fused_computation.8 | convolution fusion | flops 1346371584 | bytes 10027008 | tf_op jit(solution)/shard_map/dot_general | solution.py:155
  199.4 5.9 %convolution_convert_fusion = bf16[1024,4096]{1,0:T(8,128)(2,1)} fusion(bf16[160,4096]{1,0:T(8,128)(2,1)S(1)} %copy-done.5, f32[160,1024]{1,0:T(8,128)S(1)} %copy-done.7, f32[160]{0:T(256)S(1)} %copy-done.14), kind=kOutput, calls=%fused_computation.7 | convolution fusion | flops 1346863104 | bytes 10355328 | tf_op jit(solution)/shard_map/dot_general | solution.py:152
  206.1 19.0 %all-to-all-done.3 = bf16[16,10,4096]{2,1,0:T(8,128)(2,1)S(1)} async-done(((bf16[16,10,4096]{2,1,0:T(8,128)(2,1)}), bf16[16,10,4096]{2,1,0:T(8,128)(2,1)S(1)}, u32[]{:S(2)}, u32[]{:S(2)}) %all-to-all-start.3) | async-done | bytes 1310752 | tf_op jit(solution)/shard_map/all_to_all | solution.py:163
  (96 shorter events, 34.9 us)
Async XLA Ops:
  0.6 56.8 %copy-start = (bf16[16,4096]{1,0:T(8,128)(2,1)S(1)}, bf16[16,4096]{1,0:T(8,128)(2,1)}, u32[]{:S(2)}) copy-start(bf16[16,4096]{1,0:T(8,128)(2,1)} %param.17) | copy-start | bytes 393220
  0.7 12.8 %copy-start.18 = (s32[128]{0:T(128)S(1)}, s32[128]{0:T(128)}, u32[]{:S(2)}) copy-start(s32[128]{0:T(128)} %param.20) | copy-start | bytes 1540
  0.7 19.9 %copy-start.19 = (s32[16]{0:T(128)S(1)}, s32[16]{0:T(128)}, u32[]{:S(2)}) copy-start(s32[16]{0:T(128)} %param.25) | copy-start | bytes 196
  0.7 19.9 %copy-start.17 = (s32[16]{0:T(128)S(1)}, s32[16]{0:T(128)}, u32[]{:S(2)}) copy-start(s32[16]{0:T(128)} %param.24) | copy-start | bytes 196
  0.7 20.3 %copy-start.20 = (bf16[16]{0:T(256)(128)(2,1)S(1)}, bf16[16]{0:T(256)(128)(2,1)}, u32[]{:S(2)}) copy-start(bf16[16]{0:T(256)(128)(2,1)} %param.23) | copy-start | bytes 100
  0.7 26.1 %copy-start.10 = (bf16[16,4096]{1,0:T(8,128)(2,1)S(1)}, bf16[16,4096]{1,0:T(8,128)(2,1)}, u32[]{:S(2)}) copy-start(bf16[16,4096]{1,0:T(8,128)(2,1)} %param.21) | copy-start | bytes 393220
  0.7 26.3 %copy-start.11 = (bf16[16,4096]{1,0:T(8,128)(2,1)S(1)}, bf16[16,4096]{1,0:T(8,128)(2,1)}, u32[]{:S(2)}) copy-start(bf16[16,4096]{1,0:T(8,128)(2,1)} %param.22) | copy-start | bytes 393220
  0.7 27.2 %copy-start.21 = (s32[16]{0:T(128)S(1)}, s32[16]{0:T(128)}, u32[]{:S(2)}) copy-start(s32[16]{0:T(128)} %param.18) | copy-start | bytes 196
  5.4 40.3 %collective-permute-start.1 = (bf16[64,2,4096]{2,0,1:T(8,128)(2,1)}, bf16[64,2,4096]{2,0,1:T(8,128)(2,1)S(1)}, u32[]{:S(2)}, u32[]{:S(2)}) collective-permute-start(bf16[64,2,4096]{2,0,1:T(8,128)(2,1)} %copy.79), channel_id=1, source_target_pairs={{1,0},{2,1},{3,2},{4,3},{5,4},{6,5},{7,6},{8,7},{9,8},{10,9},{11,1... | collective-permute-start | bytes 3145736 | tf_op jit(solution)/shard_map/ppermute | solution.py:28
  9.6 38.0 %collective-permute-start = (bf16[64,2,4096]{2,0,1:T(8,128)(2,1)}, bf16[64,2,4096]{2,0,1:T(8,128)(2,1)}, u32[]{:S(2)}, u32[]{:S(2)}) collective-permute-start(bf16[64,2,4096]{2,0,1:T(8,128)(2,1)} %copy.78), channel_id=1, source_target_pairs={{0,1},{1,2},{2,3},{3,4},{4,5},{5,6},{6,7},{7,8},{8,9},{9,10},{10,1... | collective-permute-start | bytes 3145736 | tf_op jit(solution)/shard_map/ppermute | solution.py:26
  14.0 21.0 %collective-permute-start.3 = (s32[64]{0:T(128)}, s32[64]{0:T(128)S(1)}, u32[]{:S(2)}, u32[]{:S(2)}) collective-permute-start(s32[64]{0:T(128)} %get-tuple-element.41), channel_id=1, source_target_pairs={{1,0},{2,1},{3,2},{4,3},{5,4},{6,5},{7,6},{8,7},{9,8},{10,9},{11,1... | collective-permute-start | bytes 776 | tf_op jit(solution)/shard_map/ppermute | solution.py:28
  16.0 19.1 %collective-permute-start.2 = (s32[64]{0:T(128)}, s32[64]{0:T(128)}, u32[]{:S(2)}, u32[]{:S(2)}) collective-permute-start(s32[64]{0:T(128)} %get-tuple-element.40), channel_id=1, source_target_pairs={{0,1},{1,2},{2,3},{3,4},{4,5},{5,6},{6,7},{7,8},{8,9},{9,10},{10,1... | collective-permute-start | bytes 776 | tf_op jit(solution)/shard_map/ppermute | solution.py:26
  21.0 12.4 %copy-start.15 = (s32[16]{0:T(128)}, s32[16]{0:T(128)S(1)}, u32[]{:S(2)}) copy-start(s32[16]{0:T(128)S(1)} %and_select_fusion) | copy-start | bytes 196
  21.8 15.3 %all-to-all-start.1 = ((bf16[16,1,10]{2,1,0:T(2,128)(2,1)}), bf16[16,1,10]{2,1,0:T(2,128)(2,1)S(1)}, u32[]{:S(2)}, u32[]{:S(2)}) async-start(bf16[16,1,10]{2,1,0:T(2,128)(2,1)} %copy.72), calls=%async_computation.1 | async-start | bytes 16384 | tf_op jit(solution)/shard_map/all_to_all | solution.py:137
  39.6 53.5 %all-to-all-start = ((bf16[16,10,4096]{2,1,0:T(8,128)(2,1)}), bf16[16,10,4096]{2,1,0:T(8,128)(2,1)}, u32[]{:S(2)}, u32[]{:S(2)}) async-start(bf16[16,10,4096]{2,1,0:T(8,128)(2,1)} %bitcast.98), calls=%async_computation | async-start | bytes 4194304 | tf_op jit(solution)/shard_map/all_to_all | solution.py:131
  45.8 104.6 %copy-start.13 = (f32[160]{0:T(256)}, f32[160]{0:T(256)S(1)}, u32[]{:S(2)}) copy-start(f32[160]{0:T(256)S(1)} %reshape.195) | copy-start | bytes 1924
  54.5 2.0 copy-start.12
  94.7 53.9 %all-to-all-start.2 = ((bf16[16,10,4096]{2,1,0:T(8,128)(2,1)}), bf16[16,10,4096]{2,1,0:T(8,128)(2,1)}, u32[]{:S(2)}, u32[]{:S(2)}) async-start(bf16[16,10,4096]{2,1,0:T(8,128)(2,1)} %bitcast.99), calls=%async_computation.2 | async-start | bytes 4194304 | tf_op jit(solution)/shard_map/all_to_all | solution.py:134
  99.6 20.0 %copy-start.3 = (f32[256,1,4096]{2,1,0:T(1,128)S(1)}, f32[256,1,4096]{2,1,0:T(1,128)}, u32[]{:S(2)}) copy-start(f32[256,1,4096]{2,1,0:T(1,128)} %copy.71) | copy-start | bytes 12582916
  109.0 10.7 %copy-start.2 = (f32[256,1,4096]{2,1,0:T(1,128)S(1)}, f32[256,1,4096]{2,1,0:T(1,128)}, u32[]{:S(2)}) copy-start(f32[256,1,4096]{2,1,0:T(1,128)} %copy.70) | copy-start | bytes 12582916
  113.2 64.5 %collective-permute-start.4 = (bf16[64,2,4096]{2,1,0:T(2,128)(2,1)}, bf16[64,2,4096]{2,1,0:T(2,128)(2,1)}, u32[]{:S(2)}, u32[]{:S(2)}) collective-permute-start(bf16[64,2,4096]{2,1,0:T(2,128)(2,1)} %get-tuple-element.31), channel_id=1, source_target_pairs={{1,0},{2,1},{3,2},{4,3},{5,4},{6,5},{7,6},{8,7},{9,8},{10,9},{11,1... | collective-permute-start | bytes 3145736 | tf_op jit(solution)/shard_map/ppermute | solution.py:38
  115.4 67.5 %collective-permute-start.5 = (bf16[64,2,4096]{2,1,0:T(2,128)(2,1)}, bf16[64,2,4096]{2,1,0:T(2,128)(2,1)}, u32[]{:S(2)}, u32[]{:S(2)}) collective-permute-start(bf16[64,2,4096]{2,1,0:T(2,128)(2,1)} %get-tuple-element.30), channel_id=1, source_target_pairs={{0,1},{1,2},{2,3},{3,4},{4,5},{5,6},{6,7},{7,8},{8,9},{9,10},{10,1... | collective-permute-start | bytes 3145736 | tf_op jit(solution)/shard_map/ppermute | solution.py:38
  131.5 26.6 %copy-start.6 = (f32[160,1024]{1,0:T(8,128)}, f32[160,1024]{1,0:T(8,128)S(1)}, u32[]{:S(2)}) copy-start(f32[160,1024]{1,0:T(8,128)S(1)} %fusion.59) | copy-start | bytes 1966084
  150.4 7.7 %copy-start.4 = (bf16[160,4096]{1,0:T(8,128)(2,1)}, bf16[160,4096]{1,0:T(8,128)(2,1)S(1)}, u32[]{:S(2)}) copy-start(bf16[160,4096]{1,0:T(8,128)(2,1)S(1)} %reshape.190) | copy-start | bytes 3932164
  158.8 12.8 %all-to-all-start.4 = ((bf16[16,1,10]{2,1,0:T(2,128)(2,1)}), bf16[16,1,10]{2,1,0:T(2,128)(2,1)S(1)}, u32[]{:S(2)}, u32[]{:S(2)}) async-start(bf16[16,1,10]{2,1,0:T(2,128)(2,1)} %convert_element_type.124), calls=%async_computation.4 | async-start | bytes 16384 | tf_op jit(solution)/shard_map/all_to_all | solution.py:170
  171.6 53.4 %all-to-all-start.3 = ((bf16[16,10,4096]{2,1,0:T(8,128)(2,1)}), bf16[16,10,4096]{2,1,0:T(8,128)(2,1)S(1)}, u32[]{:S(2)}, u32[]{:S(2)}) async-start(bf16[16,10,4096]{2,1,0:T(8,128)(2,1)} %convert_element_type.113), calls=%async_computation.3 | async-start | bytes 4194304 | tf_op jit(solution)/shard_map/all_to_all | solution.py:163
  188.0 5.5 %copy-start.8 = (bf16[160,1024]{1,0:T(8,128)(2,1)S(1)}, bf16[160,1024]{1,0:T(8,128)(2,1)}, u32[]{:S(2)}) copy-start(bf16[160,1024]{1,0:T(8,128)(2,1)} %get-tuple-element.37) | copy-start | bytes 983044
  193.5 5.8 %copy-start.5 = (bf16[160,4096]{1,0:T(8,128)(2,1)S(1)}, bf16[160,4096]{1,0:T(8,128)(2,1)}, u32[]{:S(2)}) copy-start(bf16[160,4096]{1,0:T(8,128)(2,1)} %copy-done.4) | copy-start | bytes 3932164
  193.6 5.8 %copy-start.7 = (f32[160,1024]{1,0:T(8,128)S(1)}, f32[160,1024]{1,0:T(8,128)}, u32[]{:S(2)}) copy-start(f32[160,1024]{1,0:T(8,128)} %copy-done.6) | copy-start | bytes 1966084
  193.6 5.8 %copy-start.14 = (f32[160]{0:T(256)S(1)}, f32[160]{0:T(256)}, u32[]{:S(2)}) copy-start(f32[160]{0:T(256)} %copy-done.13) | copy-start | bytes 1924
  199.4 6.0 %copy-start.16 = (s32[16]{0:T(128)S(1)}, s32[16]{0:T(128)}, u32[]{:S(2)}) copy-start(s32[16]{0:T(128)} %copy-done.15) | copy-start | bytes 196
  199.4 27.1 %copy-start.1 = (bf16[16,4096]{1,0:T(8,128)(2,1)S(1)}, bf16[16,4096]{1,0:T(8,128)(2,1)}, u32[]{:S(2)}) copy-start(bf16[16,4096]{1,0:T(8,128)(2,1)} %param.17) | copy-start | bytes 393220
  (1 other events, 1.6 us)
where the time goes:
time: 228 us; the launch traced here: 226 us
  local copies, waits for them, and re-layouts  54.3 us (24%)
  starting transfers between devices  46.1 us (20%)
  matrix products  45.3 us (20%)
  waiting for transfers between devices  40.6 us (18%)
  other arithmetic  38.9 us (17%)
    another operation x2, local copies, waits for them, and re-layouts, attention_grads(): jnp.stack([key_grad.reshape(key_rows, HEADS * HEAD_DIM), value_grad.resha...  20.3 us
    all_to_all x1, waiting for transfers between devices, local(): lax.all_to_all(input_part.reshape(devices, CAP, D).astype(jnp.bfloat16),...  19 us
    all_to_all x1, waiting for transfers between devices, local(): lax.all_to_all(jnp.repeat(sent_grad, shards, axis=0), 'seq', split_axis=0...  17.1 us
    scatter-add x2, other arithmetic, local(): own_grad.at[ENC_DEV - HALO:].add(from_right).at[:HALO].add(from_left)  10.4 us
    another operation x1, other arithmetic  9.33 us
    ppermute x2, starting transfers between devices, with_halo(): lax.ppermute(tail, axis, [(i, (i + 1) % count) for i in range(ends)])  8.41 us
    unnamed x47, local copies, waits for them, and re-layouts  8.1 us
    dot_general x1, matrix products, local(): lax.dot_general(slot_grad, w_output, (((1,), (1,)), ((), ())), preferred_...  7.67 us
  transfers between devices with their start and end apart: 11, of which 3 were waited for; matrix products, arithmetic and copies ran while one was open for 58% of the time, Pallas kernels for 0%

commit v1 on v0

v1 whole, which is shorter than its diff:
```python
import functools

import jax
import jax.numpy as jnp
from jax import lax
from jax.experimental import pallas as pl
from jax.experimental.pallas import tpu as pltpu
from jax.sharding import PartitionSpec as P

D = 4096
HEADS = 32
HEAD_DIM = 128
EXPERTS = 2
CAP = 10
SCALE = 0.125
NONE = -1e30
LANES = 128
BLOCK = 24
GATE_ROW = 20


def iota(shape, dim):
    return lax.broadcasted_iota(jnp.int32, shape, dim)


def one_hot(mask):
    return jnp.where(mask, 1.0, 0.0).astype(jnp.bfloat16)


def mm(a, b, dims=((1,), (0,))):
    return lax.dot_general(a, b, (dims, ((), ())), preferred_element_type=jnp.float32)


def slots_of(ids, keep, expert):
    tokens = ids.shape[1]
    row, col = iota((tokens, tokens), 0), iota((tokens, tokens), 1)
    chosen = (ids == expert) & (keep == 1)
    chosen_f = jnp.where(chosen, 1.0, 0.0)
    as_column = jnp.sum(jnp.where(row == col, chosen_f, 0.0), axis=1, keepdims=True)
    earlier = jnp.sum(jnp.where(row < col, as_column, 0.0), axis=0, keepdims=True)
    slot = earlier.astype(jnp.int32)
    return jnp.where(chosen & (slot < CAP), slot, -1)


def pack_kernel(mine, ids_ref, keep_ref, gate_ref, input_ref, grad_ref, own_ref, other_ref):
    ids, keep = ids_ref[...], keep_ref[...]
    tokens = ids.shape[1]
    gate = gate_ref[...].astype(jnp.float32)
    moe_input, moe_grad = input_ref[...], grad_ref[...]
    expert = mine()
    row = iota((BLOCK, tokens), 0)
    input_slot = jnp.where(row < 8, row, jnp.where((row == 16) | (row == 17), row - 8, -2))
    grad_slot = jnp.where(
        (row >= 8) & (row < 16), row - 8, jnp.where((row == 18) | (row == 19), row - 10, -2)
    )
    diagonal = iota((tokens, tokens), 0) == iota((tokens, tokens), 1)
    gate_column = jnp.sum(jnp.where(diagonal, gate, 0.0), axis=1, keepdims=True)
    for which, out_ref in ((expert, own_ref), (1 - expert, other_ref)):
        slot = slots_of(ids, keep, which)
        block = mm(one_hot(input_slot == slot), moe_input) + mm(one_hot(grad_slot == slot), moe_grad)
        slot_column = jnp.sum(jnp.where(diagonal, slot, 0), axis=1, keepdims=True)
        gates = jnp.sum(
            jnp.where(slot_column == iota((tokens, LANES), 1), gate_column, 0.0), axis=0, keepdims=True
        )
        out_ref[...] = block.astype(jnp.bfloat16)
        out_ref[:, :LANES] = (
            block[:, :LANES] + jnp.where(iota((BLOCK, LANES), 0) == GATE_ROW, gates, 0.0)
        ).astype(jnp.bfloat16)


def slot_rows(count):
    rows = iota((count * CAP, 1), 0)
    tail = rows - 8 * count
    source = jnp.where(rows < 8 * count, rows // 8, tail // 2)
    return source, jnp.where(rows < 8 * count, rows % 8, 8 + tail % 2)


def main_kernel(places, *refs):
    blocks = refs[: len(places)]
    w_in_ref, w_out_ref = refs[len(places) : len(places) + 2]
    x_out, g_out, hidden_ref, scaled_ref, keep_ref, send_ref = refs[len(places) + 2 : len(places) + 8]
    tails, gate_col, total, gate_part = refs[len(places) + 8 :]
    step, steps = pl.program_id(0), pl.num_programs(0)
    count = sum(r.shape[0] for r in blocks) * 2
    rows = count * CAP
    source, slot = slot_rows(count)

    @pl.when(step == 0)
    def _():
        for block, place in zip(blocks, places):
            for i in range(block.shape[0]):
                at = place + i
                first, second = block[i, 0], block[i, 1]
                x_out[pl.ds(16 * at, 16), :] = jnp.concatenate([first[:8], second[:8]], axis=0)
                g_out[pl.ds(16 * at, 16), :] = jnp.concatenate([first[8:16], second[8:16]], axis=0)
                tails[pl.ds(16 * at, 16), :] = jnp.concatenate([first[16:], second[16:]], axis=0)
        row, col = iota((2 * count, 8 * count), 0), iota((2 * count, 8 * count), 1)
        pick = 8 * (row // 2) + row % 2
        tail = tails[...]
        x_out[pl.ds(8 * count, 2 * count), :] = mm(one_hot(col == pick), tail).astype(jnp.bfloat16)
        g_out[pl.ds(8 * count, 2 * count), :] = mm(one_hot(col == pick + 2), tail).astype(jnp.bfloat16)
        of_row = one_hot(iota((rows, 8 * count), 1) == 8 * source + GATE_ROW - 16)
        gates = mm(of_row, tails[:, :LANES])
        gate_col[...] = jnp.sum(
            jnp.where(iota((rows, LANES), 1) == slot, gates, 0.0), axis=1, keepdims=True
        )
        total[...] = jnp.zeros_like(total)
        gate_part[...] = jnp.zeros_like(gate_part)

    w_in = w_in_ref[...]
    pre = mm(x_out[...], w_in)
    back = mm(g_out[...], w_out_ref[...], ((1,), (1,)))
    active = jnp.maximum(pre, 0.0)
    gate = gate_col[...]
    hidden = (gate * back * jnp.where(pre > 0, 1.0, 0.0)).astype(jnp.bfloat16)
    hidden_ref[...] = hidden
    scaled_ref[...] = (gate * active).astype(jnp.bfloat16)
    total[...] += mm(hidden, w_in, ((1,), (1,)))
    gate_part[...] += jnp.sum(active * back, axis=1, keepdims=True)

    @pl.when(step == steps - 1)
    def _():
        units = count // 2
        lane = iota((rows, LANES), 1)
        placed = jnp.where(lane == 16 * (source % 2) + slot, gate_part[...], 0.0).astype(jnp.bfloat16)
        low = total[pl.ds(8 * count, 2 * count), :].astype(jnp.bfloat16)
        row, col = iota((8 * units, 2 * count), 0), iota((8 * units, 2 * count), 1)
        ends = mm(one_hot((row % 8 < 4) & (col == 4 * (row // 8) + row % 8)), low)
        at = iota((8 * units, rows), 1)
        unit = jnp.where(at < 8 * count, at // 16, (at - 8 * count) // 4)
        row = iota((8 * units, rows), 0)
        gates = mm(one_hot((row % 8 == GATE_ROW - 16) & (unit == row // 8)), placed)
        for u in range(units):
            half, index = (keep_ref, u) if u < keep_ref.shape[0] else (send_ref, u - keep_ref.shape[0])
            half[index, :16, :] = total[pl.ds(16 * u, 16), :].astype(jnp.bfloat16)
            half[index, 16:, :] = ends[8 * u : 8 * u + 8].astype(jnp.bfloat16)
            half[index, 16:, :LANES] = (
                ends[8 * u : 8 * u + 8, :LANES] + gates[8 * u : 8 * u + 8]
            ).astype(jnp.bfloat16)


def sum_pairs_kernel(keep_ref, got_ref, own_ref, *out_refs):
    own_ref[...] = keep_ref[0].astype(jnp.float32) + got_ref[0].astype(jnp.float32)
    for i, out_ref in enumerate(out_refs):
        out_ref[...] = (
            keep_ref[i + 1].astype(jnp.float32) + got_ref[i + 1].astype(jnp.float32)
        ).astype(jnp.bfloat16)


def sum_unit_kernel(*refs):
    parts, (own_ref, send_ref) = refs[:-2], refs[-2:]
    unit = parts[0][...].astype(jnp.float32)
    for part in parts[1:]:
        unit = unit + part[...].astype(jnp.float32)
    own_ref[...] = unit
    send_ref[...] = unit[8:].astype(jnp.bfloat16)


def scatter_kernel(mine, ids_ref, keep_ref, own_ref, got_ref, grad_ref, gate_ref):
    ids, keep = ids_ref[...], keep_ref[...]
    tokens = ids.shape[1]
    expert = mine()
    diagonal = iota((tokens, tokens), 0) == iota((tokens, tokens), 1)
    own, got = own_ref[...], got_ref[...].astype(jnp.float32)
    grad = jnp.zeros((tokens, own.shape[1]), jnp.float32)
    gate = jnp.zeros((1, tokens), jnp.float32)
    for which, part, first, tail, lane in (
        (expert, own, 0, 16, 0),
        (1 - expert, got, 0, 10, 16),
    ):
        slot = slots_of(ids, keep, which)
        column = jnp.sum(jnp.where(diagonal, slot, 0), axis=1, keepdims=True)
        row = iota((tokens, part.shape[0]), 1)
        place = jnp.where(column < 8, first + column, tail + column - 8)
        grad = grad + mm(one_hot((row == place) & (column >= 0)), part.astype(jnp.bfloat16))
        gates = part[GATE_ROW - BLOCK + part.shape[0] :][:1, :LANES]
        wide = jnp.where(iota((LANES, tokens), 0) == slot + lane, 1.0, 0.0)
        wide = jnp.where(slot >= 0, wide, 0.0)
        column_gates = jnp.sum(
            jnp.where(iota((LANES, LANES), 0) == iota((LANES, LANES), 1), gates, 0.0), axis=1, keepdims=True
        )
        gate = gate + jnp.sum(wide * column_gates, axis=0, keepdims=True)
    grad_ref[...] = grad.astype(jnp.bfloat16)
    gate_ref[...] = gate


def params(limit=None):
    return pltpu.CompilerParams(vmem_limit_bytes=limit)


def expert_layer(moe_input, moe_grad, gate_prob, expert_ids, keep_mask, w_input, w_output):
    devices = lax.axis_size("seq")
    shards = devices // EXPERTS
    tokens = moe_input.shape[0]
    width = w_input.shape[1]

    def mine():
        return lax.axis_index("seq") // shards

    def flip(block, bits):
        return lax.ppermute(block, "seq", [(i, i ^ bits) for i in range(devices)])

    ids, keep = expert_ids.reshape(1, tokens), keep_mask.reshape(1, tokens)
    block_type = jax.ShapeDtypeStruct((BLOCK, D), jnp.bfloat16)
    own, other = pl.pallas_call(
        functools.partial(pack_kernel, mine), out_shape=(block_type, block_type), compiler_params=params()
    )(ids, keep, gate_prob.reshape(1, tokens), moe_input, moe_grad)
    across = (devices - 1) & ~3
    got = flip(other, across)
    pair = jnp.stack([own, got])[None]
    square = shards == 8
    if square:
        near = [pair, flip(pair, 2), flip(pair, 4), flip(pair, 6)]
        blocks = near + [flip(b, 1) for b in near]
    else:
        halves = [list(range(e * shards, (e + 1) * shards)) for e in range(EXPERTS)]
        blocks = [lax.all_gather(pair, "seq", axis_index_groups=halves, tiled=True)]
    places, at = [], 0
    for b in blocks:
        places.append(at)
        at += b.shape[0]
    sources = 2 * at
    rows = sources * CAP
    chunk = min(width, 256)
    keep_units = shards // 2
    slots = jax.ShapeDtypeStruct((rows, D), jnp.bfloat16)
    hidden_type = jax.ShapeDtypeStruct((rows, width), jnp.bfloat16)
    units_type = jax.ShapeDtypeStruct((keep_units, BLOCK, D), jnp.bfloat16)
    once = pl.Buffered(1)

    def whole(shape):
        return pl.BlockSpec(shape, lambda i: (0,) * len(shape), pipeline_mode=once)

    x, g, hidden, scaled, keep_half, send_half = pl.pallas_call(
        functools.partial(main_kernel, places),
        grid=(width // chunk,),
        in_specs=[whole(b.shape) for b in blocks]
        + [pl.BlockSpec((D, chunk), lambda i: (0, i)), pl.BlockSpec((chunk, D), lambda i: (i, 0))],
        out_specs=[
            whole(slots.shape),
            whole(slots.shape),
            pl.BlockSpec((rows, chunk), lambda i: (0, i)),
            pl.BlockSpec((rows, chunk), lambda i: (0, i)),
            whole(units_type.shape),
            whole(units_type.shape),
        ],
        out_shape=[slots, slots, hidden_type, hidden_type, units_type, units_type],
        scratch_shapes=[
            pltpu.VMEM((8 * sources, D), jnp.bfloat16),
            pltpu.VMEM((rows, 1), jnp.float32),
            pltpu.VMEM((rows, D), jnp.float32),
            pltpu.VMEM((rows, 1), jnp.float32),
        ],
        compiler_params=params(62 * 2**20 if not square else 48 * 2**20),
    )(*blocks, w_input, w_output)

    w_output_grad = mm(scaled, g, ((0,), (0,))).astype(jnp.bfloat16)
    w_input_grad = mm(x, hidden, ((0,), (0,))).astype(jnp.bfloat16)

    unit_wide = jax.ShapeDtypeStruct((BLOCK, D), jnp.float32)
    tail_type = jax.ShapeDtypeStruct((BLOCK - 8, D), jnp.bfloat16)
    if square:
        summed = pl.pallas_call(
            sum_pairs_kernel,
            out_shape=[unit_wide] + [block_type] * 3,
            compiler_params=params(),
        )(keep_half, flip(send_half, 1))
        parts = [summed[0], flip(summed[1], 2), flip(summed[2], 4), flip(summed[3], 6)]
    else:
        units = jnp.concatenate([keep_half, send_half]).astype(jnp.float32)
        parts = [
            lax.psum_scatter(units, "seq", axis_index_groups=halves, tiled=True).reshape(BLOCK, D)
        ]
    own_unit, send_unit = pl.pallas_call(
        sum_unit_kernel, out_shape=(unit_wide, tail_type), compiler_params=params()
    )(*parts)
    moe_input_grad, gate_grad = pl.pallas_call(
        functools.partial(scatter_kernel, mine),
        out_shape=(
            jax.ShapeDtypeStruct((tokens, D), jnp.bfloat16),
            jax.ShapeDtypeStruct((1, tokens), jnp.float32),
        ),
        compiler_params=params(),
    )(ids, keep, own_unit, flip(send_unit, across))
    return moe_input_grad, gate_grad.reshape(tokens), w_input_grad, w_output_grad


def token_kernel(query_ref, grad_ref, segments_ref, out_ref):
    tokens = query_ref.shape[0]
    out_ref[:tokens, :] = query_ref[...]
    out_ref[tokens : 2 * tokens, :] = grad_ref[...]
    out_ref[2 * tokens :, :] = jnp.zeros((8, out_ref.shape[1]), jnp.bfloat16)
    segments = segments_ref[...] + 1
    diagonal = iota((tokens, tokens), 0) == iota((tokens, tokens), 1)
    column = jnp.sum(jnp.where(diagonal, segments, 0), axis=1, keepdims=True)
    lane = iota((tokens, LANES), 1)
    row = iota((tokens, LANES), 0)
    digits = jnp.zeros((tokens, LANES), jnp.int32)
    for i in range(3):
        digits = digits + jnp.where(lane == row + i * tokens, (column >> (7 * i)) & 127, 0)
    line = jnp.sum(digits, axis=0, keepdims=True).astype(jnp.float32)
    out_ref[2 * tokens :, :LANES] = jnp.where(iota((8, LANES), 0) == 0, line, 0.0).astype(jnp.bfloat16)


def segment_column(token_ref, tokens):
    line = token_ref[2 * tokens :, :LANES][:1].astype(jnp.float32)
    lane, row = iota((tokens, LANES), 1), iota((tokens, LANES), 0)
    weight = jnp.zeros((tokens, LANES), jnp.float32)
    for i in range(3):
        weight = weight + jnp.where(lane == row + i * tokens, float(128**i), 0.0)
    return jnp.sum(weight * line, axis=1, keepdims=True).astype(jnp.int32)


def head_scores(token_refs, kv, head, tokens):
    lanes = pl.ds(head * HEAD_DIM, HEAD_DIM)
    queries = jnp.concatenate([r[:tokens, lanes] for r in token_refs], axis=0)
    grads = jnp.concatenate([r[tokens : 2 * tokens, lanes] for r in token_refs], axis=0)
    both = mm(jnp.concatenate([queries, grads], axis=0), kv, ((1,), (1,)))
    count = queries.shape[0]
    return queries, grads, both[:count], pltpu.roll(both[count:], both.shape[1] - 1, 1)


def allowed_pairs(token_refs, rows_ref, tokens):
    column = jnp.concatenate([segment_column(r, tokens) for r in token_refs], axis=0)
    rows = rows_ref[...]
    even = iota(rows.shape, 1) % 2 == 0
    return jnp.where(even, rows + 1, -1) == column


def load_head(kv_ref, head):
    rows = kv_ref.shape[0]
    return kv_ref[:, :, pl.ds(head * HEAD_DIM, HEAD_DIM)].reshape(2 * rows, HEAD_DIM)


def stats_kernel(own_ref, sib_ref, near_ref, rows_ref, kv_ref, stats_ref):
    token_refs = (own_ref, sib_ref, near_ref)
    tokens = (own_ref.shape[0] - 8) // 2
    allowed = allowed_pairs(token_refs, rows_ref, tokens)
    lane = iota((3 * tokens, LANES), 1)
    stats = jnp.zeros((3 * tokens, LANES), jnp.float32)
    for head in range(HEADS):
        _, _, scores, prob_grad = head_scores(token_refs, load_head(kv_ref, head), head, tokens)
        scores = jnp.where(allowed, SCALE * scores, NONE)
        peak = jnp.max(scores, axis=1, keepdims=True)
        weight = jnp.where(allowed, jnp.exp(scores - peak), 0.0)
        mass = jnp.sum(weight, axis=1, keepdims=True)
        delta = jnp.sum(weight * prob_grad, axis=1, keepdims=True)
        stats = jnp.where(lane == head, peak, stats)
        stats = jnp.where(lane == HEADS + head, mass, stats)
        stats = jnp.where(lane == 2 * HEADS + head, delta, stats)
    stats_ref[...] = stats


def merged(parts):
    peaks = [jnp.where(p[:, HEADS : 2 * HEADS] > 0, p[:, :HEADS], NONE) for p in parts]
    peak = jnp.maximum(jnp.maximum(peaks[0], peaks[1]), peaks[2])
    scale = [jnp.exp(p - peak) for p in peaks]
    mass = sum(s * p[:, HEADS : 2 * HEADS] for s, p in zip(scale, parts))
    delta = sum(s * p[:, 2 * HEADS : 3 * HEADS] for s, p in zip(scale, parts))
    inverse = jnp.where(mass > 0, 1.0 / mass, 0.0)
    return peak, inverse, delta * inverse


def grads_kernel(
    own_ref, sib_ref, near_ref, rows_ref, kv_ref, st_ref, st_sib_ref, st_near_ref, st_far_ref, st_side_ref,
    query_ref, to_sib_ref, to_near_ref, kv_grad_ref,
):
    token_refs = (own_ref, sib_ref, near_ref)
    tokens = (own_ref.shape[0] - 8) // 2
    allowed = allowed_pairs(token_refs, rows_ref, tokens)
    a, b, c = slice(0, tokens), slice(tokens, 2 * tokens), slice(2 * tokens, 3 * tokens)
    totals = [
        merged((st_ref[a], st_sib_ref[b], st_near_ref[c])),
        merged((st_ref[b], st_sib_ref[a], st_side_ref[c])),
        merged((st_ref[c], st_near_ref[a], st_far_ref[b])),
    ]
    peak, scale, delta = (jnp.concatenate([t[i] for t in totals], axis=0) for i in range(3))
    for head in range(HEADS):
        kv = load_head(kv_ref, head)
        queries, grads, scores, prob_grad = head_scores(token_refs, kv, head, tokens)
        at = slice(head, head + 1)
        probs = jnp.exp(jnp.where(allowed, SCALE * scores - peak[:, at], NONE)) * scale[:, at]
        score_grad = SCALE * (probs * (prob_grad - delta[:, at]))
        moved = pltpu.roll(probs, 1, 1)
        score_low = score_grad.astype(jnp.bfloat16)
        query = mm(score_low, kv)
        lanes = pl.ds(head * HEAD_DIM, HEAD_DIM)
        query_ref[:, lanes] = query[a]
        to_sib_ref[:, lanes] = query[b].astype(jnp.bfloat16)
        to_near_ref[:, lanes] = query[c].astype(jnp.bfloat16)
        both = jnp.concatenate([score_low, moved.astype(jnp.bfloat16)], axis=0)
        grad = mm(both, jnp.concatenate([queries, grads], axis=0), ((0,), (0,)))
        kv_grad_ref[:, :, lanes] = grad.astype(jnp.bfloat16).reshape(kv_grad_ref.shape[0], 2, HEAD_DIM)


def attention(dec_query, ctx_grad, dec_segments, enc_kv, enc_segments):
    devices = lax.axis_size("seq")
    tokens = dec_query.shape[0]
    rows = enc_kv.shape[0]
    crossing = [(i, i + 1) for i in range(1, devices - 1, 2)]

    def core(block):
        return lax.ppermute(block, "seq", [(i, i ^ 1) for i in range(devices)])

    def cross(block):
        return lax.ppermute(block, "seq", crossing + [(j, i) for i, j in crossing])

    own = pl.pallas_call(
        token_kernel,
        out_shape=jax.ShapeDtypeStruct((2 * tokens + 8, D), jnp.bfloat16),
        compiler_params=params(),
    )(dec_query, ctx_grad, dec_segments.reshape(1, tokens))
    held = (own, core(own), cross(own), jnp.repeat(enc_segments, 2).reshape(1, 2 * rows), enc_kv)
    stats_type = jax.ShapeDtypeStruct((3 * tokens, LANES), jnp.float32)
    stats = pl.pallas_call(stats_kernel, out_shape=stats_type, compiler_params=params(32 * 2**20))(*held)
    stats_sib, stats_near = core(stats), cross(stats)
    low = jax.ShapeDtypeStruct((tokens, D), jnp.bfloat16)
    query, to_sib, to_near, kv_grad = pl.pallas_call(
        grads_kernel,
        out_shape=(
            jax.ShapeDtypeStruct((tokens, D), jnp.float32), low, low,
            jax.ShapeDtypeStruct(enc_kv.shape, jnp.bfloat16),
        ),
        compiler_params=params(32 * 2**20),
    )(*held, stats, stats_sib, stats_near, cross(stats_sib), core(stats_near))
    query_grad = query + core(to_sib).astype(jnp.float32) + cross(to_near).astype(jnp.float32)
    return query_grad.astype(jnp.bfloat16), kv_grad


def local(
    dec_query,
    ctx_grad,
    dec_segments,
    enc_kv,
    enc_segments,
    moe_input,
    moe_grad,
    gate_prob,
    expert_ids,
    keep_mask,
    w_input,
    w_output,
):
    query_grad, kv_grad = attention(dec_query, ctx_grad, dec_segments, enc_kv, enc_segments)
    moe_input_grad, gate_grad, w_input_grad, w_output_grad = expert_layer(
        moe_input, moe_grad, gate_prob, expert_ids, keep_mask, w_input, w_output
    )
    return (query_grad, kv_grad, moe_input_grad, gate_grad, w_input_grad, w_output_grad)


def solution(mesh):
    return jax.shard_map(
        local,
        mesh=mesh,
        in_specs=(
            P(("groups", "seq"), None),
            P(("groups", "seq"), None),
            P(("groups", "seq")),
            P(("groups", "seq"), None, None),
            P(("groups", "seq")),
            P(("groups", "seq"), None),
            P(("groups", "seq"), None),
            P(("groups", "seq")),
            P(("groups", "seq")),
            P(("groups", "seq")),
            P(None, "seq"),
            P("seq", None),
        ),
        out_specs=(
            P(("groups", "seq"), None),
            P(("groups", "seq"), None, None),
            P(("groups", "seq"), None),
            P(("groups", "seq")),
            P("groups", "seq"),
            P("seq", "groups"),
        ),
        check_vma=False,
    )
```

time: 228 us -> 125 us (0.55)
  the two profiles are of different devices: /device:TPU:13 before, /device:TPU:1 now
where the time goes in v1:
time: 125 us; the launch traced here: 123 us
  starting transfers between devices  43.8 us (35%)
  Pallas kernels  39.2 us (31%)
  waiting for transfers between devices  18.1 us (14%)
  matrix products  13 us (10%)
  local copies, waits for them, and re-layouts  6.55 us (5%)
  other arithmetic  1.66 us (1%)
    ppermute x13, starting transfers between devices, flip(): return lax.ppermute(block, 'seq', [(i, i ^ bits) for i in range(devices)])  23.9 us
    ppermute x4, starting transfers between devices, cross(): return lax.ppermute(block, 'seq', crossing + [(j, i) for i, j in crossing])  18.7 us
    pallas_call x1, Pallas kernels, expert_layer(): pl.pallas_call(functools.partial(main_kernel, places), grid=(width // chu...  14.6 us
    dot_general x2, matrix products, mm(): lax.dot_general(a, b, (dims, ((), ())), preferred_element_type=jnp.float32)  13 us
    ppermute x13, waiting for transfers between devices, flip(): return lax.ppermute(block, 'seq', [(i, i ^ bits) for i in range(devices)])  11.1 us
    pallas_call x1, Pallas kernels, attention(): pl.pallas_call(grads_kernel, out_shape=(jax.ShapeDtypeStruct((tokens, D),...  9.16 us
    unnamed x18, local copies, waits for them, and re-layouts  5.67 us
    pallas_call x1, Pallas kernels, attention(): pl.pallas_call(stats_kernel, out_shape=stats_type, compiler_params=params...  4.85 us
  transfers between devices with their start and end apart: 21, of which 10 were waited for; matrix products, arithmetic and copies ran while one was open for 13% of the time, Pallas kernels for 25%

profile of v1, /device:TPU:1, one launch (start us, length us, event | category | flops | bytes accessed | tf_op | source)
XLA Modules:
  0.0 123.1 jit_solution(836860100364049578)
XLA Ops:
  0.6 2.2 %shard_map.166 = (bf16[24,4096]{1,0:T(8,128)(2,1)}, bf16[24,4096]{1,0:T(8,128)(2,1)}) custom-call(s32[1,16]{1,0:T(1,128)} %bitcast.15, s32[1,16]{1,0:T(1,128)} %bitcast.17, bf16[1,16]{1,0:T(2,128)(2,1)} %bitcast.19, bf16[16,4096]{1,0:T(8,128)(2,1)} %input_ref.1, bf16[16,4096]{1,0:T(8,128)(2,1)} %grad_ref.3), custom_call_target="tpu_custom_call" | custom-call | tf_op jit(solution)/shard_map/pallas_call | solution.py:205
  2.8 4.2 %collective-permute-start.8 = (bf16[24,4096]{1,0:T(8,128)(2,1)}, bf16[24,4096]{1,0:T(8,128)(2,1)S(1)}, u32[]{:S(2)}, u32[]{:S(2)}) collective-permute-start(bf16[24,4096]{1,0:T(8,128)(2,1)} %get-tuple-element.31), channel_id=1, source_target_pairs={{0,12},{1,13},{2,14},{3,15},{4,8},{5,9},{6,10},{7,11},{8,4},{9,5},... | collective-permute-start | bytes 589832 | tf_op jit(solution)/shard_map/ppermute | solution.py:201
  7.0 1.8 %shard_map.163.own_ref = bf16[40,4096]{1,0:T(8,128)(2,1)} custom-call(bf16[16,4096]{1,0:T(8,128)(2,1)} %query_ref.1, bf16[16,4096]{1,0:T(8,128)(2,1)} %grad_ref.2, s32[1,16]{1,0:T(1,128)} %bitcast.20), custom_call_target="tpu_custom_call" | custom-call | tf_op jit(solution)/shard_map/pallas_call | solution.py:408
  9.7 2.1 %collective-permute-done.8 = bf16[24,4096]{1,0:T(8,128)(2,1)S(1)} collective-permute-done((bf16[24,4096]{1,0:T(8,128)(2,1)}, bf16[24,4096]{1,0:T(8,128)(2,1)S(1)}, u32[]{:S(2)}, u32[]{:S(2)}) %collective-permute-start.8) | collective-permute-done | bytes 196640 | tf_op jit(solution)/shard_map/ppermute | solution.py:201
  12.8 1.1 collective-permute-start.9
  13.9 3.7 %collective-permute-start.10 = (bf16[1,2,24,4096]{3,2,1,0:T(8,128)(2,1)S(1)}, bf16[1,2,24,4096]{3,2,1,0:T(8,128)(2,1)S(1)}, u32[]{:S(2)}, u32[]{:S(2)}) collective-permute-start(bf16[1,2,24,4096]{3,2,1,0:T(8,128)(2,1)S(1)} %maximum_bitcast_fusion.refs_0_), channel_id=1, source_target_pairs={{0,4},{1,5},{2,6},{3,7},{4,0},{5,1},{6,2},{7,3},{8,12},{9,13},{10,... | collective-permute-start | bytes 1179656 | tf_op jit(solution)/shard_map/ppermute | solution.py:201
  17.6 4.9 %collective-permute-start.1 = (bf16[40,4096]{1,0:T(8,128)(2,1)}, bf16[40,4096]{1,0:T(8,128)(2,1)S(1)}, u32[]{:S(2)}, u32[]{:S(2)}) collective-permute-start(bf16[40,4096]{1,0:T(8,128)(2,1)} %shard_map.163.own_ref), channel_id=1, source_target_pairs={{1,2},{3,4},{5,6},{7,8},{9,10},{11,12},{13,14},{2,1},{4,3},{6,5},{... | collective-permute-start | bytes 983048 | tf_op jit(solution)/shard_map/ppermute | solution.py:406
  22.6 1.8 %collective-permute-start.13 = (bf16[1,2,24,4096]{3,2,1,0:T(8,128)(2,1)S(1)}, bf16[1,2,24,4096]{3,2,1,0:T(8,128)(2,1)S(1)}, u32[]{:S(2)}, u32[]{:S(2)}) collective-permute-start(bf16[1,2,24,4096]{3,2,1,0:T(8,128)(2,1)S(1)} %collective-permute-done.9.refs_1_), channel_id=1, source_target_pairs={{0,1},{1,0},{2,3},{3,2},{4,5},{5,4},{6,7},{7,6},{8,9},{9,8},{10,11... | collective-permute-start | bytes 1179656 | tf_op jit(solution)/shard_map/ppermute | solution.py:201
  25.4 4.2 %collective-permute-start.14 = (bf16[1,2,24,4096]{3,2,1,0:T(8,128)(2,1)S(1)}, bf16[1,2,24,4096]{3,2,1,0:T(8,128)(2,1)S(1)}, u32[]{:S(2)}, u32[]{:S(2)}) collective-permute-start(bf16[1,2,24,4096]{3,2,1,0:T(8,128)(2,1)S(1)} %collective-permute-done.10.refs_2_), channel_id=1, source_target_pairs={{0,1},{1,0},{2,3},{3,2},{4,5},{5,4},{6,7},{7,6},{8,9},{9,8},{10,11... | collective-permute-start | bytes 1179656 | tf_op jit(solution)/shard_map/ppermute | solution.py:201
  29.6 4.3 %collective-permute-done.11.refs_3_ = bf16[1,2,24,4096]{3,2,1,0:T(8,128)(2,1)S(1)} collective-permute-done((bf16[1,2,24,4096]{3,2,1,0:T(8,128)(2,1)S(1)}, bf16[1,2,24,4096]{3,2,1,0:T(8,128)(2,1)S(1)}, u32[]{:S(2)}, u32[]{:S(2)}) %collective-permute-start.11) | collective-permute-done | bytes 393248 | tf_op jit(solution)/shard_map/ppermute | solution.py:201
  33.8 2.4 %collective-permute-start.15 = (bf16[1,2,24,4096]{3,2,1,0:T(8,128)(2,1)S(1)}, bf16[1,2,24,4096]{3,2,1,0:T(8,128)(2,1)}, u32[]{:S(2)}, u32[]{:S(2)}) collective-permute-start(bf16[1,2,24,4096]{3,2,1,0:T(8,128)(2,1)S(1)} %collective-permute-done.11.refs_3_), channel_id=1, source_target_pairs={{0,1},{1,0},{2,3},{3,2},{4,5},{5,4},{6,7},{7,6},{8,9},{9,8},{10,11... | collective-permute-start | bytes 1179656 | tf_op jit(solution)/shard_map/ppermute | solution.py:201
  37.1 1.7 %collective-permute-done.1.near_ref = bf16[40,4096]{1,0:T(8,128)(2,1)S(1)} collective-permute-done((bf16[40,4096]{1,0:T(8,128)(2,1)}, bf16[40,4096]{1,0:T(8,128)(2,1)S(1)}, u32[]{:S(2)}, u32[]{:S(2)}) %collective-permute-start.1) | collective-permute-done | bytes 327712 | tf_op jit(solution)/shard_map/ppermute | solution.py:406
  38.8 1.6 %copy-done = bf16[128,2,4096]{2,1,0:T(2,128)(2,1)S(1)} copy-done((bf16[128,2,4096]{2,1,0:T(2,128)(2,1)S(1)}, bf16[128,2,4096]{2,1,0:T(2,128)(2,1)}, u32[]{:S(2)}) %copy-start) | copy-done | bytes 2097176
  41.4 4.8 %shard_map.164.st_ref = f32[48,128]{1,0:T(8,128)S(1)} custom-call(bf16[40,4096]{1,0:T(8,128)(2,1)S(1)} %copy-done.1, bf16[40,4096]{1,0:T(8,128)(2,1)S(1)} %collective-permute-done.sib_ref, bf16[40,4096]{1,0:T(8,128)(2,1)S(1)} %collective-permute-done.1.near_ref, s32[1,256]{1,0:T(1,128)S(1)} %reshape_reshape.3.rows_ref, bf16[128,2,4096]{2,1,0:T(2,128)(2,1)S(1)} %copy-done), custom_call_target="tpu_custom_call" | custom-call | tf_op jit(solution)/shard_map/pallas_call | solution.py:415
  46.3 1.2 collective-permute-done.2.st_sib_ref
  47.5 4.2 %collective-permute-start.3 = (f32[48,128]{1,0:T(8,128)S(1)}, f32[48,128]{1,0:T(8,128)S(1)}, u32[]{:S(2)}, u32[]{:S(2)}) collective-permute-start(f32[48,128]{1,0:T(8,128)S(1)} %shard_map.164.st_ref), channel_id=1, source_target_pairs={{1,2},{3,4},{5,6},{7,8},{9,10},{11,12},{13,14},{2,1},{4,3},{6,5},{... | collective-permute-start | bytes 73736 | tf_op jit(solution)/shard_map/ppermute | solution.py:406
  51.7 1.5 %collective-permute-done.3.st_near_ref = f32[48,128]{1,0:T(8,128)S(1)} collective-permute-done((f32[48,128]{1,0:T(8,128)S(1)}, f32[48,128]{1,0:T(8,128)S(1)}, u32[]{:S(2)}, u32[]{:S(2)}) %collective-permute-start.3) | collective-permute-done | bytes 24608 | tf_op jit(solution)/shard_map/ppermute | solution.py:406
  53.2 3.6 %collective-permute-start.4 = (f32[48,128]{1,0:T(8,128)S(1)}, f32[48,128]{1,0:T(8,128)S(1)}, u32[]{:S(2)}, u32[]{:S(2)}) collective-permute-start(f32[48,128]{1,0:T(8,128)S(1)} %collective-permute-done.2.st_sib_ref), channel_id=1, source_target_pairs={{1,2},{3,4},{5,6},{7,8},{9,10},{11,12},{13,14},{2,1},{4,3},{6,5},{... | collective-permute-start | bytes 73736 | tf_op jit(solution)/shard_map/ppermute | solution.py:406
  56.9 1.5 %collective-permute-done.4.st_far_ref = f32[48,128]{1,0:T(8,128)S(1)} collective-permute-done((f32[48,128]{1,0:T(8,128)S(1)}, f32[48,128]{1,0:T(8,128)S(1)}, u32[]{:S(2)}, u32[]{:S(2)}) %collective-permute-start.4) | collective-permute-done | bytes 24608 | tf_op jit(solution)/shard_map/ppermute | solution.py:406
  58.4 1.2 collective-permute-done.5.st_side_ref
  59.5 9.2 %shard_map.165 = (f32[16,4096]{1,0:T(8,128)S(1)}, bf16[16,4096]{1,0:T(8,128)(2,1)S(1)}, bf16[16,4096]{1,0:T(8,128)(2,1)S(1)}, bf16[128,2,4096]{2,1,0:T(2,128)(2,1)}) custom-call(bf16[40,4096]{1,0:T(8,128)(2,1)S(1)} %copy-done.1, bf16[40,4096]{1,0:T(8,128)(2,1)S(1)} %collective-permute-done.sib_ref, bf16[40,4096]{1,0:T(8,128)(2,1)S(1)} %collective-permute-done.1.near_ref, ...), custom_call_target="tpu_custom_call" | custom-call | tf_op jit(solution)/shard_map/pallas_call | solution.py:418
  68.9 6.0 %collective-permute-start.7 = (bf16[16,4096]{1,0:T(8,128)(2,1)S(1)}, bf16[16,4096]{1,0:T(8,128)(2,1)S(1)}, u32[]{:S(2)}, u32[]{:S(2)}) collective-permute-start(bf16[16,4096]{1,0:T(8,128)(2,1)S(1)} %get-tuple-element.28), channel_id=1, source_target_pairs={{1,2},{3,4},{5,6},{7,8},{9,10},{11,12},{13,14},{2,1},{4,3},{6,5},{... | collective-permute-start | bytes 393224 | tf_op jit(solution)/shard_map/ppermute | solution.py:406
  74.9 14.6 %shard_map.167 = (bf16[160,4096]{1,0:T(8,128)(2,1)}, bf16[160,4096]{1,0:T(8,128)(2,1)}, bf16[160,1024]{1,0:T(8,128)(2,1)S(1)}, bf16[160,1024]{1,0:T(8,128)(2,1)S...) custom-call(bf16[1,2,24,4096]{3,2,1,0:T(8,128)(2,1)S(1)} %maximum_bitcast_fusion.refs_0_, ...), custom_call_target="tpu_custom_call" | custom-call | tf_op jit(solution)/shard_map/pallas_call | solution.py:234
  91.1 1.6 %collective-permute-done.16.got_ref = bf16[4,24,4096]{2,1,0:T(8,128)(2,1)S(1)} collective-permute-done((bf16[4,24,4096]{2,1,0:T(8,128)(2,1)S(1)}, bf16[4,24,4096]{2,1,0:T(8,128)(2,1)S(1)}, u32[]{:S(2)}, u32[]{:S(2)}) %collective-permute-start.16) | collective-permute-done | bytes 786464 | tf_op jit(solution)/shard_map/ppermute | solution.py:201
  93.5 2.4 %shard_map.168 = (f32[24,4096]{1,0:T(8,128)}, bf16[24,4096]{1,0:T(8,128)(2,1)}, bf16[24,4096]{1,0:T(8,128)(2,1)}, bf16[24,4096]{1,0:T(8,128)(2,1)}) custom-call(bf16[4,24,4096]{2,1,0:T(8,128)(2,1)} %copy-done.2, bf16[4,24,4096]{2,1,0:T(8,128)(2,1)} %copy-done.4), custom_call_target="tpu_custom_call" | custom-call | tf_op jit(solution)/shard_map/pallas_call | solution.py:263
  95.9 2.4 %collective-permute-start.17 = (bf16[24,4096]{1,0:T(8,128)(2,1)}, bf16[24,4096]{1,0:T(8,128)(2,1)S(1)}, u32[]{:S(2)}, u32[]{:S(2)}) collective-permute-start(bf16[24,4096]{1,0:T(8,128)(2,1)} %get-tuple-element.35), channel_id=1, source_target_pairs={{0,2},{1,3},{2,0},{3,1},{4,6},{5,7},{6,4},{7,5},{8,10},{9,11},{10,... | collective-permute-start | bytes 589832 | tf_op jit(solution)/shard_map/ppermute | solution.py:201
  100.1 7.2 %convolution_convert_fusion = bf16[1024,4096]{1,0:T(8,128)(2,1)} fusion(bf16[160,1024]{1,0:T(8,128)(2,1)S(1)} %get-tuple-element.44, bf16[160,4096]{1,0:T(8,128)(2,1)} %get-tuple-element.45), kind=kOutput, calls=%fused_computation | convolution fusion | flops 1346371584 | bytes 10027008 | tf_op jit(solution)/shard_map/dot_general | solution.py:31
  107.3 2.1 %collective-permute-done.19.refs_3_ = bf16[24,4096]{1,0:T(8,128)(2,1)S(1)} collective-permute-done((bf16[24,4096]{1,0:T(8,128)(2,1)}, bf16[24,4096]{1,0:T(8,128)(2,1)S(1)}, u32[]{:S(2)}, u32[]{:S(2)}) %collective-permute-start.19) | collective-permute-done | bytes 196640 | tf_op jit(solution)/shard_map/ppermute | solution.py:201
  110.1 2.1 %shard_map.169 = (f32[24,4096]{1,0:T(8,128)}, bf16[16,4096]{1,0:T(8,128)(2,1)}) custom-call(f32[24,4096]{1,0:T(8,128)} %get-tuple-element.34.refs_0_, bf16[24,4096]{1,0:T(8,128)(2,1)} %copy-done.5, bf16[24,4096]{1,0:T(8,128)(2,1)} %copy-done.6, bf16[24,4096]{1,0:T(8,128)(2,1)} %copy-done.7), custom_call_target="tpu_custom_call" | custom-call | tf_op jit(solution)/shard_map/pallas_call | solution.py:274
  112.2 2.4 %collective-permute-start.20 = (bf16[16,4096]{1,0:T(8,128)(2,1)}, bf16[16,4096]{1,0:T(8,128)(2,1)S(1)}, u32[]{:S(2)}, u32[]{:S(2)}) collective-permute-start(bf16[16,4096]{1,0:T(8,128)(2,1)} %get-tuple-element.39), channel_id=1, source_target_pairs={{0,12},{1,13},{2,14},{3,15},{4,8},{5,9},{6,10},{7,11},{8,4},{9,5},... | collective-permute-start | bytes 393224 | tf_op jit(solution)/shard_map/ppermute | solution.py:201
  114.6 5.8 %convolution_convert_fusion.1 = bf16[4096,1024]{1,0:T(8,128)(2,1)} fusion(bf16[160,4096]{1,0:T(8,128)(2,1)S(1)} %copy-done.3, bf16[160,1024]{1,0:T(8,128)(2,1)S(1)} %get-tuple-element.43), kind=kOutput, calls=%fused_computation.1 | convolution fusion | flops 1346371584 | bytes 10027008 | tf_op jit(solution)/shard_map/dot_general | solution.py:31
  121.0 2.1 %shard_map.170 = (bf16[16,4096]{1,0:T(8,128)(2,1)}, f32[1,16]{1,0:T(1,128)}) custom-call(s32[1,16]{1,0:T(1,128)} %bitcast.16, s32[1,16]{1,0:T(1,128)} %bitcast.18, f32[24,4096]{1,0:T(8,128)} %get-tuple-element.38.own_ref, bf16[16,4096]{1,0:T(8,128)(2,1)} %copy-done.8), custom_call_target="tpu_custom_call" | custom-call | tf_op jit(solution)/shard_map/pallas_call | solution.py:277
  (42 shorter events, 10.7 us)
Async XLA Ops:
  2.8 9.0 %collective-permute-start.8 = (bf16[24,4096]{1,0:T(8,128)(2,1)}, bf16[24,4096]{1,0:T(8,128)(2,1)S(1)}, u32[]{:S(2)}, u32[]{:S(2)}) collective-permute-start(bf16[24,4096]{1,0:T(8,128)(2,1)} %get-tuple-element.31), channel_id=1, source_target_pairs={{0,12},{1,13},{2,14},{3,15},{4,8},{5,9},{6,10},{7,11},{8,4},{9,5},... | collective-permute-start | bytes 589832 | tf_op jit(solution)/shard_map/ppermute | solution.py:201
  8.8 13.7 %collective-permute-start = (bf16[40,4096]{1,0:T(8,128)(2,1)}, bf16[40,4096]{1,0:T(8,128)(2,1)S(1)}, u32[]{:S(2)}, u32[]{:S(2)}) collective-permute-start(bf16[40,4096]{1,0:T(8,128)(2,1)} %shard_map.163.own_ref), channel_id=1, source_target_pairs={{0,1},{1,0},{2,3},{3,2},{4,5},{5,4},{6,7},{7,6},{8,9},{9,8},{10,11... | collective-permute-start | bytes 983048 | tf_op jit(solution)/shard_map/ppermute | solution.py:403
  12.8 9.8 %collective-permute-start.9 = (bf16[1,2,24,4096]{3,2,1,0:T(8,128)(2,1)S(1)}, bf16[1,2,24,4096]{3,2,1,0:T(8,128)(2,1)S(1)}, u32[]{:S(2)}, u32[]{:S(2)}) collective-permute-start(bf16[1,2,24,4096]{3,2,1,0:T(8,128)(2,1)S(1)} %maximum_bitcast_fusion.refs_0_), channel_id=1, source_target_pairs={{0,2},{1,3},{2,0},{3,1},{4,6},{5,7},{6,4},{7,5},{8,10},{9,11},{10,... | collective-permute-start | bytes 1179656 | tf_op jit(solution)/shard_map/ppermute | solution.py:201
  13.9 11.5 %collective-permute-start.10 = (bf16[1,2,24,4096]{3,2,1,0:T(8,128)(2,1)S(1)}, bf16[1,2,24,4096]{3,2,1,0:T(8,128)(2,1)S(1)}, u32[]{:S(2)}, u32[]{:S(2)}) collective-permute-start(bf16[1,2,24,4096]{3,2,1,0:T(8,128)(2,1)S(1)} %maximum_bitcast_fusion.refs_0_), channel_id=1, source_target_pairs={{0,4},{1,5},{2,6},{3,7},{4,0},{5,1},{6,2},{7,3},{8,12},{9,13},{10,... | collective-permute-start | bytes 1179656 | tf_op jit(solution)/shard_map/ppermute | solution.py:201
  17.6 16.2 %collective-permute-start.11 = (bf16[1,2,24,4096]{3,2,1,0:T(8,128)(2,1)S(1)}, bf16[1,2,24,4096]{3,2,1,0:T(8,128)(2,1)S(1)}, u32[]{:S(2)}, u32[]{:S(2)}) collective-permute-start(bf16[1,2,24,4096]{3,2,1,0:T(8,128)(2,1)S(1)} %maximum_bitcast_fusion.refs_0_), channel_id=1, source_target_pairs={{0,6},{1,7},{2,4},{3,5},{4,2},{5,3},{6,0},{7,1},{8,14},{9,15},{10,... | collective-permute-start | bytes 1179656 | tf_op jit(solution)/shard_map/ppermute | solution.py:201
  17.6 21.2 %collective-permute-start.1 = (bf16[40,4096]{1,0:T(8,128)(2,1)}, bf16[40,4096]{1,0:T(8,128)(2,1)S(1)}, u32[]{:S(2)}, u32[]{:S(2)}) collective-permute-start(bf16[40,4096]{1,0:T(8,128)(2,1)} %shard_map.163.own_ref), channel_id=1, source_target_pairs={{1,2},{3,4},{5,6},{7,8},{9,10},{11,12},{13,14},{2,1},{4,3},{6,5},{... | collective-permute-start | bytes 983048 | tf_op jit(solution)/shard_map/ppermute | solution.py:406
  22.5 46.4 %collective-permute-start.12 = (bf16[1,2,24,4096]{3,2,1,0:T(8,128)(2,1)S(1)}, bf16[1,2,24,4096]{3,2,1,0:T(8,128)(2,1)S(1)}, u32[]{:S(2)}, u32[]{:S(2)}) collective-permute-start(bf16[1,2,24,4096]{3,2,1,0:T(8,128)(2,1)S(1)} %maximum_bitcast_fusion.refs_0_), channel_id=1, source_target_pairs={{0,1},{1,0},{2,3},{3,2},{4,5},{5,4},{6,7},{7,6},{8,9},{9,8},{10,11... | collective-permute-start | bytes 1179656 | tf_op jit(solution)/shard_map/ppermute | solution.py:201
  22.6 52.3 %collective-permute-start.13 = (bf16[1,2,24,4096]{3,2,1,0:T(8,128)(2,1)S(1)}, bf16[1,2,24,4096]{3,2,1,0:T(8,128)(2,1)S(1)}, u32[]{:S(2)}, u32[]{:S(2)}) collective-permute-start(bf16[1,2,24,4096]{3,2,1,0:T(8,128)(2,1)S(1)} %collective-permute-done.9.refs_1_), channel_id=1, source_target_pairs={{0,1},{1,0},{2,3},{3,2},{4,5},{5,4},{6,7},{7,6},{8,9},{9,8},{10,11... | collective-permute-start | bytes 1179656 | tf_op jit(solution)/shard_map/ppermute | solution.py:201
  25.4 49.5 %collective-permute-start.14 = (bf16[1,2,24,4096]{3,2,1,0:T(8,128)(2,1)S(1)}, bf16[1,2,24,4096]{3,2,1,0:T(8,128)(2,1)S(1)}, u32[]{:S(2)}, u32[]{:S(2)}) collective-permute-start(bf16[1,2,24,4096]{3,2,1,0:T(8,128)(2,1)S(1)} %collective-permute-done.10.refs_2_), channel_id=1, source_target_pairs={{0,1},{1,0},{2,3},{3,2},{4,5},{5,4},{6,7},{7,6},{8,9},{9,8},{10,11... | collective-permute-start | bytes 1179656 | tf_op jit(solution)/shard_map/ppermute | solution.py:201
  33.8 41.1 %collective-permute-start.15 = (bf16[1,2,24,4096]{3,2,1,0:T(8,128)(2,1)S(1)}, bf16[1,2,24,4096]{3,2,1,0:T(8,128)(2,1)}, u32[]{:S(2)}, u32[]{:S(2)}) collective-permute-start(bf16[1,2,24,4096]{3,2,1,0:T(8,128)(2,1)S(1)} %collective-permute-done.11.refs_3_), channel_id=1, source_target_pairs={{0,1},{1,0},{2,3},{3,2},{4,5},{5,4},{6,7},{7,6},{8,9},{9,8},{10,11... | collective-permute-start | bytes 1179656 | tf_op jit(solution)/shard_map/ppermute | solution.py:201
  38.8 1.6 %copy-start = (bf16[128,2,4096]{2,1,0:T(2,128)(2,1)S(1)}, bf16[128,2,4096]{2,1,0:T(2,128)(2,1)}, u32[]{:S(2)}) copy-start(bf16[128,2,4096]{2,1,0:T(2,128)(2,1)} %kv_ref.3) | copy-start | bytes 6291460
  40.4 1.0 copy-start.1
  46.2 1.3 %collective-permute-start.2 = (f32[48,128]{1,0:T(8,128)S(1)}, f32[48,128]{1,0:T(8,128)S(1)}, u32[]{:S(2)}, u32[]{:S(2)}) collective-permute-start(f32[48,128]{1,0:T(8,128)S(1)} %shard_map.164.st_ref), channel_id=1, source_target_pairs={{0,1},{1,0},{2,3},{3,2},{4,5},{5,4},{6,7},{7,6},{8,9},{9,8},{10,11... | collective-permute-start | bytes 73736 | tf_op jit(solution)/shard_map/ppermute | solution.py:403
  47.5 5.7 %collective-permute-start.3 = (f32[48,128]{1,0:T(8,128)S(1)}, f32[48,128]{1,0:T(8,128)S(1)}, u32[]{:S(2)}, u32[]{:S(2)}) collective-permute-start(f32[48,128]{1,0:T(8,128)S(1)} %shard_map.164.st_ref), channel_id=1, source_target_pairs={{1,2},{3,4},{5,6},{7,8},{9,10},{11,12},{13,14},{2,1},{4,3},{6,5},{... | collective-permute-start | bytes 73736 | tf_op jit(solution)/shard_map/ppermute | solution.py:406
  53.2 5.1 %collective-permute-start.4 = (f32[48,128]{1,0:T(8,128)S(1)}, f32[48,128]{1,0:T(8,128)S(1)}, u32[]{:S(2)}, u32[]{:S(2)}) collective-permute-start(f32[48,128]{1,0:T(8,128)S(1)} %collective-permute-done.2.st_sib_ref), channel_id=1, source_target_pairs={{1,2},{3,4},{5,6},{7,8},{9,10},{11,12},{13,14},{2,1},{4,3},{6,5},{... | collective-permute-start | bytes 73736 | tf_op jit(solution)/shard_map/ppermute | solution.py:406
  58.4 1.2 collective-permute-start.5
  68.7 21.7 %collective-permute-start.6 = (bf16[16,4096]{1,0:T(8,128)(2,1)S(1)}, bf16[16,4096]{1,0:T(8,128)(2,1)S(1)}, u32[]{:S(2)}, u32[]{:S(2)}) collective-permute-start(bf16[16,4096]{1,0:T(8,128)(2,1)S(1)} %get-tuple-element.27), channel_id=1, source_target_pairs={{0,1},{1,0},{2,3},{3,2},{4,5},{5,4},{6,7},{7,6},{8,9},{9,8},{10,11... | collective-permute-start | bytes 393224 | tf_op jit(solution)/shard_map/ppermute | solution.py:403
  68.9 21.5 %collective-permute-start.7 = (bf16[16,4096]{1,0:T(8,128)(2,1)S(1)}, bf16[16,4096]{1,0:T(8,128)(2,1)S(1)}, u32[]{:S(2)}, u32[]{:S(2)}) collective-permute-start(bf16[16,4096]{1,0:T(8,128)(2,1)S(1)} %get-tuple-element.28), channel_id=1, source_target_pairs={{1,2},{3,4},{5,6},{7,8},{9,10},{11,12},{13,14},{2,1},{4,3},{6,5},{... | collective-permute-start | bytes 393224 | tf_op jit(solution)/shard_map/ppermute | solution.py:406
  89.5 0.9 copy-start.2
  90.4 2.3 %collective-permute-start.16 = (bf16[4,24,4096]{2,1,0:T(8,128)(2,1)S(1)}, bf16[4,24,4096]{2,1,0:T(8,128)(2,1)S(1)}, u32[]{:S(2)}, u32[]{:S(2)}) collective-permute-start(bf16[4,24,4096]{2,1,0:T(8,128)(2,1)S(1)} %get-tuple-element.33), channel_id=1, source_target_pairs={{0,1},{1,0},{2,3},{3,2},{4,5},{5,4},{6,7},{7,6},{8,9},{9,8},{10,11... | collective-permute-start | bytes 2359304 | tf_op jit(solution)/shard_map/ppermute | solution.py:201
  92.7 0.9 copy-start.4
  95.9 11.4 %collective-permute-start.17 = (bf16[24,4096]{1,0:T(8,128)(2,1)}, bf16[24,4096]{1,0:T(8,128)(2,1)S(1)}, u32[]{:S(2)}, u32[]{:S(2)}) collective-permute-start(bf16[24,4096]{1,0:T(8,128)(2,1)} %get-tuple-element.35), channel_id=1, source_target_pairs={{0,2},{1,3},{2,0},{3,1},{4,6},{5,7},{6,4},{7,5},{8,10},{9,11},{10,... | collective-permute-start | bytes 589832 | tf_op jit(solution)/shard_map/ppermute | solution.py:201
  98.3 9.0 %collective-permute-start.18 = (bf16[24,4096]{1,0:T(8,128)(2,1)}, bf16[24,4096]{1,0:T(8,128)(2,1)S(1)}, u32[]{:S(2)}, u32[]{:S(2)}) collective-permute-start(bf16[24,4096]{1,0:T(8,128)(2,1)} %get-tuple-element.36), channel_id=1, source_target_pairs={{0,4},{1,5},{2,6},{3,7},{4,0},{5,1},{6,2},{7,3},{8,12},{9,13},{10,... | collective-permute-start | bytes 589832 | tf_op jit(solution)/shard_map/ppermute | solution.py:201
  99.4 10.0 %collective-permute-start.19 = (bf16[24,4096]{1,0:T(8,128)(2,1)}, bf16[24,4096]{1,0:T(8,128)(2,1)S(1)}, u32[]{:S(2)}, u32[]{:S(2)}) collective-permute-start(bf16[24,4096]{1,0:T(8,128)(2,1)} %get-tuple-element.37), channel_id=1, source_target_pairs={{0,6},{1,7},{2,4},{3,5},{4,2},{5,3},{6,0},{7,1},{8,14},{9,15},{10,... | collective-permute-start | bytes 589832 | tf_op jit(solution)/shard_map/ppermute | solution.py:201
  100.1 14.5 %copy-start.3 = (bf16[160,4096]{1,0:T(8,128)(2,1)S(1)}, bf16[160,4096]{1,0:T(8,128)(2,1)}, u32[]{:S(2)}) copy-start(bf16[160,4096]{1,0:T(8,128)(2,1)} %get-tuple-element.42) | copy-start | bytes 3932164
  107.3 2.1 %copy-start.5 = (bf16[24,4096]{1,0:T(8,128)(2,1)}, bf16[24,4096]{1,0:T(8,128)(2,1)S(1)}, u32[]{:S(2)}) copy-start(bf16[24,4096]{1,0:T(8,128)(2,1)S(1)} %collective-permute-done.17.refs_1_) | copy-start | bytes 589828
  107.3 2.1 %copy-start.6 = (bf16[24,4096]{1,0:T(8,128)(2,1)}, bf16[24,4096]{1,0:T(8,128)(2,1)S(1)}, u32[]{:S(2)}) copy-start(bf16[24,4096]{1,0:T(8,128)(2,1)S(1)} %collective-permute-done.18.refs_2_) | copy-start | bytes 589828
  109.4 0.7 copy-start.7
  112.2 8.2 %collective-permute-start.20 = (bf16[16,4096]{1,0:T(8,128)(2,1)}, bf16[16,4096]{1,0:T(8,128)(2,1)S(1)}, u32[]{:S(2)}, u32[]{:S(2)}) collective-permute-start(bf16[16,4096]{1,0:T(8,128)(2,1)} %get-tuple-element.39), channel_id=1, source_target_pairs={{0,12},{1,13},{2,14},{3,15},{4,8},{5,9},{6,10},{7,11},{8,4},{9,5},... | collective-permute-start | bytes 393224 | tf_op jit(solution)/shard_map/ppermute | solution.py:201
  120.4 0.7 copy-start.8

commit v2 on v1

v2 whole, which is shorter than its diff:
```python
import functools

import jax
import jax.numpy as jnp
from jax import lax
from jax.experimental import pallas as pl
from jax.experimental.pallas import tpu as pltpu
from jax.sharding import PartitionSpec as P

D = 4096
HEADS = 32
HEAD_DIM = 128
EXPERTS = 2
CAP = 10
SCALE = 0.125
NONE = -1e30
LANES = 128
BLOCK = 24
GATE_ROW = 20
PIECE = 512
MAIN_LIMIT = 14 * 2**20
SMALL_LIMIT = 56 * 2**20


def iota(shape, dim):
    return lax.broadcasted_iota(jnp.int32, shape, dim)


def one_hot(mask):
    return jnp.where(mask, 1.0, 0.0).astype(jnp.bfloat16)


def mm(a, b, dims=((1,), (0,))):
    return lax.dot_general(a, b, (dims, ((), ())), preferred_element_type=jnp.float32)


def slots_of(ids, keep, expert):
    tokens = ids.shape[1]
    row, col = iota((tokens, tokens), 0), iota((tokens, tokens), 1)
    chosen = (ids == expert) & (keep == 1)
    chosen_f = jnp.where(chosen, 1.0, 0.0)
    as_column = jnp.sum(jnp.where(row == col, chosen_f, 0.0), axis=1, keepdims=True)
    earlier = jnp.sum(jnp.where(row < col, as_column, 0.0), axis=0, keepdims=True)
    slot = earlier.astype(jnp.int32)
    return jnp.where(chosen & (slot < CAP), slot, -1)


def pack_kernel(
    mine, ids_ref, keep_ref, gate_ref, input_ref, grad_ref, query_ref, ctx_ref, segments_ref,
    own_ref, other_ref, tokens_ref,
):
    pack_tokens(query_ref, ctx_ref, segments_ref, tokens_ref)
    ids, keep = ids_ref[...], keep_ref[...]
    tokens = ids.shape[1]
    gate = gate_ref[...].astype(jnp.float32)
    moe_input, moe_grad = input_ref[...], grad_ref[...]
    expert = mine()
    row = iota((BLOCK, tokens), 0)
    input_slot = jnp.where(row < 8, row, jnp.where((row == 16) | (row == 17), row - 8, -2))
    grad_slot = jnp.where(
        (row >= 8) & (row < 16), row - 8, jnp.where((row == 18) | (row == 19), row - 10, -2)
    )
    diagonal = iota((tokens, tokens), 0) == iota((tokens, tokens), 1)
    gate_column = jnp.sum(jnp.where(diagonal, gate, 0.0), axis=1, keepdims=True)
    for which, out_ref in ((expert, own_ref), (1 - expert, other_ref)):
        slot = slots_of(ids, keep, which)
        block = mm(one_hot(input_slot == slot), moe_input) + mm(one_hot(grad_slot == slot), moe_grad)
        slot_column = jnp.sum(jnp.where(diagonal, slot, 0), axis=1, keepdims=True)
        gates = jnp.sum(
            jnp.where(slot_column == iota((tokens, LANES), 1), gate_column, 0.0), axis=0, keepdims=True
        )
        out_ref[...] = block.astype(jnp.bfloat16)
        out_ref[:, :LANES] = (
            block[:, :LANES] + jnp.where(iota((BLOCK, LANES), 0) == GATE_ROW, gates, 0.0)
        ).astype(jnp.bfloat16)


def slot_rows(count):
    rows = iota((count * CAP, 1), 0)
    tail = rows - 8 * count
    source = jnp.where(rows < 8 * count, rows // 8, tail // 2)
    return source, jnp.where(rows < 8 * count, rows % 8, 8 + tail % 2)


def main_kernel(places, *refs):
    blocks, refs = refs[: len(places)], refs[len(places) :]
    w_in_ref, w_out_ref, x_out, g_out, hidden_ref, scaled_ref, keep_ref, send_ref = refs[:8]
    (tails,) = refs[8:]
    count = sum(r.shape[0] for r in blocks) * 2
    rows = count * CAP
    units = count // 2
    width = w_in_ref.shape[1]
    chunk = min(width, 256)
    source, slot = slot_rows(count)
    for block, place in zip(blocks, places):
        for i in range(block.shape[0]):
            at = place + i
            first, second = block[i, 0], block[i, 1]
            x_out[pl.ds(16 * at, 16), :] = jnp.concatenate([first[:8], second[:8]], axis=0)
            g_out[pl.ds(16 * at, 16), :] = jnp.concatenate([first[8:16], second[8:16]], axis=0)
            tails[pl.ds(16 * at, 16), :] = jnp.concatenate([first[16:], second[16:]], axis=0)
    row, col = iota((2 * count, 8 * count), 0), iota((2 * count, 8 * count), 1)
    pick = 8 * (row // 2) + row % 2
    tail = tails[...]
    x_out[pl.ds(8 * count, 2 * count), :] = mm(one_hot(col == pick), tail).astype(jnp.bfloat16)
    g_out[pl.ds(8 * count, 2 * count), :] = mm(one_hot(col == pick + 2), tail).astype(jnp.bfloat16)
    of_row = one_hot(iota((rows, 8 * count), 1) == 8 * source + GATE_ROW - 16)
    gates = mm(of_row, tails[:, :LANES])
    gate = jnp.sum(jnp.where(iota((rows, LANES), 1) == slot, gates, 0.0), axis=1, keepdims=True)

    gate_part = jnp.zeros((rows, 1), jnp.float32)
    for i in range(width // chunk):
        at = pl.ds(i * chunk, chunk)
        pre = mm(x_out[...], w_in_ref[:, at])
        back = mm(g_out[...], w_out_ref[at, :], ((1,), (1,)))
        active = jnp.maximum(pre, 0.0)
        hidden_ref[:, at] = (gate * back * jnp.where(pre > 0, 1.0, 0.0)).astype(jnp.bfloat16)
        scaled_ref[:, at] = (gate * active).astype(jnp.bfloat16)
        gate_part += jnp.sum(active * back, axis=1, keepdims=True)

    lane = iota((rows, LANES), 1)
    placed = jnp.where(lane == 16 * (source % 2) + slot, gate_part, 0.0).astype(jnp.bfloat16)
    at = iota((8 * units, rows), 1)
    unit = jnp.where(at < 8 * count, at // 16, (at - 8 * count) // 4)
    row = iota((8 * units, rows), 0)
    gates = mm(one_hot((row % 8 == GATE_ROW - 16) & (unit == row // 8)), placed)
    row, col = iota((8 * units, 2 * count), 0), iota((8 * units, 2 * count), 1)
    to_end = one_hot((row % 8 < 4) & (col == 4 * (row // 8) + row % 8))
    hidden = hidden_ref[...]
    for start in range(0, D, PIECE):
        lanes = pl.ds(start, PIECE)
        part = mm(hidden, w_in_ref[lanes, :], ((1,), (1,))).astype(jnp.bfloat16)
        ends = mm(to_end, part[8 * count :])
        if start == 0:
            ends = jnp.concatenate([ends[:, :LANES] + gates, ends[:, LANES:]], axis=1)
        ends = ends.astype(jnp.bfloat16)
        for u in range(units):
            half, index = (keep_ref, u) if u < keep_ref.shape[0] else (send_ref, u - keep_ref.shape[0])
            half[index, :16, lanes] = part[16 * u : 16 * u + 16]
            half[index, 16:, lanes] = ends[8 * u : 8 * u + 8]


def weights_kernel(x_ref, hidden_ref, scaled_ref, g_ref, w_in_ref, w_out_ref):
    w_in_ref[...] = mm(x_ref[...], hidden_ref[...], ((0,), (0,))).astype(jnp.bfloat16)
    w_out_ref[...] = mm(scaled_ref[...], g_ref[...], ((0,), (0,))).astype(jnp.bfloat16)


def sum_pairs_kernel(keep_ref, got_ref, own_ref, *out_refs):
    own_ref[...] = keep_ref[0].astype(jnp.float32) + got_ref[0].astype(jnp.float32)
    for i, out_ref in enumerate(out_refs):
        out_ref[...] = (
            keep_ref[i + 1].astype(jnp.float32) + got_ref[i + 1].astype(jnp.float32)
        ).astype(jnp.bfloat16)


def sum_unit_kernel(*refs):
    parts, (own_ref, send_ref) = refs[:-2], refs[-2:]
    unit = parts[0][...].astype(jnp.float32)
    for part in parts[1:]:
        unit = unit + part[...].astype(jnp.float32)
    own_ref[...] = unit
    send_ref[...] = unit[8:].astype(jnp.bfloat16)


def scatter_kernel(mine, ids_ref, keep_ref, own_ref, got_ref, grad_ref, gate_ref):
    ids, keep = ids_ref[...], keep_ref[...]
    tokens = ids.shape[1]
    expert = mine()
    diagonal = iota((tokens, tokens), 0) == iota((tokens, tokens), 1)
    own, got = own_ref[...], got_ref[...].astype(jnp.float32)
    grad = jnp.zeros((tokens, own.shape[1]), jnp.float32)
    gate = jnp.zeros((1, tokens), jnp.float32)
    for which, part, first, tail, lane in (
        (expert, own, 0, 16, 0),
        (1 - expert, got, 0, 10, 16),
    ):
        slot = slots_of(ids, keep, which)
        column = jnp.sum(jnp.where(diagonal, slot, 0), axis=1, keepdims=True)
        row = iota((tokens, part.shape[0]), 1)
        place = jnp.where(column < 8, first + column, tail + column - 8)
        grad = grad + mm(one_hot((row == place) & (column >= 0)), part.astype(jnp.bfloat16))
        gates = part[GATE_ROW - BLOCK + part.shape[0] :][:1, :LANES]
        wide = jnp.where(iota((LANES, tokens), 0) == slot + lane, 1.0, 0.0)
        wide = jnp.where(slot >= 0, wide, 0.0)
        column_gates = jnp.sum(
            jnp.where(iota((LANES, LANES), 0) == iota((LANES, LANES), 1), gates, 0.0), axis=1, keepdims=True
        )
        gate = gate + jnp.sum(wide * column_gates, axis=0, keepdims=True)
    grad_ref[...] = grad.astype(jnp.bfloat16)
    gate_ref[...] = gate


def params(limit=4 * 2**20):
    return pltpu.CompilerParams(vmem_limit_bytes=limit)


def pack_tokens(query_ref, grad_ref, segments_ref, out_ref):
    tokens = query_ref.shape[0]
    out_ref[:tokens, :] = query_ref[...]
    out_ref[tokens : 2 * tokens, :] = grad_ref[...]
    out_ref[2 * tokens :, :] = jnp.zeros((8, out_ref.shape[1]), jnp.bfloat16)
    segments = segments_ref[...] + 1
    diagonal = iota((tokens, tokens), 0) == iota((tokens, tokens), 1)
    column = jnp.sum(jnp.where(diagonal, segments, 0), axis=1, keepdims=True)
    lane = iota((tokens, LANES), 1)
    row = iota((tokens, LANES), 0)
    digits = jnp.zeros((tokens, LANES), jnp.int32)
    for i in range(3):
        digits = digits + jnp.where(lane == row + i * tokens, (column >> (7 * i)) & 127, 0)
    line = jnp.sum(digits, axis=0, keepdims=True).astype(jnp.float32)
    out_ref[2 * tokens :, :LANES] = jnp.where(iota((8, LANES), 0) == 0, line, 0.0).astype(jnp.bfloat16)


def segment_column(token_ref, tokens):
    line = token_ref[2 * tokens :, :LANES][:1].astype(jnp.float32)
    lane, row = iota((tokens, LANES), 1), iota((tokens, LANES), 0)
    weight = jnp.zeros((tokens, LANES), jnp.float32)
    for i in range(3):
        weight = weight + jnp.where(lane == row + i * tokens, float(128**i), 0.0)
    return jnp.sum(weight * line, axis=1, keepdims=True).astype(jnp.int32)


def head_scores(token_refs, kv, head, tokens):
    lanes = pl.ds(head * HEAD_DIM, HEAD_DIM)
    queries = jnp.concatenate([r[:tokens, lanes] for r in token_refs], axis=0)
    grads = jnp.concatenate([r[tokens : 2 * tokens, lanes] for r in token_refs], axis=0)
    both = mm(jnp.concatenate([queries, grads], axis=0), kv, ((1,), (1,)))
    count = queries.shape[0]
    return queries, grads, both[:count], pltpu.roll(both[count:], both.shape[1] - 1, 1)


def allowed_pairs(token_refs, rows_ref, tokens):
    column = jnp.concatenate([segment_column(r, tokens) for r in token_refs], axis=0)
    rows = rows_ref[...] + 1
    count = rows.shape[1]
    diagonal = iota((count, count), 0) == iota((count, count), 1)
    as_column = jnp.sum(jnp.where(diagonal, rows, 0), axis=1, keepdims=True)
    even = iota((count, 2 * count), 1) == 2 * iota((count, 2 * count), 0)
    spread = jnp.sum(jnp.where(even, as_column, 0), axis=0, keepdims=True)
    return jnp.where(spread > 0, spread, -1) == column


def load_head(kv_ref, head):
    rows = kv_ref.shape[0]
    return kv_ref[:, :, pl.ds(head * HEAD_DIM, HEAD_DIM)].reshape(2 * rows, HEAD_DIM)


def stats_kernel(own_ref, sib_ref, near_ref, rows_ref, kv_ref, stats_ref):
    token_refs = (own_ref, sib_ref, near_ref)
    tokens = (own_ref.shape[0] - 8) // 2
    allowed = allowed_pairs(token_refs, rows_ref, tokens)
    lane = iota((3 * tokens, LANES), 1)
    stats = jnp.zeros((3 * tokens, LANES), jnp.float32)
    for head in range(HEADS):
        _, _, scores, prob_grad = head_scores(token_refs, load_head(kv_ref, head), head, tokens)
        scores = jnp.where(allowed, SCALE * scores, NONE)
        peak = jnp.max(scores, axis=1, keepdims=True)
        weight = jnp.where(allowed, jnp.exp(scores - peak), 0.0)
        mass = jnp.sum(weight, axis=1, keepdims=True)
        delta = jnp.sum(weight * prob_grad, axis=1, keepdims=True)
        stats = jnp.where(lane == head, peak, stats)
        stats = jnp.where(lane == HEADS + head, mass, stats)
        stats = jnp.where(lane == 2 * HEADS + head, delta, stats)
    stats_ref[...] = stats


def merged(parts):
    peaks = [jnp.where(p[:, HEADS : 2 * HEADS] > 0, p[:, :HEADS], NONE) for p in parts]
    peak = jnp.maximum(jnp.maximum(peaks[0], peaks[1]), peaks[2])
    scale = [jnp.exp(p - peak) for p in peaks]
    mass = sum(s * p[:, HEADS : 2 * HEADS] for s, p in zip(scale, parts))
    delta = sum(s * p[:, 2 * HEADS : 3 * HEADS] for s, p in zip(scale, parts))
    inverse = jnp.where(mass > 0, 1.0 / mass, 0.0)
    return peak, inverse, delta * inverse


def grads_kernel(
    own_ref, sib_ref, near_ref, rows_ref, kv_ref, st_ref, st_sib_ref, st_near_ref, st_far_ref, st_side_ref,
    query_ref, to_sib_ref, to_near_ref, kv_grad_ref,
):
    token_refs = (own_ref, sib_ref, near_ref)
    tokens = (own_ref.shape[0] - 8) // 2
    allowed = allowed_pairs(token_refs, rows_ref, tokens)
    a, b, c = slice(0, tokens), slice(tokens, 2 * tokens), slice(2 * tokens, 3 * tokens)
    totals = [
        merged((st_ref[a], st_sib_ref[b], st_near_ref[c])),
        merged((st_ref[b], st_sib_ref[a], st_side_ref[c])),
        merged((st_ref[c], st_near_ref[a], st_far_ref[b])),
    ]
    peak, scale, delta = (jnp.concatenate([t[i] for t in totals], axis=0) for i in range(3))
    for head in range(HEADS):
        kv = load_head(kv_ref, head)
        queries, grads, scores, prob_grad = head_scores(token_refs, kv, head, tokens)
        at = slice(head, head + 1)
        probs = jnp.exp(jnp.where(allowed, SCALE * scores - peak[:, at], NONE)) * scale[:, at]
        score_grad = SCALE * (probs * (prob_grad - delta[:, at]))
        moved = pltpu.roll(probs, 1, 1)
        score_low = score_grad.astype(jnp.bfloat16)
        query = mm(score_low, kv)
        lanes = pl.ds(head * HEAD_DIM, HEAD_DIM)
        query_ref[:, lanes] = query[a]
        to_sib_ref[:, lanes] = query[b].astype(jnp.bfloat16)
        to_near_ref[:, lanes] = query[c].astype(jnp.bfloat16)
        both = jnp.concatenate([score_low, moved.astype(jnp.bfloat16)], axis=0)
        grad = mm(both, jnp.concatenate([queries, grads], axis=0), ((0,), (0,)))
        kv_grad_ref[:, :, lanes] = grad.astype(jnp.bfloat16).reshape(kv_grad_ref.shape[0], 2, HEAD_DIM)


def core(block):
    return lax.ppermute(block, "seq", [(i, i ^ 1) for i in range(lax.axis_size("seq"))])


def cross(block):
    crossing = [(i, i + 1) for i in range(1, lax.axis_size("seq") - 1, 2)]
    return lax.ppermute(block, "seq", crossing + [(j, i) for i, j in crossing])


def attention_stats(held):
    tokens = (held[0].shape[0] - 8) // 2
    return pl.pallas_call(
        stats_kernel,
        out_shape=jax.ShapeDtypeStruct((3 * tokens, LANES), jnp.float32),
        compiler_params=params(12 * 2**20),
        cost_estimate=pl.CostEstimate(flops=10**9, bytes_accessed=16 * 10**6, transcendentals=0),
    )(*held)


def attention_grads(held, stats):
    tokens = (held[0].shape[0] - 8) // 2
    low = jax.ShapeDtypeStruct((tokens, D), jnp.bfloat16)
    return pl.pallas_call(
        grads_kernel,
        out_shape=(
            jax.ShapeDtypeStruct((tokens, D), jnp.float32),
            low,
            low,
            jax.ShapeDtypeStruct(held[-1].shape, jnp.bfloat16),
        ),
        compiler_params=params(12 * 2**20),
        cost_estimate=pl.CostEstimate(flops=10**9, bytes_accessed=32 * 10**6, transcendentals=0),
    )(*held, *stats)


def after(value, *others):
    return lax.optimization_barrier((value, *others))[0]


def far(value):
    return pltpu.with_memory_space_constraint(value, pltpu.HBM)


def fetch_kernel(count, *refs):
    arrived = refs[2 * count]
    copies = [
        pltpu.make_async_copy(refs[i], refs[count + i], arrived.at[i]) for i in range(count)
    ]
    for copy in copies:
        copy.start()
    for copy in copies:
        copy.wait()


def fetch(*arrays):
    return pl.pallas_call(
        functools.partial(fetch_kernel, len(arrays)),
        in_specs=[pl.BlockSpec(memory_space=pltpu.HBM)] * len(arrays),
        out_specs=[pl.BlockSpec(memory_space=pltpu.VMEM)] * len(arrays),
        out_shape=[jax.ShapeDtypeStruct(a.shape, a.dtype) for a in arrays],
        scratch_shapes=[pltpu.SemaphoreType.DMA((len(arrays),))],
        compiler_params=params(24 * 2**20),
        cost_estimate=pl.CostEstimate(
            flops=0, bytes_accessed=sum(a.size * 2 for a in arrays), transcendentals=0
        ),
    )(*map(far, arrays))


def local(
    dec_query,
    ctx_grad,
    dec_segments,
    enc_kv,
    enc_segments,
    moe_input,
    moe_grad,
    gate_prob,
    expert_ids,
    keep_mask,
    w_input,
    w_output,
):
    devices = lax.axis_size("seq")
    shards = devices // EXPERTS
    tokens = moe_input.shape[0]
    width = w_input.shape[1]
    square = shards == 8

    def mine():
        return lax.axis_index("seq") // shards

    def flip(block, bits):
        return lax.ppermute(block, "seq", [(i, i ^ bits) for i in range(devices)])

    ids, keep = expert_ids.reshape(1, tokens), keep_mask.reshape(1, tokens)
    block_type = jax.ShapeDtypeStruct((BLOCK, D), jnp.bfloat16)
    own, other, packed = pl.pallas_call(
        functools.partial(pack_kernel, mine),
        out_shape=(block_type, block_type, jax.ShapeDtypeStruct((2 * tokens + 8, D), jnp.bfloat16)),
        compiler_params=params(8 * 2**20),
    )(
        *map(far, (ids, keep, gate_prob.reshape(1, tokens), moe_input, moe_grad)),
        *map(far, (dec_query, ctx_grad, dec_segments.reshape(1, tokens))),
    )
    across = (devices - 1) & ~3
    got = flip(other, across)
    near_w_input, near_w_output, near_kv = w_input, w_output, enc_kv
    if square:
        near_w_input, near_w_output, near_kv = fetch(w_input, w_output, enc_kv)
    held = (packed, core(packed), cross(packed), far(enc_segments.reshape(1, -1)), near_kv)
    stats = attention_stats(held)
    stats_sib, stats_near = core(stats), cross(stats)

    pair = jnp.stack([own, got])
    if square:
        pair = after(pair, held[1], held[2], near_w_input)
        near = [pair, flip(pair, 2), flip(pair, 4), flip(pair, 6)]
        *near, stats, stats_sib, stats_near = lax.optimization_barrier(
            (*near, stats, stats_sib, stats_near)
        )
        blocks = [b[None] for b in near + [flip(b, 1) for b in near]]
    else:
        halves = [list(range(e * shards, (e + 1) * shards)) for e in range(EXPERTS)]
        blocks = [lax.all_gather(pair[None], "seq", axis_index_groups=halves, tiled=True)]
    places, at = [], 0
    for b in blocks:
        places.append(at)
        at += b.shape[0]
    sources = 2 * at
    rows = sources * CAP
    keep_units = shards // 2
    slots = jax.ShapeDtypeStruct((rows, D), jnp.bfloat16)
    hidden_type = jax.ShapeDtypeStruct((rows, width), jnp.bfloat16)
    units_type = jax.ShapeDtypeStruct((keep_units, BLOCK, D), jnp.bfloat16)
    x, g, hidden, scaled, keep_half, send_half = pl.pallas_call(
        functools.partial(main_kernel, places),
        out_shape=[slots, slots, hidden_type, hidden_type, units_type, units_type],
        in_specs=[pl.BlockSpec(memory_space=pltpu.VMEM)] * len(places)
        + [pl.BlockSpec(memory_space=pltpu.VMEM)] * 2,
        scratch_shapes=[pltpu.VMEM((8 * sources, D), jnp.bfloat16)],
        compiler_params=params(MAIN_LIMIT if square else 62 * 2**20),
        cost_estimate=pl.CostEstimate(flops=6 * rows * D * width, bytes_accessed=4 * D * width, transcendentals=0),
    )(*blocks, near_w_input, near_w_output)

    unit_wide = jax.ShapeDtypeStruct((BLOCK, D), jnp.float32)
    tail_type = jax.ShapeDtypeStruct((BLOCK - 8, D), jnp.bfloat16)
    if square:
        swapped = flip(send_half, 1)
        stats_sib, stats_near = after((stats_sib, stats_near), keep_half)
        stats_far, stats_side = cross(stats_sib), core(stats_near)
        summed = pl.pallas_call(
            sum_pairs_kernel,
            out_shape=[unit_wide] + [block_type] * 3,
            compiler_params=params(),
        )(keep_half, swapped)
        parts = [summed[0], flip(summed[1], 2), flip(summed[2], 4), flip(summed[3], 6)]
        all_stats = after((stats, stats_sib, stats_near, stats_far, stats_side), summed[0])
    else:
        units = jnp.concatenate([keep_half, send_half]).astype(jnp.float32)
        parts = [
            lax.psum_scatter(units, "seq", axis_index_groups=halves, tiled=True).reshape(BLOCK, D)
        ]
        all_stats = (stats, stats_sib, stats_near, cross(stats_sib), core(stats_near))
    query, to_sib, to_near, kv_grad = attention_grads(held, all_stats)
    parts[0] = after(parts[0], query)
    own_unit, send_unit = pl.pallas_call(
        sum_unit_kernel, out_shape=(unit_wide, tail_type), compiler_params=params()
    )(*parts)
    returned = flip(send_unit, across)
    to_sib, to_near = after((to_sib, to_near), own_unit)
    query_grad = query + core(to_sib).astype(jnp.float32) + cross(to_near).astype(jnp.float32)

    x, hidden, scaled, g = after((x, hidden, scaled, g), own_unit)
    pieces = max(1, min(4, width // 128))
    once = pl.Buffered(1)
    w_input_grad, w_output_grad = pl.pallas_call(
        weights_kernel,
        grid=(pieces,),
        in_specs=[
            pl.BlockSpec((rows, D // pieces), lambda i: (0, i)),
            pl.BlockSpec((rows, width), lambda i: (0, 0), pipeline_mode=once),
            pl.BlockSpec((rows, width // pieces), lambda i: (0, i)),
            pl.BlockSpec((rows, D), lambda i: (0, 0), pipeline_mode=once),
        ],
        out_specs=[
            pl.BlockSpec((D // pieces, width), lambda i: (i, 0)),
            pl.BlockSpec((width // pieces, D), lambda i: (i, 0)),
        ],
        out_shape=[
            jax.ShapeDtypeStruct((D, width), jnp.bfloat16),
            jax.ShapeDtypeStruct((width, D), jnp.bfloat16),
        ],
        compiler_params=params(24 * 2**20),
        cost_estimate=pl.CostEstimate(flops=4 * rows * D * width, bytes_accessed=4 * D * width, transcendentals=0),
    )(x, hidden, scaled, g)

    moe_input_grad, gate_grad = pl.pallas_call(
        functools.partial(scatter_kernel, mine),
        out_shape=(
            jax.ShapeDtypeStruct((tokens, D), jnp.bfloat16),
            jax.ShapeDtypeStruct((1, tokens), jnp.float32),
        ),
        compiler_params=params(),
    )(ids, keep, own_unit, returned)
    return (
        query_grad.astype(jnp.bfloat16),
        kv_grad,
        moe_input_grad,
        gate_grad.reshape(tokens),
        w_input_grad,
        w_output_grad,
    )


def solution(mesh):
    return jax.shard_map(
        local,
        mesh=mesh,
        in_specs=(
            P(("groups", "seq"), None),
            P(("groups", "seq"), None),
            P(("groups", "seq")),
            P(("groups", "seq"), None, None),
            P(("groups", "seq")),
            P(("groups", "seq"), None),
            P(("groups", "seq"), None),
            P(("groups", "seq")),
            P(("groups", "seq")),
            P(("groups", "seq")),
            P(None, "seq"),
            P("seq", None),
        ),
        out_specs=(
            P(("groups", "seq"), None),
            P(("groups", "seq"), None, None),
            P(("groups", "seq"), None),
            P(("groups", "seq")),
            P("groups", "seq"),
            P("seq", "groups"),
        ),
        check_vma=False,
    )
```

time: 125 us -> 89.1 us (0.71)
  starting transfers between devices: 43.8 us -> 30.6 us
  matrix products: 13 us -> 0 us
  local copies, waits for them, and re-layouts: 6.55 us -> 0.01 us
  waiting for transfers between devices: 18.1 us -> 14.4 us
  Pallas kernels: 39.2 us -> 40.8 us
    dot_general x2 -> x0, matrix products: 13 us -> none  [mm(): lax.dot_general(a, b, (dims, ((), ())), preferred_element_type=jnp.float32)]
    ppermute x13, starting transfers between devices: 23.9 us -> 11.1 us  [flip(): return lax.ppermute(block, 'seq', [(i, i ^ bits) for i in range(devices)])]
    ppermute x13, waiting for transfers between devices: 11.1 us -> 4.39 us  [flip(): return lax.ppermute(block, 'seq', [(i, i ^ bits) for i in range(devices)])]
    unnamed x18 -> x4, local copies, waits for them, and re-layouts: 5.67 us -> 0.01 us
    ppermute x4, waiting for transfers between devices: 4.69 us -> 9.96 us  [cross(): return lax.ppermute(block, 'seq', crossing + [(j, i) for i, j in crossing])]
    ppermute x4, waiting for transfers between devices: 2.38 us -> 0.01 us  [core(): lax.ppermute(block, 'seq', [(i, i ^ 1) for i in range(lax.axis_size('seq'...]
    pallas_call x8 -> x9, Pallas kernels: 39.2 us -> 40.8 us  [the longest x1 9.89 us: attention_grads(): pl.pallas_call(grads_kernel, out_shape=(jax.ShapeDtypeStruct((tokens, D),...]
  transfers between devices with their start and end apart: 21 -> 21, of which waited for: 10 -> 8; matrix products, arithmetic and copies ran while one was open for 13% -> 0% of each run, Pallas kernels for 25% -> 34%
where the time goes in v2:
time: 89.1 us; the launch traced here: 87.3 us
  Pallas kernels  40.8 us (46%)
  starting transfers between devices  30.6 us (34%)
  waiting for transfers between devices  14.4 us (16%)
    ppermute x4, starting transfers between devices, cross(): return lax.ppermute(block, 'seq', crossing + [(j, i) for i, j in crossing])  19.2 us
    ppermute x13, starting transfers between devices, flip(): return lax.ppermute(block, 'seq', [(i, i ^ bits) for i in range(devices)])  11.1 us
    ppermute x4, waiting for transfers between devices, cross(): return lax.ppermute(block, 'seq', crossing + [(j, i) for i, j in crossing])  9.96 us
    pallas_call x1, Pallas kernels, attention_grads(): pl.pallas_call(grads_kernel, out_shape=(jax.ShapeDtypeStruct((tokens, D),...  9.89 us
    pallas_call x1, Pallas kernels, local(): pl.pallas_call(functools.partial(main_kernel, places), out_shape=[slots,...  8.95 us
    pallas_call x1, Pallas kernels, local(): pl.pallas_call(weights_kernel, grid=(pieces,), in_specs=[pl.BlockSpec((ro...  6.92 us
    pallas_call x1, Pallas kernels, fetch(): pl.pallas_call(functools.partial(fetch_kernel, len(arrays)), in_specs=[pl...  6.39 us
    pallas_call x1, Pallas kernels, attention_stats(): pl.pallas_call(stats_kernel, out_shape=jax.ShapeDtypeStruct((3 * tokens,...  5.63 us
  transfers between devices with their start and end apart: 21, of which 8 were waited for; matrix products, arithmetic and copies ran while one was open for 0% of the time, Pallas kernels for 34%

profile of v2, /device:TPU:1, one launch (start us, length us, event | category | flops | bytes accessed | tf_op | source)
XLA Modules:
  0.0 87.3 jit_solution(14790647749665355707)
XLA Ops:
  0.6 1.7 %shard_map.163 = (bf16[24,4096]{1,0:T(8,128)(2,1)S(1)}, bf16[24,4096]{1,0:T(8,128)(2,1)S(1)}, bf16[40,4096]{1,0:T(8,128)(2,1)S(1)}) custom-call(s32[1,16]{1,0:T(1,128)} %bitcast.25, s32[1,16]{1,0:T(1,128)} %bitcast.27, bf16[1,16]{1,0:T(2,128)(2,1)} %bitcast.30, bf16[16,4096]{1,0:T(8,128)(2,1)} %input_ref.1, bf16[16,4096]{1,0:T(8,128)(2,1)} %grad_ref.1, ...), custom_call_target="tpu_custom_call" | custom-call | tf_op jit(solution)/shard_map/pallas_call | solution.py:405
  2.3 4.2 %collective-permute-start.2 = (bf16[24,4096]{1,0:T(8,128)(2,1)S(1)}, bf16[24,4096]{1,0:T(8,128)(2,1)S(1)}, u32[]{:S(2)}, u32[]{:S(2)}) collective-permute-start(bf16[24,4096]{1,0:T(8,128)(2,1)S(1)} %get-tuple-element.57), channel_id=1, source_target_pairs={{0,12},{1,13},{2,14},{3,15},{4,8},{5,9},{6,10},{7,11},{8,4},{9,5},... | collective-permute-start | bytes 589832 | tf_op jit(solution)/shard_map/ppermute | solution.py:401
  6.5 4.0 %collective-permute-start.1 = (bf16[40,4096]{1,0:T(8,128)(2,1)S(1)}, bf16[40,4096]{1,0:T(8,128)(2,1)S(1)}, u32[]{:S(2)}, u32[]{:S(2)}) collective-permute-start(bf16[40,4096]{1,0:T(8,128)(2,1)S(1)} %get-tuple-element.54.own_ref), channel_id=1, source_target_pairs={{1,2},{3,4},{5,6},{7,8},{9,10},{11,12},{13,14},{2,1},{4,3},{6,5},{... | collective-permute-start | bytes 983048 | tf_op jit(solution)/shard_map/ppermute | solution.py:315
  10.6 6.4 %shard_map.164 = (bf16[4096,1024]{1,0:T(8,128)(2,1)S(1)}, bf16[1024,4096]{1,0:T(8,128)(2,1)S(1)}, bf16[128,2,4096]{2,1,0:T(2,128)(2,1)S(1)}) custom-call(bf16[4096,1024]{1,0:T(8,128)(2,1)} %refs_0_.1, bf16[1024,4096]{1,0:T(8,128)(2,1)} %refs_1_.1, bf16[128,2,4096]{2,1,0:T(2,128)(2,1)} %refs_2_.1), custom_call_target="tpu_custom_call" | custom-call | bytes 18874368 | tf_op jit(solution)/shard_map/pallas_call | solution.py:364
  17.1 1.0 %collective-permute-done.1.near_ref = bf16[40,4096]{1,0:T(8,128)(2,1)S(1)} collective-permute-done((bf16[40,4096]{1,0:T(8,128)(2,1)S(1)}, bf16[40,4096]{1,0:T(8,128)(2,1)S(1)}, u32[]{:S(2)}, u32[]{:S(2)}) %collective-permute-start.1) | collective-permute-done | bytes 327712 | tf_op jit(solution)/shard_map/ppermute | solution.py:315
  18.0 1.7 %collective-permute-start.5 = (bf16[2,24,4096]{2,1,0:T(8,128)(2,1)S(1)}, bf16[2,24,4096]{2,1,0:T(8,128)(2,1)S(1)}, u32[]{:S(2)}, u32[]{:S(2)}) collective-permute-start(bf16[2,24,4096]{2,1,0:T(8,128)(2,1)S(1)} %pad_maximum_fusion), channel_id=1, source_target_pairs={{0,6},{1,7},{2,4},{3,5},{4,2},{5,3},{6,0},{7,1},{8,14},{9,15},{10,... | collective-permute-start | bytes 1179656 | tf_op jit(solution)/shard_map/ppermute | solution.py:401
  19.8 0.9 %collective-permute-start.3 = (bf16[2,24,4096]{2,1,0:T(8,128)(2,1)S(1)}, bf16[2,24,4096]{2,1,0:T(8,128)(2,1)S(1)}, u32[]{:S(2)}, u32[]{:S(2)}) collective-permute-start(bf16[2,24,4096]{2,1,0:T(8,128)(2,1)S(1)} %pad_maximum_fusion), channel_id=1, source_target_pairs={{0,2},{1,3},{2,0},{3,1},{4,6},{5,7},{6,4},{7,5},{8,10},{9,11},{10,... | collective-permute-start | bytes 1179656 | tf_op jit(solution)/shard_map/ppermute | solution.py:401
  20.7 5.6 %shard_map.165.st_ref = f32[48,128]{1,0:T(8,128)S(1)} custom-call(bf16[40,4096]{1,0:T(8,128)(2,1)S(1)} %get-tuple-element.54.own_ref, bf16[40,4096]{1,0:T(8,128)(2,1)S(1)} %collective-permute-done.sib_ref, bf16[40,4096]{1,0:T(8,128)(2,1)S(1)} %collective-permute-done.1.near_ref, s32[1,128]{1,0:T(1,128)} %bitcast.32, ...), custom_call_target="tpu_custom_call" | custom-call | flops 1000000000 | bytes 16000000 | tf_op jit(solution)/shard_map/pallas_call | solution.py:320
  26.3 5.2 %collective-permute-start.7 = (f32[48,128]{1,0:T(8,128)S(1)}, f32[48,128]{1,0:T(8,128)S(1)}, u32[]{:S(2)}, u32[]{:S(2)}) collective-permute-start(f32[48,128]{1,0:T(8,128)S(1)} %shard_map.165.st_ref), channel_id=1, source_target_pairs={{1,2},{3,4},{5,6},{7,8},{9,10},{11,12},{13,14},{2,1},{4,3},{6,5},{... | collective-permute-start | bytes 73736 | tf_op jit(solution)/shard_map/ppermute | solution.py:315
  31.6 6.9 %collective-permute-done.7.st_near_ref = f32[48,128]{1,0:T(8,128)S(1)} collective-permute-done((f32[48,128]{1,0:T(8,128)S(1)}, f32[48,128]{1,0:T(8,128)S(1)}, u32[]{:S(2)}, u32[]{:S(2)}) %collective-permute-start.7) | collective-permute-done | bytes 24608 | tf_op jit(solution)/shard_map/ppermute | solution.py:315
  38.5 0.4 collective-permute-start.8
  38.9 0.2 collective-permute-start.9
  39.1 0.3 collective-permute-start.10
  39.4 0.2 collective-permute-start.11
  39.6 0.7 collective-permute-done.8
  40.3 0.6 collective-permute-done.9
  40.9 0.6 collective-permute-done.10
  41.4 0.6 collective-permute-done.11
  42.0 9.0 %shard_map.166 = (bf16[160,4096]{1,0:T(8,128)(2,1)S(1)}, bf16[160,4096]{1,0:T(8,128)(2,1)S(1)}, bf16[160,1024]{1,0:T(8,128)(2,1)S(1)}, bf16[160,1024]{1,0:T(8,12...) custom-call(bf16[1,2,24,4096]{3,2,1,0:T(8,128)(2,1)S(1)} %bitcast.16, ...), custom_call_target="tpu_custom_call" | custom-call | flops 4026531840 | bytes 16777216 | tf_op jit(solution)/shard_map/pallas_call | solution.py:443
  51.0 0.4 collective-permute-start.14
  51.3 2.0 %collective-permute-done.14.got_ref = bf16[4,24,4096]{2,1,0:T(8,128)(2,1)S(1)} collective-permute-done((bf16[4,24,4096]{2,1,0:T(8,128)(2,1)S(1)}, bf16[4,24,4096]{2,1,0:T(8,128)(2,1)S(1)}, u32[]{:S(2)}, u32[]{:S(2)}) %collective-permute-start.14) | collective-permute-done | bytes 786464 | tf_op jit(solution)/shard_map/ppermute | solution.py:401
  53.3 0.2 shard_map.167
  53.5 0.3 collective-permute-start.15
  53.8 0.7 collective-permute-start.16
  54.6 1.6 %collective-permute-start.17 = (bf16[24,4096]{1,0:T(8,128)(2,1)S(1)}, bf16[24,4096]{1,0:T(8,128)(2,1)S(1)}, u32[]{:S(2)}, u32[]{:S(2)}) collective-permute-start(bf16[24,4096]{1,0:T(8,128)(2,1)S(1)} %get-tuple-element.84), channel_id=1, source_target_pairs={{0,6},{1,7},{2,4},{3,5},{4,2},{5,3},{6,0},{7,1},{8,14},{9,15},{10,... | collective-permute-start | bytes 589832 | tf_op jit(solution)/shard_map/ppermute | solution.py:401
  56.2 3.5 %collective-permute-start.12 = (f32[48,128]{1,0:T(8,128)S(1)}, f32[48,128]{1,0:T(8,128)S(1)}, u32[]{:S(2)}, u32[]{:S(2)}) collective-permute-start(f32[48,128]{1,0:T(8,128)S(1)} %collective-permute-done.6.st_sib_ref), channel_id=1, source_target_pairs={{1,2},{3,4},{5,6},{7,8},{9,10},{11,12},{13,14},{2,1},{4,3},{6,5},{... | collective-permute-start | bytes 73736 | tf_op jit(solution)/shard_map/ppermute | solution.py:315
  59.8 2.1 %collective-permute-done.12.st_far_ref = f32[48,128]{1,0:T(8,128)S(1)} collective-permute-done((f32[48,128]{1,0:T(8,128)S(1)}, f32[48,128]{1,0:T(8,128)S(1)}, u32[]{:S(2)}, u32[]{:S(2)}) %collective-permute-start.12) | collective-permute-done | bytes 24608 | tf_op jit(solution)/shard_map/ppermute | solution.py:315
  61.9 9.9 %shard_map.168 = (f32[16,4096]{1,0:T(8,128)S(1)}, bf16[16,4096]{1,0:T(8,128)(2,1)S(1)}, bf16[16,4096]{1,0:T(8,128)(2,1)S(1)}, bf16[128,2,4096]{2,1,0:T(2,128)(2,1)}) custom-call(bf16[40,4096]{1,0:T(8,128)(2,1)S(1)} %get-tuple-element.54.own_ref, bf16[40,4096]{1,0:T(8,128)(2,1)S(1)} %collective-permute-done.sib_ref, ...), custom_call_target="tpu_custom_call" | custom-call | flops 1000000000 | bytes 32000000 | tf_op jit(solution)/shard_map/pallas_call | solution.py:331
  72.0 6.5 %collective-permute-start.19 = (bf16[16,4096]{1,0:T(8,128)(2,1)S(1)}, bf16[16,4096]{1,0:T(8,128)(2,1)S(1)}, u32[]{:S(2)}, u32[]{:S(2)}) collective-permute-start(bf16[16,4096]{1,0:T(8,128)(2,1)S(1)} %get-tuple-element.87), channel_id=1, source_target_pairs={{1,2},{3,4},{5,6},{7,8},{9,10},{11,12},{13,14},{2,1},{4,3},{6,5},{... | collective-permute-start | bytes 393224 | tf_op jit(solution)/shard_map/ppermute | solution.py:315
  78.6 6.9 %shard_map.171 = (bf16[4096,1024]{1,0:T(8,128)(2,1)}, bf16[1024,4096]{1,0:T(8,128)(2,1)}) custom-call(bf16[160,4096]{1,0:T(8,128)(2,1)S(1)} %get-tuple-element.96.x_ref, bf16[160,1024]{1,0:T(8,128)(2,1)S(1)} %get-tuple-element.97.hidden_ref, bf16[160,1024]{1,0:T(8,128)(2,1)S(1)} %get-tuple-element.98.scaled_ref, bf16[160,4096]{1,0:T(8,128)(2,1)S(1)} %get-tuple-element.99.g_ref), custom_call_target="tpu_custom_call" | custom-call | flops 2684354560 | bytes 16777216 | tf_op jit(solution)/shard_map/pallas_call | solution.py:484
  85.6 1.1 %shard_map.170 = (bf16[16,4096]{1,0:T(8,128)(2,1)}, f32[1,16]{1,0:T(1,128)}) custom-call(s32[1,16]{1,0:T(1,128)S(1)} %bitcast.26, s32[1,16]{1,0:T(1,128)S(1)} %bitcast.28, f32[24,4096]{1,0:T(8,128)S(1)} %get-tuple-element.85.own_ref, bf16[16,4096]{1,0:T(8,128)(2,1)S(1)} %collective-permute-done.20.got_ref), custom_call_target="tpu_custom_call" | custom-call | tf_op jit(solution)/shard_map/pallas_call | solution.py:505
  86.6 0.7 add_convert_fusion
  (25 shorter events, 0.5 us)
Async XLA Ops:
  2.3 14.7 %collective-permute-start.2 = (bf16[24,4096]{1,0:T(8,128)(2,1)S(1)}, bf16[24,4096]{1,0:T(8,128)(2,1)S(1)}, u32[]{:S(2)}, u32[]{:S(2)}) collective-permute-start(bf16[24,4096]{1,0:T(8,128)(2,1)S(1)} %get-tuple-element.57), channel_id=1, source_target_pairs={{0,12},{1,13},{2,14},{3,15},{4,8},{5,9},{6,10},{7,11},{8,4},{9,5},... | collective-permute-start | bytes 589832 | tf_op jit(solution)/shard_map/ppermute | solution.py:401
  6.5 11.5 %collective-permute-start.1 = (bf16[40,4096]{1,0:T(8,128)(2,1)S(1)}, bf16[40,4096]{1,0:T(8,128)(2,1)S(1)}, u32[]{:S(2)}, u32[]{:S(2)}) collective-permute-start(bf16[40,4096]{1,0:T(8,128)(2,1)S(1)} %get-tuple-element.54.own_ref), channel_id=1, source_target_pairs={{1,2},{3,4},{5,6},{7,8},{9,10},{11,12},{13,14},{2,1},{4,3},{6,5},{... | collective-permute-start | bytes 983048 | tf_op jit(solution)/shard_map/ppermute | solution.py:315
  10.5 7.5 %collective-permute-start = (bf16[40,4096]{1,0:T(8,128)(2,1)S(1)}, bf16[40,4096]{1,0:T(8,128)(2,1)S(1)}, u32[]{:S(2)}, u32[]{:S(2)}) collective-permute-start(bf16[40,4096]{1,0:T(8,128)(2,1)S(1)} %get-tuple-element.54.own_ref), channel_id=1, source_target_pairs={{0,1},{1,0},{2,3},{3,2},{4,5},{5,4},{6,7},{7,6},{8,9},{9,8},{10,11... | collective-permute-start | bytes 983048 | tf_op jit(solution)/shard_map/ppermute | solution.py:310
  18.0 20.5 %collective-permute-start.5 = (bf16[2,24,4096]{2,1,0:T(8,128)(2,1)S(1)}, bf16[2,24,4096]{2,1,0:T(8,128)(2,1)S(1)}, u32[]{:S(2)}, u32[]{:S(2)}) collective-permute-start(bf16[2,24,4096]{2,1,0:T(8,128)(2,1)S(1)} %pad_maximum_fusion), channel_id=1, source_target_pairs={{0,6},{1,7},{2,4},{3,5},{4,2},{5,3},{6,0},{7,1},{8,14},{9,15},{10,... | collective-permute-start | bytes 1179656 | tf_op jit(solution)/shard_map/ppermute | solution.py:401
  19.7 18.7 %collective-permute-start.4 = (bf16[2,24,4096]{2,1,0:T(8,128)(2,1)S(1)}, bf16[2,24,4096]{2,1,0:T(8,128)(2,1)S(1)}, u32[]{:S(2)}, u32[]{:S(2)}) collective-permute-start(bf16[2,24,4096]{2,1,0:T(8,128)(2,1)S(1)} %pad_maximum_fusion), channel_id=1, source_target_pairs={{0,4},{1,5},{2,6},{3,7},{4,0},{5,1},{6,2},{7,3},{8,12},{9,13},{10,... | collective-permute-start | bytes 1179656 | tf_op jit(solution)/shard_map/ppermute | solution.py:401
  19.8 18.8 %collective-permute-start.3 = (bf16[2,24,4096]{2,1,0:T(8,128)(2,1)S(1)}, bf16[2,24,4096]{2,1,0:T(8,128)(2,1)S(1)}, u32[]{:S(2)}, u32[]{:S(2)}) collective-permute-start(bf16[2,24,4096]{2,1,0:T(8,128)(2,1)S(1)} %pad_maximum_fusion), channel_id=1, source_target_pairs={{0,2},{1,3},{2,0},{3,1},{4,6},{5,7},{6,4},{7,5},{8,10},{9,11},{10,... | collective-permute-start | bytes 1179656 | tf_op jit(solution)/shard_map/ppermute | solution.py:401
  26.3 12.2 %collective-permute-start.7 = (f32[48,128]{1,0:T(8,128)S(1)}, f32[48,128]{1,0:T(8,128)S(1)}, u32[]{:S(2)}, u32[]{:S(2)}) collective-permute-start(f32[48,128]{1,0:T(8,128)S(1)} %shard_map.165.st_ref), channel_id=1, source_target_pairs={{1,2},{3,4},{5,6},{7,8},{9,10},{11,12},{13,14},{2,1},{4,3},{6,5},{... | collective-permute-start | bytes 73736 | tf_op jit(solution)/shard_map/ppermute | solution.py:315
  31.6 6.9 %collective-permute-start.6 = (f32[48,128]{1,0:T(8,128)S(1)}, f32[48,128]{1,0:T(8,128)S(1)}, u32[]{:S(2)}, u32[]{:S(2)}) collective-permute-start(f32[48,128]{1,0:T(8,128)S(1)} %shard_map.165.st_ref), channel_id=1, source_target_pairs={{0,1},{1,0},{2,3},{3,2},{4,5},{5,4},{6,7},{7,6},{8,9},{9,8},{10,11... | collective-permute-start | bytes 73736 | tf_op jit(solution)/shard_map/ppermute | solution.py:310
  38.5 1.8 %collective-permute-start.8 = (bf16[2,24,4096]{2,1,0:T(8,128)(2,1)S(1)}, bf16[2,24,4096]{2,1,0:T(8,128)(2,1)S(1)}, u32[]{:S(2)}, u32[]{:S(2)}) collective-permute-start(bf16[2,24,4096]{2,1,0:T(8,128)(2,1)S(1)} %pad_maximum_fusion), channel_id=1, source_target_pairs={{0,1},{1,0},{2,3},{3,2},{4,5},{5,4},{6,7},{7,6},{8,9},{9,8},{10,11... | collective-permute-start | bytes 1179656 | tf_op jit(solution)/shard_map/ppermute | solution.py:401
  38.9 2.0 %collective-permute-start.9 = (bf16[2,24,4096]{2,1,0:T(8,128)(2,1)S(1)}, bf16[2,24,4096]{2,1,0:T(8,128)(2,1)S(1)}, u32[]{:S(2)}, u32[]{:S(2)}) collective-permute-start(bf16[2,24,4096]{2,1,0:T(8,128)(2,1)S(1)} %collective-permute-done.3), channel_id=1, source_target_pairs={{0,1},{1,0},{2,3},{3,2},{4,5},{5,4},{6,7},{7,6},{8,9},{9,8},{10,11... | collective-permute-start | bytes 1179656 | tf_op jit(solution)/shard_map/ppermute | solution.py:401
  39.1 2.3 %collective-permute-start.10 = (bf16[2,24,4096]{2,1,0:T(8,128)(2,1)S(1)}, bf16[2,24,4096]{2,1,0:T(8,128)(2,1)S(1)}, u32[]{:S(2)}, u32[]{:S(2)}) collective-permute-start(bf16[2,24,4096]{2,1,0:T(8,128)(2,1)S(1)} %collective-permute-done.4), channel_id=1, source_target_pairs={{0,1},{1,0},{2,3},{3,2},{4,5},{5,4},{6,7},{7,6},{8,9},{9,8},{10,11... | collective-permute-start | bytes 1179656 | tf_op jit(solution)/shard_map/ppermute | solution.py:401
  39.4 2.6 %collective-permute-start.11 = (bf16[2,24,4096]{2,1,0:T(8,128)(2,1)S(1)}, bf16[2,24,4096]{2,1,0:T(8,128)(2,1)S(1)}, u32[]{:S(2)}, u32[]{:S(2)}) collective-permute-start(bf16[2,24,4096]{2,1,0:T(8,128)(2,1)S(1)} %collective-permute-done.5), channel_id=1, source_target_pairs={{0,1},{1,0},{2,3},{3,2},{4,5},{5,4},{6,7},{7,6},{8,9},{9,8},{10,11... | collective-permute-start | bytes 1179656 | tf_op jit(solution)/shard_map/ppermute | solution.py:401
  50.9 34.6 %copy-start = (s32[16]{0:T(128)S(1)}, s32[16]{0:T(128)}, u32[]{:S(2)}) copy-start(s32[16]{0:T(128)} %param.20) | copy-start | bytes 196
  51.0 34.6 %copy-start.1 = (s32[16]{0:T(128)S(1)}, s32[16]{0:T(128)}, u32[]{:S(2)}) copy-start(s32[16]{0:T(128)} %param.21) | copy-start | bytes 196
  51.0 2.4 %collective-permute-start.14 = (bf16[4,24,4096]{2,1,0:T(8,128)(2,1)S(1)}, bf16[4,24,4096]{2,1,0:T(8,128)(2,1)S(1)}, u32[]{:S(2)}, u32[]{:S(2)}) collective-permute-start(bf16[4,24,4096]{2,1,0:T(8,128)(2,1)S(1)} %get-tuple-element.71), channel_id=1, source_target_pairs={{0,1},{1,0},{2,3},{3,2},{4,5},{5,4},{6,7},{7,6},{8,9},{9,8},{10,11... | collective-permute-start | bytes 2359304 | tf_op jit(solution)/shard_map/ppermute | solution.py:401
  53.5 18.3 %collective-permute-start.15 = (bf16[24,4096]{1,0:T(8,128)(2,1)S(1)}, bf16[24,4096]{1,0:T(8,128)(2,1)S(1)}, u32[]{:S(2)}, u32[]{:S(2)}) collective-permute-start(bf16[24,4096]{1,0:T(8,128)(2,1)S(1)} %get-tuple-element.82), channel_id=1, source_target_pairs={{0,2},{1,3},{2,0},{3,1},{4,6},{5,7},{6,4},{7,5},{8,10},{9,11},{10,... | collective-permute-start | bytes 589832 | tf_op jit(solution)/shard_map/ppermute | solution.py:401
  53.8 17.9 %collective-permute-start.16 = (bf16[24,4096]{1,0:T(8,128)(2,1)S(1)}, bf16[24,4096]{1,0:T(8,128)(2,1)S(1)}, u32[]{:S(2)}, u32[]{:S(2)}) collective-permute-start(bf16[24,4096]{1,0:T(8,128)(2,1)S(1)} %get-tuple-element.83), channel_id=1, source_target_pairs={{0,4},{1,5},{2,6},{3,7},{4,0},{5,1},{6,2},{7,3},{8,12},{9,13},{10,... | collective-permute-start | bytes 589832 | tf_op jit(solution)/shard_map/ppermute | solution.py:401
  54.6 17.2 %collective-permute-start.17 = (bf16[24,4096]{1,0:T(8,128)(2,1)S(1)}, bf16[24,4096]{1,0:T(8,128)(2,1)S(1)}, u32[]{:S(2)}, u32[]{:S(2)}) collective-permute-start(bf16[24,4096]{1,0:T(8,128)(2,1)S(1)} %get-tuple-element.84), channel_id=1, source_target_pairs={{0,6},{1,7},{2,4},{3,5},{4,2},{5,3},{6,0},{7,1},{8,14},{9,15},{10,... | collective-permute-start | bytes 589832 | tf_op jit(solution)/shard_map/ppermute | solution.py:401
  56.2 5.7 %collective-permute-start.12 = (f32[48,128]{1,0:T(8,128)S(1)}, f32[48,128]{1,0:T(8,128)S(1)}, u32[]{:S(2)}, u32[]{:S(2)}) collective-permute-start(f32[48,128]{1,0:T(8,128)S(1)} %collective-permute-done.6.st_sib_ref), channel_id=1, source_target_pairs={{1,2},{3,4},{5,6},{7,8},{9,10},{11,12},{13,14},{2,1},{4,3},{6,5},{... | collective-permute-start | bytes 73736 | tf_op jit(solution)/shard_map/ppermute | solution.py:315
  59.7 2.2 %collective-permute-start.13 = (f32[48,128]{1,0:T(8,128)S(1)}, f32[48,128]{1,0:T(8,128)S(1)}, u32[]{:S(2)}, u32[]{:S(2)}) collective-permute-start(f32[48,128]{1,0:T(8,128)S(1)} %collective-permute-done.7.st_near_ref), channel_id=1, source_target_pairs={{0,1},{1,0},{2,3},{3,2},{4,5},{5,4},{6,7},{7,6},{8,9},{9,8},{10,11... | collective-permute-start | bytes 73736 | tf_op jit(solution)/shard_map/ppermute | solution.py:310
  71.9 14.7 %collective-permute-start.18 = (bf16[16,4096]{1,0:T(8,128)(2,1)S(1)}, bf16[16,4096]{1,0:T(8,128)(2,1)S(1)}, u32[]{:S(2)}, u32[]{:S(2)}) collective-permute-start(bf16[16,4096]{1,0:T(8,128)(2,1)S(1)} %get-tuple-element.86), channel_id=1, source_target_pairs={{0,1},{1,0},{2,3},{3,2},{4,5},{5,4},{6,7},{7,6},{8,9},{9,8},{10,11... | collective-permute-start | bytes 393224 | tf_op jit(solution)/shard_map/ppermute | solution.py:310
  72.0 14.6 %collective-permute-start.19 = (bf16[16,4096]{1,0:T(8,128)(2,1)S(1)}, bf16[16,4096]{1,0:T(8,128)(2,1)S(1)}, u32[]{:S(2)}, u32[]{:S(2)}) collective-permute-start(bf16[16,4096]{1,0:T(8,128)(2,1)S(1)} %get-tuple-element.87), channel_id=1, source_target_pairs={{1,2},{3,4},{5,6},{7,8},{9,10},{11,12},{13,14},{2,1},{4,3},{6,5},{... | collective-permute-start | bytes 393224 | tf_op jit(solution)/shard_map/ppermute | solution.py:315
  78.5 7.0 %collective-permute-start.20 = (bf16[16,4096]{1,0:T(8,128)(2,1)S(1)}, bf16[16,4096]{1,0:T(8,128)(2,1)S(1)}, u32[]{:S(2)}, u32[]{:S(2)}) collective-permute-start(bf16[16,4096]{1,0:T(8,128)(2,1)S(1)} %get-tuple-element.89), channel_id=1, source_target_pairs={{0,12},{1,13},{2,14},{3,15},{4,8},{5,9},{6,10},{7,11},{8,4},{9,5},... | collective-permute-start | bytes 393224 | tf_op jit(solution)/shard_map/ppermute | solution.py:401

commit v3 on v2

--- a/solution.py
+++ b/solution.py
@@ -15,11 +15,11 @@
 SCALE = 0.125
 NONE = -1e30
 LANES = 128
-BLOCK = 24
-GATE_ROW = 20
-PIECE = 512
-MAIN_LIMIT = 14 * 2**20
-SMALL_LIMIT = 56 * 2**20
+FOLD = D // 4
+WIDE = D + FOLD + LANES
+TAILS = slice(D, D + FOLD)
+SIDE = slice(D + FOLD, WIDE)
+MAIN_LIMIT = 24 * 2**20
 
 
 def iota(shape, dim):
@@ -55,89 +55,83 @@
     gate = gate_ref[...].astype(jnp.float32)
     moe_input, moe_grad = input_ref[...], grad_ref[...]
     expert = mine()
-    row = iota((BLOCK, tokens), 0)
+    row = iota((24, tokens), 0)
     input_slot = jnp.where(row < 8, row, jnp.where((row == 16) | (row == 17), row - 8, -2))
     grad_slot = jnp.where(
         (row >= 8) & (row < 16), row - 8, jnp.where((row == 18) | (row == 19), row - 10, -2)
     )
-    diagonal = iota((tokens, tokens), 0) == iota((tokens, tokens), 1)
-    gate_column = jnp.sum(jnp.where(diagonal, gate, 0.0), axis=1, keepdims=True)
+    gate_slot = jnp.where(row < CAP, row, -2)
     for which, out_ref in ((expert, own_ref), (1 - expert, other_ref)):
         slot = slots_of(ids, keep, which)
         block = mm(one_hot(input_slot == slot), moe_input) + mm(one_hot(grad_slot == slot), moe_grad)
-        slot_column = jnp.sum(jnp.where(diagonal, slot, 0), axis=1, keepdims=True)
-        gates = jnp.sum(
-            jnp.where(slot_column == iota((tokens, LANES), 1), gate_column, 0.0), axis=0, keepdims=True
-        )
-        out_ref[...] = block.astype(jnp.bfloat16)
-        out_ref[:, :LANES] = (
-            block[:, :LANES] + jnp.where(iota((BLOCK, LANES), 0) == GATE_ROW, gates, 0.0)
-        ).astype(jnp.bfloat16)
-
-
-def slot_rows(count):
-    rows = iota((count * CAP, 1), 0)
-    tail = rows - 8 * count
-    source = jnp.where(rows < 8 * count, rows // 8, tail // 2)
-    return source, jnp.where(rows < 8 * count, rows % 8, 8 + tail % 2)
+        block = block.astype(jnp.bfloat16)
+        out_ref[:, :D] = block[:16]
+        for b in range(4):
+            out_ref[4 * b : 4 * b + 4, TAILS] = block[16:20, b * FOLD : (b + 1) * FOLD]
+        gates = jnp.sum(jnp.where(gate_slot == slot, gate, 0.0), axis=1, keepdims=True)
+        out_ref[:, SIDE] = jnp.broadcast_to(gates[:16], (16, LANES)).astype(jnp.bfloat16)
 
 
 def main_kernel(places, *refs):
     blocks, refs = refs[: len(places)], refs[len(places) :]
-    w_in_ref, w_out_ref, x_out, g_out, hidden_ref, scaled_ref, keep_ref, send_ref = refs[:8]
-    (tails,) = refs[8:]
-    count = sum(r.shape[0] for r in blocks) * 2
-    rows = count * CAP
-    units = count // 2
+    w_in_ref, w_out_far, x_out, g_out, hidden_ref, scaled_ref, keep_ref, send_ref = refs[:8]
+    tails, gate_ref, pre_ref, w_out_ref, arrived = refs[8:]
+    fetched = pltpu.make_async_copy(w_out_far, w_out_ref, arrived)
+    fetched.start()
+    units = sum(r.shape[0] for r in blocks)
+    heads, rows = 16 * units, 20 * units
     width = w_in_ref.shape[1]
     chunk = min(width, 256)
-    source, slot = slot_rows(count)
     for block, place in zip(blocks, places):
         for i in range(block.shape[0]):
             at = place + i
-            first, second = block[i, 0], block[i, 1]
-            x_out[pl.ds(16 * at, 16), :] = jnp.concatenate([first[:8], second[:8]], axis=0)
-            g_out[pl.ds(16 * at, 16), :] = jnp.concatenate([first[8:16], second[8:16]], axis=0)
-            tails[pl.ds(16 * at, 16), :] = jnp.concatenate([first[16:], second[16:]], axis=0)
-    row, col = iota((2 * count, 8 * count), 0), iota((2 * count, 8 * count), 1)
-    pick = 8 * (row // 2) + row % 2
+            pair = block[i]
+            both = jnp.concatenate([pair[:8], pair[16:24]], axis=0)
+            x_out[pl.ds(16 * at, 16), :] = both[:, :D]
+            gate_ref[pl.ds(16 * at, 16), :] = both[:, SIDE].astype(jnp.float32)
+            g_out[pl.ds(16 * at, 16), :] = jnp.concatenate([pair[8:16, :D], pair[24:32, :D]], axis=0)
+            gate_ref[pl.ds(heads + 4 * at, 4), :] = jnp.concatenate(
+                [pair[8:10, SIDE], pair[24:26, SIDE]], axis=0
+            ).astype(jnp.float32)
+            for b in range(4):
+                tails[pl.ds(8 * at, 8), pl.ds(b * FOLD, FOLD)] = jnp.concatenate(
+                    [pair[4 * b : 4 * b + 4, TAILS], pair[16 + 4 * b : 20 + 4 * b, TAILS]], axis=0
+                )
+    row, col = iota((4 * units, 8 * units), 0), iota((4 * units, 8 * units), 1)
+    pick = 4 * (row // 2) + row % 2
     tail = tails[...]
-    x_out[pl.ds(8 * count, 2 * count), :] = mm(one_hot(col == pick), tail).astype(jnp.bfloat16)
-    g_out[pl.ds(8 * count, 2 * count), :] = mm(one_hot(col == pick + 2), tail).astype(jnp.bfloat16)
-    of_row = one_hot(iota((rows, 8 * count), 1) == 8 * source + GATE_ROW - 16)
-    gates = mm(of_row, tails[:, :LANES])
-    gate = jnp.sum(jnp.where(iota((rows, LANES), 1) == slot, gates, 0.0), axis=1, keepdims=True)
-
+    x_out[pl.ds(heads, 4 * units), :] = mm(one_hot(col == pick), tail).astype(jnp.bfloat16)
+    g_out[pl.ds(heads, 4 * units), :] = mm(one_hot(col == pick + 2), tail).astype(jnp.bfloat16)
+    gate = gate_ref[:, :1]
+
+    for start in range(0, width, chunk):
+        at = pl.ds(start, chunk)
+        pre_ref[:, at] = mm(x_out[...], w_in_ref[:, at])
+    fetched.wait()
     gate_part = jnp.zeros((rows, 1), jnp.float32)
-    for i in range(width // chunk):
-        at = pl.ds(i * chunk, chunk)
-        pre = mm(x_out[...], w_in_ref[:, at])
+    for start in range(0, width, chunk):
+        at = pl.ds(start, chunk)
+        pre = pre_ref[:, at]
         back = mm(g_out[...], w_out_ref[at, :], ((1,), (1,)))
         active = jnp.maximum(pre, 0.0)
         hidden_ref[:, at] = (gate * back * jnp.where(pre > 0, 1.0, 0.0)).astype(jnp.bfloat16)
         scaled_ref[:, at] = (gate * active).astype(jnp.bfloat16)
         gate_part += jnp.sum(active * back, axis=1, keepdims=True)
 
-    lane = iota((rows, LANES), 1)
-    placed = jnp.where(lane == 16 * (source % 2) + slot, gate_part, 0.0).astype(jnp.bfloat16)
-    at = iota((8 * units, rows), 1)
-    unit = jnp.where(at < 8 * count, at // 16, (at - 8 * count) // 4)
-    row = iota((8 * units, rows), 0)
-    gates = mm(one_hot((row % 8 == GATE_ROW - 16) & (unit == row // 8)), placed)
-    row, col = iota((8 * units, 2 * count), 0), iota((8 * units, 2 * count), 1)
-    to_end = one_hot((row % 8 < 4) & (col == 4 * (row // 8) + row % 8))
+    halves = [(keep_ref, u) for u in range(keep_ref.shape[0])] + [(send_ref, u) for u in range(send_ref.shape[0])]
     hidden = hidden_ref[...]
-    for start in range(0, D, PIECE):
-        lanes = pl.ds(start, PIECE)
+    for b in range(4):
+        lanes = pl.ds(b * FOLD, FOLD)
         part = mm(hidden, w_in_ref[lanes, :], ((1,), (1,))).astype(jnp.bfloat16)
-        ends = mm(to_end, part[8 * count :])
-        if start == 0:
-            ends = jnp.concatenate([ends[:, :LANES] + gates, ends[:, LANES:]], axis=1)
-        ends = ends.astype(jnp.bfloat16)
-        for u in range(units):
-            half, index = (keep_ref, u) if u < keep_ref.shape[0] else (send_ref, u - keep_ref.shape[0])
-            half[index, :16, lanes] = part[16 * u : 16 * u + 16]
-            half[index, 16:, lanes] = ends[8 * u : 8 * u + 8]
+        for u, (half, index) in enumerate(halves):
+            half[index, :, lanes] = part[16 * u : 16 * u + 16]
+            half[index, 4 * b : 4 * b + 4, TAILS] = part[heads + 4 * u : heads + 4 * u + 4]
+    lane = iota((16, LANES), 1)
+    for u, (half, index) in enumerate(halves):
+        ends = gate_part[heads + 4 * u : heads + 4 * u + 4]
+        ends = jnp.concatenate([ends, jnp.zeros((12, 1), jnp.float32)], axis=0)
+        side = jnp.where(lane == 0, gate_part[16 * u : 16 * u + 16], jnp.where(lane == 1, ends, 0.0))
+        half[index, :, SIDE] = side.astype(jnp.bfloat16)
 
 
 def weights_kernel(x_ref, hidden_ref, scaled_ref, g_ref, w_in_ref, w_out_ref):
@@ -159,7 +153,13 @@
     for part in parts[1:]:
         unit = unit + part[...].astype(jnp.float32)
     own_ref[...] = unit
-    send_ref[...] = unit[8:].astype(jnp.bfloat16)
+    low = unit.astype(jnp.bfloat16)
+    send_ref[:, :D] = low[8:, :D]
+    for b in range(4):
+        send_ref[2 * b : 2 * b + 2, TAILS] = low[4 * b + 2 : 4 * b + 4, TAILS]
+    lane = iota((8, LANES), 1)
+    ends = jnp.concatenate([unit[2:4, SIDE], jnp.zeros((6, LANES), jnp.float32)], axis=0)
+    send_ref[:, SIDE] = jnp.where(lane == 0, unit[8:, SIDE], ends).astype(jnp.bfloat16)
 
 
 def scatter_kernel(mine, ids_ref, keep_ref, own_ref, got_ref, grad_ref, gate_ref):
@@ -168,24 +168,17 @@
     expert = mine()
     diagonal = iota((tokens, tokens), 0) == iota((tokens, tokens), 1)
     own, got = own_ref[...], got_ref[...].astype(jnp.float32)
-    grad = jnp.zeros((tokens, own.shape[1]), jnp.float32)
+    grad = jnp.zeros((tokens, D), jnp.float32)
     gate = jnp.zeros((1, tokens), jnp.float32)
-    for which, part, first, tail, lane in (
-        (expert, own, 0, 16, 0),
-        (1 - expert, got, 0, 10, 16),
-    ):
+    for which, part, step in ((expert, own, 4), (1 - expert, got, 2)):
         slot = slots_of(ids, keep, which)
         column = jnp.sum(jnp.where(diagonal, slot, 0), axis=1, keepdims=True)
-        row = iota((tokens, part.shape[0]), 1)
-        place = jnp.where(column < 8, first + column, tail + column - 8)
-        grad = grad + mm(one_hot((row == place) & (column >= 0)), part.astype(jnp.bfloat16))
-        gates = part[GATE_ROW - BLOCK + part.shape[0] :][:1, :LANES]
-        wide = jnp.where(iota((LANES, tokens), 0) == slot + lane, 1.0, 0.0)
-        wide = jnp.where(slot >= 0, wide, 0.0)
-        column_gates = jnp.sum(
-            jnp.where(iota((LANES, LANES), 0) == iota((LANES, LANES), 1), gates, 0.0), axis=1, keepdims=True
-        )
-        gate = gate + jnp.sum(wide * column_gates, axis=0, keepdims=True)
+        ends = jnp.concatenate([part[step * b : step * b + 2, TAILS] for b in range(4)], axis=1)
+        full = jnp.concatenate([part[:8, :D], ends, jnp.zeros((6, D), jnp.float32)], axis=0)
+        grad = grad + mm(one_hot(iota((tokens, 16), 1) == column), full.astype(jnp.bfloat16))
+        side = part[:, SIDE]
+        gates = jnp.concatenate([side[:8, :1], side[:2, 1:2], jnp.zeros((6, 1), jnp.float32)], axis=0)
+        gate = gate + jnp.sum(jnp.where(iota((16, tokens), 0) == slot, gates, 0.0), axis=0, keepdims=True)
     grad_ref[...] = grad.astype(jnp.bfloat16)
     gate_ref[...] = gate
 
@@ -196,28 +189,26 @@
 
 def pack_tokens(query_ref, grad_ref, segments_ref, out_ref):
     tokens = query_ref.shape[0]
-    out_ref[:tokens, :] = query_ref[...]
-    out_ref[tokens : 2 * tokens, :] = grad_ref[...]
-    out_ref[2 * tokens :, :] = jnp.zeros((8, out_ref.shape[1]), jnp.bfloat16)
+    out_ref[:tokens, :D] = query_ref[...]
+    out_ref[tokens:, :D] = grad_ref[...]
     segments = segments_ref[...] + 1
     diagonal = iota((tokens, tokens), 0) == iota((tokens, tokens), 1)
     column = jnp.sum(jnp.where(diagonal, segments, 0), axis=1, keepdims=True)
     lane = iota((tokens, LANES), 1)
-    row = iota((tokens, LANES), 0)
     digits = jnp.zeros((tokens, LANES), jnp.int32)
     for i in range(3):
-        digits = digits + jnp.where(lane == row + i * tokens, (column >> (7 * i)) & 127, 0)
-    line = jnp.sum(digits, axis=0, keepdims=True).astype(jnp.float32)
-    out_ref[2 * tokens :, :LANES] = jnp.where(iota((8, LANES), 0) == 0, line, 0.0).astype(jnp.bfloat16)
+        digits = digits + jnp.where(lane == i, (column >> (7 * i)) & 127, 0)
+    out_ref[:tokens, D:] = digits.astype(jnp.float32).astype(jnp.bfloat16)
+    out_ref[tokens:, D:] = jnp.zeros((tokens, LANES), jnp.bfloat16)
 
 
 def segment_column(token_ref, tokens):
-    line = token_ref[2 * tokens :, :LANES][:1].astype(jnp.float32)
-    lane, row = iota((tokens, LANES), 1), iota((tokens, LANES), 0)
+    digits = token_ref[:tokens, D:].astype(jnp.float32)
+    lane = iota((tokens, LANES), 1)
     weight = jnp.zeros((tokens, LANES), jnp.float32)
     for i in range(3):
-        weight = weight + jnp.where(lane == row + i * tokens, float(128**i), 0.0)
-    return jnp.sum(weight * line, axis=1, keepdims=True).astype(jnp.int32)
+        weight = weight + jnp.where(lane == i, float(128**i), 0.0)
+    return jnp.sum(weight * digits, axis=1, keepdims=True).astype(jnp.int32)
 
 
 def head_scores(token_refs, kv, head, tokens):
@@ -247,7 +238,7 @@
 
 def stats_kernel(own_ref, sib_ref, near_ref, rows_ref, kv_ref, stats_ref):
     token_refs = (own_ref, sib_ref, near_ref)
-    tokens = (own_ref.shape[0] - 8) // 2
+    tokens = own_ref.shape[0] // 2
     allowed = allowed_pairs(token_refs, rows_ref, tokens)
     lane = iota((3 * tokens, LANES), 1)
     stats = jnp.zeros((3 * tokens, LANES), jnp.float32)
@@ -275,17 +266,18 @@
 
 
 def grads_kernel(
-    own_ref, sib_ref, near_ref, rows_ref, kv_ref, st_ref, st_sib_ref, st_near_ref, st_far_ref, st_side_ref,
+    own_ref, sib_ref, near_ref, rows_ref, kv_ref, st_ref, st_sib_ref, met_ref, sib_met_ref,
     query_ref, to_sib_ref, to_near_ref, kv_grad_ref,
 ):
     token_refs = (own_ref, sib_ref, near_ref)
-    tokens = (own_ref.shape[0] - 8) // 2
+    tokens = own_ref.shape[0] // 2
     allowed = allowed_pairs(token_refs, rows_ref, tokens)
     a, b, c = slice(0, tokens), slice(tokens, 2 * tokens), slice(2 * tokens, 3 * tokens)
+    far_b = slice(4 * tokens, 5 * tokens)
     totals = [
-        merged((st_ref[a], st_sib_ref[b], st_near_ref[c])),
-        merged((st_ref[b], st_sib_ref[a], st_side_ref[c])),
-        merged((st_ref[c], st_near_ref[a], st_far_ref[b])),
+        merged((st_ref[a], st_sib_ref[b], met_ref[c])),
+        merged((st_ref[b], st_sib_ref[a], sib_met_ref[c])),
+        merged((st_ref[c], met_ref[a], met_ref[far_b])),
     ]
     peak, scale, delta = (jnp.concatenate([t[i] for t in totals], axis=0) for i in range(3))
     for head in range(HEADS):
@@ -316,7 +308,7 @@
 
 
 def attention_stats(held):
-    tokens = (held[0].shape[0] - 8) // 2
+    tokens = held[0].shape[0] // 2
     return pl.pallas_call(
         stats_kernel,
         out_shape=jax.ShapeDtypeStruct((3 * tokens, LANES), jnp.float32),
@@ -326,7 +318,7 @@
 
 
 def attention_grads(held, stats):
-    tokens = (held[0].shape[0] - 8) // 2
+    tokens = held[0].shape[0] // 2
     low = jax.ShapeDtypeStruct((tokens, D), jnp.bfloat16)
     return pl.pallas_call(
         grads_kernel,
@@ -401,10 +393,11 @@
         return lax.ppermute(block, "seq", [(i, i ^ bits) for i in range(devices)])
 
     ids, keep = expert_ids.reshape(1, tokens), keep_mask.reshape(1, tokens)
-    block_type = jax.ShapeDtypeStruct((BLOCK, D), jnp.bfloat16)
+    block_type = jax.ShapeDtypeStruct((16, WIDE), jnp.bfloat16)
+    sent_type = jax.ShapeDtypeStruct((16, WIDE), jnp.bfloat16)
     own, other, packed = pl.pallas_call(
         functools.partial(pack_kernel, mine),
-        out_shape=(block_type, block_type, jax.ShapeDtypeStruct((2 * tokens + 8, D), jnp.bfloat16)),
+        out_shape=(sent_type, sent_type, jax.ShapeDtypeStruct((2 * tokens, D + LANES), jnp.bfloat16)),
         compiler_params=params(8 * 2**20),
     )(
         *map(far, (ids, keep, gate_prob.reshape(1, tokens), moe_input, moe_grad)),
@@ -412,21 +405,22 @@
     )
     across = (devices - 1) & ~3
     got = flip(other, across)
-    near_w_input, near_w_output, near_kv = w_input, w_output, enc_kv
+    near_w_input, near_kv = w_input, enc_kv
     if square:
-        near_w_input, near_w_output, near_kv = fetch(w_input, w_output, enc_kv)
+        near_w_input, near_kv = fetch(w_input, enc_kv)
     held = (packed, core(packed), cross(packed), far(enc_segments.reshape(1, -1)), near_kv)
     stats = attention_stats(held)
-    stats_sib, stats_near = core(stats), cross(stats)
-
-    pair = jnp.stack([own, got])
+    stats_sib = core(stats)
+    met = cross(jnp.concatenate([stats, stats_sib]))
+    all_stats = (stats, stats_sib, met, core(met))
+
+    pair = jnp.concatenate([own, got])
     if square:
-        pair = after(pair, held[1], held[2], near_w_input)
+        pair = after(pair, held[1], held[2], near_kv)
         near = [pair, flip(pair, 2), flip(pair, 4), flip(pair, 6)]
-        *near, stats, stats_sib, stats_near = lax.optimization_barrier(
-            (*near, stats, stats_sib, stats_near)
-        )
-        blocks = [b[None] for b in near + [flip(b, 1) for b in near]]
+        beside = flip(pair, 1)
+        *near, all_stats = lax.optimization_barrier((*near, all_stats))
+        blocks = [b[None] for b in near + [beside] + [flip(b, 1) for b in near[1:]]]
     else:
         halves = [list(range(e * shards, (e + 1) * shards)) for e in range(EXPERTS)]
         blocks = [lax.all_gather(pair[None], "seq", axis_index_groups=halves, tiled=True)]
@@ -439,36 +433,39 @@
     keep_units = shards // 2
     slots = jax.ShapeDtypeStruct((rows, D), jnp.bfloat16)
     hidden_type = jax.ShapeDtypeStruct((rows, width), jnp.bfloat16)
-    units_type = jax.ShapeDtypeStruct((keep_units, BLOCK, D), jnp.bfloat16)
+    units_type = jax.ShapeDtypeStruct((keep_units, 16, WIDE), jnp.bfloat16)
     x, g, hidden, scaled, keep_half, send_half = pl.pallas_call(
         functools.partial(main_kernel, places),
         out_shape=[slots, slots, hidden_type, hidden_type, units_type, units_type],
         in_specs=[pl.BlockSpec(memory_space=pltpu.VMEM)] * len(places)
-        + [pl.BlockSpec(memory_space=pltpu.VMEM)] * 2,
-        scratch_shapes=[pltpu.VMEM((8 * sources, D), jnp.bfloat16)],
+        + [pl.BlockSpec(memory_space=pltpu.VMEM), pl.BlockSpec(memory_space=pltpu.HBM)],
+        scratch_shapes=[
+            pltpu.VMEM((4 * sources, D), jnp.bfloat16),
+            pltpu.VMEM((rows, LANES), jnp.float32),
+            pltpu.VMEM((rows, width), jnp.float32),
+            pltpu.VMEM((width, D), jnp.bfloat16),
+            pltpu.SemaphoreType.DMA,
+        ],
         compiler_params=params(MAIN_LIMIT if square else 62 * 2**20),
         cost_estimate=pl.CostEstimate(flops=6 * rows * D * width, bytes_accessed=4 * D * width, transcendentals=0),
-    )(*blocks, near_w_input, near_w_output)
-
-    unit_wide = jax.ShapeDtypeStruct((BLOCK, D), jnp.float32)
-    tail_type = jax.ShapeDtypeStruct((BLOCK - 8, D), jnp.bfloat16)
+    )(*blocks, near_w_input, far(w_output))
+
+    unit_wide = jax.ShapeDtypeStruct((16, WIDE), jnp.float32)
+    tail_type = jax.ShapeDtypeStruct((8, WIDE), jnp.bfloat16)
     if square:
         swapped = flip(send_half, 1)
-        stats_sib, stats_near = after((stats_sib, stats_near), keep_half)
-        stats_far, stats_side = cross(stats_sib), core(stats_near)
         summed = pl.pallas_call(
             sum_pairs_kernel,
             out_shape=[unit_wide] + [block_type] * 3,
             compiler_params=params(),
         )(keep_half, swapped)
         parts = [summed[0], flip(summed[1], 2), flip(summed[2], 4), flip(summed[3], 6)]
-        all_stats = after((stats, stats_sib, stats_near, stats_far, stats_side), summed[0])
+        all_stats = after(all_stats, summed[0])
     else:
         units = jnp.concatenate([keep_half, send_half]).astype(jnp.float32)
         parts = [
-            lax.psum_scatter(units, "seq", axis_index_groups=halves, tiled=True).reshape(BLOCK, D)
+            lax.psum_scatter(units, "seq", axis_index_groups=halves, tiled=True).reshape(16, WIDE)
         ]
-        all_stats = (stats, stats_sib, stats_near, cross(stats_sib), core(stats_near))
     query, to_sib, to_near, kv_grad = attention_grads(held, all_stats)
     parts[0] = after(parts[0], query)
     own_unit, send_unit = pl.pallas_call(

time: 89.1 us -> 76.1 us (0.85); the launches traced: 87.3 us -> 75.8 us
  waiting for transfers between devices: 14.4 us -> 9.77 us
  starting transfers between devices: 30.6 us -> 26.1 us
  Pallas kernels: 40.8 us -> 38.5 us
    ppermute x4 -> x3, starting transfers between devices: 19.2 us -> 10.1 us  [cross(): return lax.ppermute(block, 'seq', crossing + [(j, i) for i, j in crossing])]
    ppermute x4 -> x3, waiting for transfers between devices: 9.96 us -> 4.28 us  [cross(): return lax.ppermute(block, 'seq', crossing + [(j, i) for i, j in crossing])]
    ppermute x4, starting transfers between devices: 0.28 us -> 3.03 us  [core(): lax.ppermute(block, 'seq', [(i, i ^ 1) for i in range(lax.axis_size('seq'...]
    pallas_call x1, Pallas kernels: 6.39 us -> 4 us  [fetch(): pl.pallas_call(functools.partial(fetch_kernel, len(arrays)), in_specs=[pl...]
    ppermute x13, starting transfers between devices: 11.1 us -> 12.9 us  [flip(): return lax.ppermute(block, 'seq', [(i, i ^ bits) for i in range(devices)])]
    ppermute x4, waiting for transfers between devices: 0.01 us -> 1.57 us  [core(): lax.ppermute(block, 'seq', [(i, i ^ 1) for i in range(lax.axis_size('seq'...]
  transfers between devices with their start and end apart: 21 -> 20, of which waited for: 8 -> 8; matrix products, arithmetic and copies ran while one was open for 0% -> 0% of each run, Pallas kernels for 34% -> 36%
where the time goes in v3:
time: 76.1 us; the launch traced here: 75.8 us
  Pallas kernels  38.5 us (51%)
  starting transfers between devices  26.1 us (34%)
  waiting for transfers between devices  9.77 us (13%)
  between operations  0.77 us (1%)
    ppermute x13, starting transfers between devices, flip(): return lax.ppermute(block, 'seq', [(i, i ^ bits) for i in range(devices)])  12.9 us
    ppermute x3, starting transfers between devices, cross(): return lax.ppermute(block, 'seq', crossing + [(j, i) for i, j in crossing])  10.1 us
    pallas_call x1, Pallas kernels, attention_grads(): pl.pallas_call(grads_kernel, out_shape=(jax.ShapeDtypeStruct((tokens, D),...  9.89 us
    pallas_call x1, Pallas kernels, local(): pl.pallas_call(functools.partial(main_kernel, places), out_shape=[slots,...  9.07 us
    pallas_call x1, Pallas kernels, local(): pl.pallas_call(weights_kernel, grid=(pieces,), in_specs=[pl.BlockSpec((ro...  6.93 us
    pallas_call x1, Pallas kernels, attention_stats(): pl.pallas_call(stats_kernel, out_shape=jax.ShapeDtypeStruct((3 * tokens,...  5.65 us
    ppermute x3, waiting for transfers between devices, cross(): return lax.ppermute(block, 'seq', crossing + [(j, i) for i, j in crossing])  4.28 us
    pallas_call x1, Pallas kernels, fetch(): pl.pallas_call(functools.partial(fetch_kernel, len(arrays)), in_specs=[pl...  4 us
  transfers between devices with their start and end apart: 20, of which 8 were waited for; matrix products, arithmetic and copies ran while one was open for 0% of the time, Pallas kernels for 36%

profile of v3, /device:TPU:1, one launch (start us, length us, event | category | flops | bytes accessed | tf_op | source)
XLA Modules:
  0.0 75.8 jit_solution(8789745837438289453)
XLA Ops:
  0.6 1.7 %shard_map.163 = (bf16[16,5248]{1,0:T(8,128)(2,1)S(1)}, bf16[16,5248]{1,0:T(8,128)(2,1)S(1)}, bf16[32,4224]{1,0:T(8,128)(2,1)S(1)}) custom-call(s32[1,16]{1,0:T(1,128)} %bitcast.22, s32[1,16]{1,0:T(1,128)} %bitcast.24, bf16[1,16]{1,0:T(2,128)(2,1)} %bitcast.26, bf16[16,4096]{1,0:T(8,128)(2,1)} %input_ref.1, bf16[16,4096]{1,0:T(8,128)(2,1)} %grad_ref.1, ...), custom_call_target="tpu_custom_call" | custom-call | tf_op jit(solution)/shard_map/pallas_call | solution.py:398
  2.3 4.2 %collective-permute-start.2 = (bf16[16,5248]{1,0:T(8,128)(2,1)S(1)}, bf16[16,5248]{1,0:T(8,128)(2,1)S(1)}, u32[]{:S(2)}, u32[]{:S(2)}) collective-permute-start(bf16[16,5248]{1,0:T(8,128)(2,1)S(1)} %get-tuple-element.54), channel_id=1, source_target_pairs={{0,12},{1,13},{2,14},{3,15},{4,8},{5,9},{6,10},{7,11},{8,4},{9,5},... | collective-permute-start | bytes 503816 | tf_op jit(solution)/shard_map/ppermute | solution.py:393
  6.5 4.0 %collective-permute-start.1 = (bf16[32,4224]{1,0:T(8,128)(2,1)S(1)}, bf16[32,4224]{1,0:T(8,128)(2,1)S(1)}, u32[]{:S(2)}, u32[]{:S(2)}) collective-permute-start(bf16[32,4224]{1,0:T(8,128)(2,1)S(1)} %get-tuple-element.51.own_ref), channel_id=1, source_target_pairs={{1,2},{3,4},{5,6},{7,8},{9,10},{11,12},{13,14},{2,1},{4,3},{6,5},{... | collective-permute-start | bytes 811016 | tf_op jit(solution)/shard_map/ppermute | solution.py:307
  10.6 4.0 %shard_map.164 = (bf16[4096,1024]{1,0:T(8,128)(2,1)S(1)}, bf16[128,2,4096]{2,1,0:T(2,128)(2,1)S(1)}) custom-call(bf16[4096,1024]{1,0:T(8,128)(2,1)} %refs_0_.1, bf16[128,2,4096]{2,1,0:T(2,128)(2,1)} %refs_1_.1), custom_call_target="tpu_custom_call" | custom-call | bytes 10485760 | tf_op jit(solution)/shard_map/pallas_call | solution.py:356
  14.6 2.2 %collective-permute-done.1.near_ref = bf16[32,4224]{1,0:T(8,128)(2,1)S(1)} collective-permute-done((bf16[32,4224]{1,0:T(8,128)(2,1)S(1)}, bf16[32,4224]{1,0:T(8,128)(2,1)S(1)}, u32[]{:S(2)}, u32[]{:S(2)}) %collective-permute-start.1) | collective-permute-done | bytes 270368 | tf_op jit(solution)/shard_map/ppermute | solution.py:307
  16.8 1.1 %collective-permute-start.5 = (bf16[32,5248]{1,0:T(8,128)(2,1)S(1)}, bf16[32,5248]{1,0:T(8,128)(2,1)S(1)}, u32[]{:S(2)}, u32[]{:S(2)}) collective-permute-start(bf16[32,5248]{1,0:T(8,128)(2,1)S(1)} %pad_maximum_fusion), channel_id=1, source_target_pairs={{0,6},{1,7},{2,4},{3,5},{4,2},{5,3},{6,0},{7,1},{8,14},{9,15},{10,... | collective-permute-start | bytes 1007624 | tf_op jit(solution)/shard_map/ppermute | solution.py:393
  17.9 1.5 %collective-permute-start.3 = (bf16[32,5248]{1,0:T(8,128)(2,1)S(1)}, bf16[32,5248]{1,0:T(8,128)(2,1)S(1)}, u32[]{:S(2)}, u32[]{:S(2)}) collective-permute-start(bf16[32,5248]{1,0:T(8,128)(2,1)S(1)} %pad_maximum_fusion), channel_id=1, source_target_pairs={{0,2},{1,3},{2,0},{3,1},{4,6},{5,7},{6,4},{7,5},{8,10},{9,11},{10,... | collective-permute-start | bytes 1007624 | tf_op jit(solution)/shard_map/ppermute | solution.py:393
  19.4 5.7 %shard_map.165.st_ref = f32[48,128]{1,0:T(8,128)S(1)} custom-call(bf16[32,4224]{1,0:T(8,128)(2,1)S(1)} %get-tuple-element.51.own_ref, bf16[32,4224]{1,0:T(8,128)(2,1)S(1)} %collective-permute-done.sib_ref, bf16[32,4224]{1,0:T(8,128)(2,1)S(1)} %collective-permute-done.1.near_ref, s32[1,128]{1,0:T(1,128)} %bitcast.28, ...), custom_call_target="tpu_custom_call" | custom-call | flops 1000000000 | bytes 16000000 | tf_op jit(solution)/shard_map/pallas_call | solution.py:312
  25.1 1.8 %collective-permute-start.6 = (f32[48,128]{1,0:T(8,128)S(1)}, f32[48,128]{1,0:T(8,128)S(1)}, u32[]{:S(2)}, u32[]{:S(2)}) collective-permute-start(f32[48,128]{1,0:T(8,128)S(1)} %shard_map.165.st_ref), channel_id=1, source_target_pairs={{0,1},{1,0},{2,3},{3,2},{4,5},{5,4},{6,7},{7,6},{8,9},{9,8},{10,11... | collective-permute-start | bytes 73736 | tf_op jit(solution)/shard_map/ppermute | solution.py:302
  26.8 0.8 %collective-permute-done.6.st_sib_ref = f32[48,128]{1,0:T(8,128)S(1)} collective-permute-done((f32[48,128]{1,0:T(8,128)S(1)}, f32[48,128]{1,0:T(8,128)S(1)}, u32[]{:S(2)}, u32[]{:S(2)}) %collective-permute-start.6) | collective-permute-done | bytes 24608 | tf_op jit(solution)/shard_map/ppermute | solution.py:302
  27.7 4.1 %collective-permute-start.7 = (f32[96,128]{1,0:T(8,128)S(1)}, f32[96,128]{1,0:T(8,128)S(1)}, u32[]{:S(2)}, u32[]{:S(2)}) collective-permute-start(f32[96,128]{1,0:T(8,128)S(1)} %pad_maximum_fusion.1), channel_id=1, source_target_pairs={{1,2},{3,4},{5,6},{7,8},{9,10},{11,12},{13,14},{2,1},{4,3},{6,5},{... | collective-permute-start | bytes 147464 | tf_op jit(solution)/shard_map/ppermute | solution.py:307
  31.8 2.1 %collective-permute-done.7.met_ref = f32[96,128]{1,0:T(8,128)S(1)} collective-permute-done((f32[96,128]{1,0:T(8,128)S(1)}, f32[96,128]{1,0:T(8,128)S(1)}, u32[]{:S(2)}, u32[]{:S(2)}) %collective-permute-start.7) | collective-permute-done | bytes 49184 | tf_op jit(solution)/shard_map/ppermute | solution.py:307
  33.9 0.5 collective-permute-start.9
  34.4 0.7 collective-permute-done.8.sib_met_ref
  35.1 0.2 collective-permute-start.10
  35.4 0.3 collective-permute-start.11
  35.9 1.0 %collective-permute-done.10 = bf16[32,5248]{1,0:T(8,128)(2,1)S(1)} collective-permute-done((bf16[32,5248]{1,0:T(8,128)(2,1)S(1)}, bf16[32,5248]{1,0:T(8,128)(2,1)S(1)}, u32[]{:S(2)}, u32[]{:S(2)}) %collective-permute-start.10) | collective-permute-done | bytes 335904 | tf_op jit(solution)/shard_map/ppermute | solution.py:393
  36.8 0.5 collective-permute-done.11
  37.3 0.5 collective-permute-done.12
  37.8 9.1 %shard_map.166 = (bf16[160,4096]{1,0:T(8,128)(2,1)S(1)}, bf16[160,4096]{1,0:T(8,128)(2,1)S(1)}, bf16[160,1024]{1,0:T(8,128)(2,1)S(1)}, bf16[160,1024]{1,0:T(8,12...) custom-call(bf16[1,32,5248]{2,1,0:T(8,128)(2,1)S(1)} %bitcast.14, ...), custom_call_target="tpu_custom_call" | custom-call | flops 4026531840 | bytes 16777216 | tf_op jit(solution)/shard_map/pallas_call | solution.py:437
  46.9 0.2 collective-permute-start.13
  47.1 2.0 %collective-permute-done.13.got_ref = bf16[4,16,5248]{2,1,0:T(8,128)(2,1)S(1)} collective-permute-done((bf16[4,16,5248]{2,1,0:T(8,128)(2,1)S(1)}, bf16[4,16,5248]{2,1,0:T(8,128)(2,1)S(1)}, u32[]{:S(2)}, u32[]{:S(2)}) %collective-permute-start.13) | collective-permute-done | bytes 671776 | tf_op jit(solution)/shard_map/ppermute | solution.py:393
  49.3 1.9 %collective-permute-start.14 = (bf16[16,5248]{1,0:T(8,128)(2,1)S(1)}, bf16[16,5248]{1,0:T(8,128)(2,1)S(1)}, u32[]{:S(2)}, u32[]{:S(2)}) collective-permute-start(bf16[16,5248]{1,0:T(8,128)(2,1)S(1)} %get-tuple-element.76), channel_id=1, source_target_pairs={{0,2},{1,3},{2,0},{3,1},{4,6},{5,7},{6,4},{7,5},{8,10},{9,11},{10,... | collective-permute-start | bytes 503816 | tf_op jit(solution)/shard_map/ppermute | solution.py:393
  51.2 0.6 collective-permute-start.15
  51.8 0.7 collective-permute-start.16
  52.4 9.9 %shard_map.168 = (f32[16,4096]{1,0:T(8,128)S(1)}, bf16[16,4096]{1,0:T(8,128)(2,1)S(1)}, bf16[16,4096]{1,0:T(8,128)(2,1)S(1)}, bf16[128,2,4096]{2,1,0:T(2,128)(2,1)}) custom-call(bf16[32,4224]{1,0:T(8,128)(2,1)S(1)} %get-tuple-element.51.own_ref, bf16[32,4224]{1,0:T(8,128)(2,1)S(1)} %collective-permute-done.sib_ref, ...), custom_call_target="tpu_custom_call" | custom-call | flops 1000000000 | bytes 32000000 | tf_op jit(solution)/shard_map/pallas_call | solution.py:323
  62.4 1.4 %collective-permute-start.19 = (bf16[8,5248]{1,0:T(8,128)(2,1)S(1)}, bf16[8,5248]{1,0:T(8,128)(2,1)S(1)}, u32[]{:S(2)}, u32[]{:S(2)}) collective-permute-start(bf16[8,5248]{1,0:T(8,128)(2,1)S(1)} %get-tuple-element.83), channel_id=1, source_target_pairs={{0,12},{1,13},{2,14},{3,15},{4,8},{5,9},{6,10},{7,11},{8,4},{9,5},... | collective-permute-start | bytes 251912 | tf_op jit(solution)/shard_map/ppermute | solution.py:393
  63.9 1.2 %collective-permute-start.17 = (bf16[16,4096]{1,0:T(8,128)(2,1)S(1)}, bf16[16,4096]{1,0:T(8,128)(2,1)S(1)}, u32[]{:S(2)}, u32[]{:S(2)}) collective-permute-start(bf16[16,4096]{1,0:T(8,128)(2,1)S(1)} %get-tuple-element.80), channel_id=1, source_target_pairs={{0,1},{1,0},{2,3},{3,2},{4,5},{5,4},{6,7},{7,6},{8,9},{9,8},{10,11... | collective-permute-start | bytes 393224 | tf_op jit(solution)/shard_map/ppermute | solution.py:302
  65.1 2.1 %collective-permute-start.18 = (bf16[16,4096]{1,0:T(8,128)(2,1)S(1)}, bf16[16,4096]{1,0:T(8,128)(2,1)S(1)}, u32[]{:S(2)}, u32[]{:S(2)}) collective-permute-start(bf16[16,4096]{1,0:T(8,128)(2,1)S(1)} %get-tuple-element.81), channel_id=1, source_target_pairs={{1,2},{3,4},{5,6},{7,8},{9,10},{11,12},{13,14},{2,1},{4,3},{6,5},{... | collective-permute-start | bytes 393224 | tf_op jit(solution)/shard_map/ppermute | solution.py:307
  67.1 6.9 %shard_map.171 = (bf16[4096,1024]{1,0:T(8,128)(2,1)}, bf16[1024,4096]{1,0:T(8,128)(2,1)}) custom-call(bf16[160,4096]{1,0:T(8,128)(2,1)S(1)} %get-tuple-element.90.x_ref, bf16[160,1024]{1,0:T(8,128)(2,1)S(1)} %get-tuple-element.91.hidden_ref, bf16[160,1024]{1,0:T(8,128)(2,1)S(1)} %get-tuple-element.92.scaled_ref, bf16[160,4096]{1,0:T(8,128)(2,1)S(1)} %get-tuple-element.93.g_ref), custom_call_target="tpu_custom_call" | custom-call | flops 2684354560 | bytes 16777216 | tf_op jit(solution)/shard_map/pallas_call | solution.py:481
  74.1 1.0 %shard_map.170 = (bf16[16,4096]{1,0:T(8,128)(2,1)}, f32[1,16]{1,0:T(1,128)}) custom-call(s32[1,16]{1,0:T(1,128)S(1)} %bitcast.23, s32[1,16]{1,0:T(1,128)S(1)} %bitcast.25, f32[16,5248]{1,0:T(8,128)S(1)} %get-tuple-element.79.own_ref, bf16[8,5248]{1,0:T(8,128)(2,1)S(1)} %collective-permute-done.19.got_ref), custom_call_target="tpu_custom_call" | custom-call | tf_op jit(solution)/shard_map/pallas_call | solution.py:502
  75.1 0.7 add_convert_fusion
  (24 shorter events, 0.5 us)
Async XLA Ops:
  2.3 12.3 %collective-permute-start.2 = (bf16[16,5248]{1,0:T(8,128)(2,1)S(1)}, bf16[16,5248]{1,0:T(8,128)(2,1)S(1)}, u32[]{:S(2)}, u32[]{:S(2)}) collective-permute-start(bf16[16,5248]{1,0:T(8,128)(2,1)S(1)} %get-tuple-element.54), channel_id=1, source_target_pairs={{0,12},{1,13},{2,14},{3,15},{4,8},{5,9},{6,10},{7,11},{8,4},{9,5},... | collective-permute-start | bytes 503816 | tf_op jit(solution)/shard_map/ppermute | solution.py:393
  6.5 10.3 %collective-permute-start.1 = (bf16[32,4224]{1,0:T(8,128)(2,1)S(1)}, bf16[32,4224]{1,0:T(8,128)(2,1)S(1)}, u32[]{:S(2)}, u32[]{:S(2)}) collective-permute-start(bf16[32,4224]{1,0:T(8,128)(2,1)S(1)} %get-tuple-element.51.own_ref), channel_id=1, source_target_pairs={{1,2},{3,4},{5,6},{7,8},{9,10},{11,12},{13,14},{2,1},{4,3},{6,5},{... | collective-permute-start | bytes 811016 | tf_op jit(solution)/shard_map/ppermute | solution.py:307
  10.5 6.3 %collective-permute-start = (bf16[32,4224]{1,0:T(8,128)(2,1)S(1)}, bf16[32,4224]{1,0:T(8,128)(2,1)S(1)}, u32[]{:S(2)}, u32[]{:S(2)}) collective-permute-start(bf16[32,4224]{1,0:T(8,128)(2,1)S(1)} %get-tuple-element.51.own_ref), channel_id=1, source_target_pairs={{0,1},{1,0},{2,3},{3,2},{4,5},{5,4},{6,7},{7,6},{8,9},{9,8},{10,11... | collective-permute-start | bytes 811016 | tf_op jit(solution)/shard_map/ppermute | solution.py:302
  16.8 18.4 %collective-permute-start.5 = (bf16[32,5248]{1,0:T(8,128)(2,1)S(1)}, bf16[32,5248]{1,0:T(8,128)(2,1)S(1)}, u32[]{:S(2)}, u32[]{:S(2)}) collective-permute-start(bf16[32,5248]{1,0:T(8,128)(2,1)S(1)} %pad_maximum_fusion), channel_id=1, source_target_pairs={{0,6},{1,7},{2,4},{3,5},{4,2},{5,3},{6,0},{7,1},{8,14},{9,15},{10,... | collective-permute-start | bytes 1007624 | tf_op jit(solution)/shard_map/ppermute | solution.py:393
  17.9 17.2 %collective-permute-start.4 = (bf16[32,5248]{1,0:T(8,128)(2,1)S(1)}, bf16[32,5248]{1,0:T(8,128)(2,1)S(1)}, u32[]{:S(2)}, u32[]{:S(2)}) collective-permute-start(bf16[32,5248]{1,0:T(8,128)(2,1)S(1)} %pad_maximum_fusion), channel_id=1, source_target_pairs={{0,4},{1,5},{2,6},{3,7},{4,0},{5,1},{6,2},{7,3},{8,12},{9,13},{10,... | collective-permute-start | bytes 1007624 | tf_op jit(solution)/shard_map/ppermute | solution.py:393
  17.9 17.2 %collective-permute-start.3 = (bf16[32,5248]{1,0:T(8,128)(2,1)S(1)}, bf16[32,5248]{1,0:T(8,128)(2,1)S(1)}, u32[]{:S(2)}, u32[]{:S(2)}) collective-permute-start(bf16[32,5248]{1,0:T(8,128)(2,1)S(1)} %pad_maximum_fusion), channel_id=1, source_target_pairs={{0,2},{1,3},{2,0},{3,1},{4,6},{5,7},{6,4},{7,5},{8,10},{9,11},{10,... | collective-permute-start | bytes 1007624 | tf_op jit(solution)/shard_map/ppermute | solution.py:393
  25.1 2.6 %collective-permute-start.6 = (f32[48,128]{1,0:T(8,128)S(1)}, f32[48,128]{1,0:T(8,128)S(1)}, u32[]{:S(2)}, u32[]{:S(2)}) collective-permute-start(f32[48,128]{1,0:T(8,128)S(1)} %shard_map.165.st_ref), channel_id=1, source_target_pairs={{0,1},{1,0},{2,3},{3,2},{4,5},{5,4},{6,7},{7,6},{8,9},{9,8},{10,11... | collective-permute-start | bytes 73736 | tf_op jit(solution)/shard_map/ppermute | solution.py:302
  27.7 6.2 %collective-permute-start.7 = (f32[96,128]{1,0:T(8,128)S(1)}, f32[96,128]{1,0:T(8,128)S(1)}, u32[]{:S(2)}, u32[]{:S(2)}) collective-permute-start(f32[96,128]{1,0:T(8,128)S(1)} %pad_maximum_fusion.1), channel_id=1, source_target_pairs={{1,2},{3,4},{5,6},{7,8},{9,10},{11,12},{13,14},{2,1},{4,3},{6,5},{... | collective-permute-start | bytes 147464 | tf_op jit(solution)/shard_map/ppermute | solution.py:307
  33.9 1.2 %collective-permute-start.8 = (f32[96,128]{1,0:T(8,128)S(1)}, f32[96,128]{1,0:T(8,128)S(1)}, u32[]{:S(2)}, u32[]{:S(2)}) collective-permute-start(f32[96,128]{1,0:T(8,128)S(1)} %collective-permute-done.7.met_ref), channel_id=1, source_target_pairs={{0,1},{1,0},{2,3},{3,2},{4,5},{5,4},{6,7},{7,6},{8,9},{9,8},{10,11... | collective-permute-start | bytes 147464 | tf_op jit(solution)/shard_map/ppermute | solution.py:302
  33.9 2.0 %collective-permute-start.9 = (bf16[32,5248]{1,0:T(8,128)(2,1)S(1)}, bf16[32,5248]{1,0:T(8,128)(2,1)S(1)}, u32[]{:S(2)}, u32[]{:S(2)}) collective-permute-start(bf16[32,5248]{1,0:T(8,128)(2,1)S(1)} %pad_maximum_fusion), channel_id=1, source_target_pairs={{0,1},{1,0},{2,3},{3,2},{4,5},{5,4},{6,7},{7,6},{8,9},{9,8},{10,11... | collective-permute-start | bytes 1007624 | tf_op jit(solution)/shard_map/ppermute | solution.py:393
  35.1 1.7 %collective-permute-start.10 = (bf16[32,5248]{1,0:T(8,128)(2,1)S(1)}, bf16[32,5248]{1,0:T(8,128)(2,1)S(1)}, u32[]{:S(2)}, u32[]{:S(2)}) collective-permute-start(bf16[32,5248]{1,0:T(8,128)(2,1)S(1)} %collective-permute-done.3), channel_id=1, source_target_pairs={{0,1},{1,0},{2,3},{3,2},{4,5},{5,4},{6,7},{7,6},{8,9},{9,8},{10,11... | collective-permute-start | bytes 1007624 | tf_op jit(solution)/shard_map/ppermute | solution.py:393
  35.4 2.0 %collective-permute-start.11 = (bf16[32,5248]{1,0:T(8,128)(2,1)S(1)}, bf16[32,5248]{1,0:T(8,128)(2,1)S(1)}, u32[]{:S(2)}, u32[]{:S(2)}) collective-permute-start(bf16[32,5248]{1,0:T(8,128)(2,1)S(1)} %collective-permute-done.4), channel_id=1, source_target_pairs={{0,1},{1,0},{2,3},{3,2},{4,5},{5,4},{6,7},{7,6},{8,9},{9,8},{10,11... | collective-permute-start | bytes 1007624 | tf_op jit(solution)/shard_map/ppermute | solution.py:393
  35.7 2.1 %collective-permute-start.12 = (bf16[32,5248]{1,0:T(8,128)(2,1)S(1)}, bf16[32,5248]{1,0:T(8,128)(2,1)S(1)}, u32[]{:S(2)}, u32[]{:S(2)}) collective-permute-start(bf16[32,5248]{1,0:T(8,128)(2,1)S(1)} %collective-permute-done.5), channel_id=1, source_target_pairs={{0,1},{1,0},{2,3},{3,2},{4,5},{5,4},{6,7},{7,6},{8,9},{9,8},{10,11... | collective-permute-start | bytes 1007624 | tf_op jit(solution)/shard_map/ppermute | solution.py:393
  46.9 27.2 %copy-start = (s32[16]{0:T(128)S(1)}, s32[16]{0:T(128)}, u32[]{:S(2)}) copy-start(s32[16]{0:T(128)} %param.20) | copy-start | bytes 196
  46.9 27.2 %copy-start.1 = (s32[16]{0:T(128)S(1)}, s32[16]{0:T(128)}, u32[]{:S(2)}) copy-start(s32[16]{0:T(128)} %param.21) | copy-start | bytes 196
  46.9 2.2 %collective-permute-start.13 = (bf16[4,16,5248]{2,1,0:T(8,128)(2,1)S(1)}, bf16[4,16,5248]{2,1,0:T(8,128)(2,1)S(1)}, u32[]{:S(2)}, u32[]{:S(2)}) collective-permute-start(bf16[4,16,5248]{2,1,0:T(8,128)(2,1)S(1)} %get-tuple-element.66), channel_id=1, source_target_pairs={{0,1},{1,0},{2,3},{3,2},{4,5},{5,4},{6,7},{7,6},{8,9},{9,8},{10,11... | collective-permute-start | bytes 2015240 | tf_op jit(solution)/shard_map/ppermute | solution.py:393
  49.3 13.1 %collective-permute-start.14 = (bf16[16,5248]{1,0:T(8,128)(2,1)S(1)}, bf16[16,5248]{1,0:T(8,128)(2,1)S(1)}, u32[]{:S(2)}, u32[]{:S(2)}) collective-permute-start(bf16[16,5248]{1,0:T(8,128)(2,1)S(1)} %get-tuple-element.76), channel_id=1, source_target_pairs={{0,2},{1,3},{2,0},{3,1},{4,6},{5,7},{6,4},{7,5},{8,10},{9,11},{10,... | collective-permute-start | bytes 503816 | tf_op jit(solution)/shard_map/ppermute | solution.py:393
  51.2 11.2 %collective-permute-start.15 = (bf16[16,5248]{1,0:T(8,128)(2,1)S(1)}, bf16[16,5248]{1,0:T(8,128)(2,1)S(1)}, u32[]{:S(2)}, u32[]{:S(2)}) collective-permute-start(bf16[16,5248]{1,0:T(8,128)(2,1)S(1)} %get-tuple-element.77), channel_id=1, source_target_pairs={{0,4},{1,5},{2,6},{3,7},{4,0},{5,1},{6,2},{7,3},{8,12},{9,13},{10,... | collective-permute-start | bytes 503816 | tf_op jit(solution)/shard_map/ppermute | solution.py:393
  51.8 10.6 %collective-permute-start.16 = (bf16[16,5248]{1,0:T(8,128)(2,1)S(1)}, bf16[16,5248]{1,0:T(8,128)(2,1)S(1)}, u32[]{:S(2)}, u32[]{:S(2)}) collective-permute-start(bf16[16,5248]{1,0:T(8,128)(2,1)S(1)} %get-tuple-element.78), channel_id=1, source_target_pairs={{0,6},{1,7},{2,4},{3,5},{4,2},{5,3},{6,0},{7,1},{8,14},{9,15},{10,... | collective-permute-start | bytes 503816 | tf_op jit(solution)/shard_map/ppermute | solution.py:393
  62.4 11.6 %collective-permute-start.19 = (bf16[8,5248]{1,0:T(8,128)(2,1)S(1)}, bf16[8,5248]{1,0:T(8,128)(2,1)S(1)}, u32[]{:S(2)}, u32[]{:S(2)}) collective-permute-start(bf16[8,5248]{1,0:T(8,128)(2,1)S(1)} %get-tuple-element.83), channel_id=1, source_target_pairs={{0,12},{1,13},{2,14},{3,15},{4,8},{5,9},{6,10},{7,11},{8,4},{9,5},... | collective-permute-start | bytes 251912 | tf_op jit(solution)/shard_map/ppermute | solution.py:393
  63.9 11.3 %collective-permute-start.17 = (bf16[16,4096]{1,0:T(8,128)(2,1)S(1)}, bf16[16,4096]{1,0:T(8,128)(2,1)S(1)}, u32[]{:S(2)}, u32[]{:S(2)}) collective-permute-start(bf16[16,4096]{1,0:T(8,128)(2,1)S(1)} %get-tuple-element.80), channel_id=1, source_target_pairs={{0,1},{1,0},{2,3},{3,2},{4,5},{5,4},{6,7},{7,6},{8,9},{9,8},{10,11... | collective-permute-start | bytes 393224 | tf_op jit(solution)/shard_map/ppermute | solution.py:302
  65.1 10.1 %collective-permute-start.18 = (bf16[16,4096]{1,0:T(8,128)(2,1)S(1)}, bf16[16,4096]{1,0:T(8,128)(2,1)S(1)}, u32[]{:S(2)}, u32[]{:S(2)}) collective-permute-start(bf16[16,4096]{1,0:T(8,128)(2,1)S(1)} %get-tuple-element.81), channel_id=1, source_target_pairs={{1,2},{3,4},{5,6},{7,8},{9,10},{11,12},{13,14},{2,1},{4,3},{6,5},{... | collective-permute-start | bytes 393224 | tf_op jit(solution)/shard_map/ppermute | solution.py:307

commit v4 on v3

--- a/solution.py
+++ b/solution.py
@@ -19,6 +19,7 @@
 WIDE = D + FOLD + LANES
 TAILS = slice(D, D + FOLD)
 SIDE = slice(D + FOLD, WIDE)
+GROUP = 4
 MAIN_LIMIT = 24 * 2**20
 
 
@@ -162,7 +163,11 @@
     send_ref[:, SIDE] = jnp.where(lane == 0, unit[8:, SIDE], ends).astype(jnp.bfloat16)
 
 
-def scatter_kernel(mine, ids_ref, keep_ref, own_ref, got_ref, grad_ref, gate_ref):
+def last_kernel(
+    mine, ids_ref, keep_ref, own_ref, got_ref, query_ref, sib_ref, near_ref, grad_ref, gate_ref, query_grad_ref
+):
+    query = query_ref[...] + sib_ref[...].astype(jnp.float32) + near_ref[...].astype(jnp.float32)
+    query_grad_ref[...] = query.astype(jnp.bfloat16)
     ids, keep = ids_ref[...], keep_ref[...]
     tokens = ids.shape[1]
     expert = mine()
@@ -189,7 +194,7 @@
 
 def pack_tokens(query_ref, grad_ref, segments_ref, out_ref):
     tokens = query_ref.shape[0]
-    out_ref[:tokens, :D] = query_ref[...]
+    out_ref[:tokens, :D] = (SCALE * query_ref[...].astype(jnp.float32)).astype(jnp.bfloat16)
     out_ref[tokens:, :D] = grad_ref[...]
     segments = segments_ref[...] + 1
     diagonal = iota((tokens, tokens), 0) == iota((tokens, tokens), 1)
@@ -240,29 +245,34 @@
     token_refs = (own_ref, sib_ref, near_ref)
     tokens = own_ref.shape[0] // 2
     allowed = allowed_pairs(token_refs, rows_ref, tokens)
+    valid = jnp.where(allowed, 1.0, 0.0)
     lane = iota((3 * tokens, LANES), 1)
     stats = jnp.zeros((3 * tokens, LANES), jnp.float32)
-    for head in range(HEADS):
-        _, _, scores, prob_grad = head_scores(token_refs, load_head(kv_ref, head), head, tokens)
-        scores = jnp.where(allowed, SCALE * scores, NONE)
-        peak = jnp.max(scores, axis=1, keepdims=True)
-        weight = jnp.where(allowed, jnp.exp(scores - peak), 0.0)
-        mass = jnp.sum(weight, axis=1, keepdims=True)
-        delta = jnp.sum(weight * prob_grad, axis=1, keepdims=True)
-        stats = jnp.where(lane == head, peak, stats)
-        stats = jnp.where(lane == HEADS + head, mass, stats)
-        stats = jnp.where(lane == 2 * HEADS + head, delta, stats)
+    for first in range(0, HEADS, GROUP):
+        products = [
+            head_scores(token_refs, load_head(kv_ref, first + i), first + i, tokens) for i in range(GROUP)
+        ]
+        for head, (_, _, scores, prob_grad) in enumerate(products, first):
+            scores = jnp.where(allowed, scores, NONE)
+            peak = jnp.max(scores, axis=1, keepdims=True)
+            weight = jnp.exp(scores - peak) * valid
+            mass = jnp.sum(weight, axis=1, keepdims=True)
+            delta = jnp.sum(weight * prob_grad, axis=1, keepdims=True)
+            stats = jnp.where(lane == head, peak, stats)
+            stats = jnp.where(lane == HEADS + head, mass, stats)
+            stats = jnp.where(lane == 2 * HEADS + head, delta, stats)
     stats_ref[...] = stats
 
 
 def merged(parts):
     peaks = [jnp.where(p[:, HEADS : 2 * HEADS] > 0, p[:, :HEADS], NONE) for p in parts]
-    peak = jnp.maximum(jnp.maximum(peaks[0], peaks[1]), peaks[2])
+    peak = functools.reduce(jnp.maximum, peaks)
     scale = [jnp.exp(p - peak) for p in peaks]
     mass = sum(s * p[:, HEADS : 2 * HEADS] for s, p in zip(scale, parts))
     delta = sum(s * p[:, 2 * HEADS : 3 * HEADS] for s, p in zip(scale, parts))
-    inverse = jnp.where(mass > 0, 1.0 / mass, 0.0)
-    return peak, inverse, delta * inverse
+    some = mass > 0
+    mass = jnp.where(some, mass, 1.0)
+    return jnp.where(some, peak + jnp.log(mass), 0.0), jnp.where(some, delta / mass, 0.0)
 
 
 def grads_kernel(
@@ -279,23 +289,28 @@
         merged((st_ref[b], st_sib_ref[a], sib_met_ref[c])),
         merged((st_ref[c], met_ref[a], met_ref[far_b])),
     ]
-    peak, scale, delta = (jnp.concatenate([t[i] for t in totals], axis=0) for i in range(3))
-    for head in range(HEADS):
-        kv = load_head(kv_ref, head)
-        queries, grads, scores, prob_grad = head_scores(token_refs, kv, head, tokens)
-        at = slice(head, head + 1)
-        probs = jnp.exp(jnp.where(allowed, SCALE * scores - peak[:, at], NONE)) * scale[:, at]
-        score_grad = SCALE * (probs * (prob_grad - delta[:, at]))
-        moved = pltpu.roll(probs, 1, 1)
-        score_low = score_grad.astype(jnp.bfloat16)
-        query = mm(score_low, kv)
-        lanes = pl.ds(head * HEAD_DIM, HEAD_DIM)
-        query_ref[:, lanes] = query[a]
-        to_sib_ref[:, lanes] = query[b].astype(jnp.bfloat16)
-        to_near_ref[:, lanes] = query[c].astype(jnp.bfloat16)
-        both = jnp.concatenate([score_low, moved.astype(jnp.bfloat16)], axis=0)
-        grad = mm(both, jnp.concatenate([queries, grads], axis=0), ((0,), (0,)))
-        kv_grad_ref[:, :, lanes] = grad.astype(jnp.bfloat16).reshape(kv_grad_ref.shape[0], 2, HEAD_DIM)
+    total, delta = (jnp.concatenate([t[i] for t in totals], axis=0) for i in range(2))
+    for first in range(0, HEADS, GROUP):
+        kvs = [load_head(kv_ref, first + i) for i in range(GROUP)]
+        products = [head_scores(token_refs, kv, first + i, tokens) for i, kv in enumerate(kvs)]
+        lows = []
+        for head, (_, _, scores, prob_grad) in enumerate(products, first):
+            at = slice(head, head + 1)
+            probs = jnp.exp(jnp.where(allowed, scores - total[:, at], NONE))
+            score_grad = probs * (prob_grad - delta[:, at])
+            moved = pltpu.roll(probs, 1, 1)
+            lows.append((score_grad.astype(jnp.bfloat16), moved.astype(jnp.bfloat16)))
+        for head, kv, (queries, grads, _, _), (score_low, probs_low) in zip(
+            range(first, first + GROUP), kvs, products, lows
+        ):
+            lanes = pl.ds(head * HEAD_DIM, HEAD_DIM)
+            query = SCALE * mm(score_low, kv)
+            query_ref[:, lanes] = query[a]
+            to_sib_ref[:, lanes] = query[b].astype(jnp.bfloat16)
+            to_near_ref[:, lanes] = query[c].astype(jnp.bfloat16)
+            both = jnp.concatenate([score_low, probs_low], axis=0)
+            grad = mm(both, jnp.concatenate([queries, grads], axis=0), ((0,), (0,)))
+            kv_grad_ref[:, :, lanes] = grad.astype(jnp.bfloat16).reshape(kv_grad_ref.shape[0], 2, HEAD_DIM)
 
 
 def core(block):
@@ -419,7 +434,8 @@
         pair = after(pair, held[1], held[2], near_kv)
         near = [pair, flip(pair, 2), flip(pair, 4), flip(pair, 6)]
         beside = flip(pair, 1)
-        *near, all_stats = lax.optimization_barrier((*near, all_stats))
+        near[1:3] = after(near[1:3], stats_sib)
+        near[3], all_stats = lax.optimization_barrier((near[3], all_stats))
         blocks = [b[None] for b in near + [beside] + [flip(b, 1) for b in near[1:]]]
     else:
         halves = [list(range(e * shards, (e + 1) * shards)) for e in range(EXPERTS)]
@@ -473,7 +489,7 @@
     )(*parts)
     returned = flip(send_unit, across)
     to_sib, to_near = after((to_sib, to_near), own_unit)
-    query_grad = query + core(to_sib).astype(jnp.float32) + cross(to_near).astype(jnp.float32)
+    from_sib, from_near = core(to_sib), cross(to_near)
 
     x, hidden, scaled, g = after((x, hidden, scaled, g), own_unit)
     pieces = max(1, min(4, width // 128))
@@ -499,16 +515,17 @@
         cost_estimate=pl.CostEstimate(flops=4 * rows * D * width, bytes_accessed=4 * D * width, transcendentals=0),
     )(x, hidden, scaled, g)
 
-    moe_input_grad, gate_grad = pl.pallas_call(
-        functools.partial(scatter_kernel, mine),
+    moe_input_grad, gate_grad, query_grad = pl.pallas_call(
+        functools.partial(last_kernel, mine),
         out_shape=(
             jax.ShapeDtypeStruct((tokens, D), jnp.bfloat16),
             jax.ShapeDtypeStruct((1, tokens), jnp.float32),
+            jax.ShapeDtypeStruct((tokens, D), jnp.bfloat16),
         ),
         compiler_params=params(),
-    )(ids, keep, own_unit, returned)
+    )(ids, keep, own_unit, returned, query, from_sib, from_near)
     return (
-        query_grad.astype(jnp.bfloat16),
+        query_grad,
         kv_grad,
         moe_input_grad,
         gate_grad.reshape(tokens),

time: 76.1 us -> 73.1 us (0.961)
  Pallas kernels: 38.5 us -> 34.9 us
  waiting for transfers between devices: 9.77 us -> 11.2 us
    pallas_call x1, Pallas kernels: 9.89 us -> 7.01 us  [attention_grads(): pl.pallas_call(grads_kernel, out_shape=(jax.ShapeDtypeStruct((tokens, D),...]
    ppermute x13, starting transfers between devices: 12.9 us -> 12.1 us  [flip(): return lax.ppermute(block, 'seq', [(i, i ^ bits) for i in range(devices)])]
    pallas_call x1, Pallas kernels: 5.65 us -> 4.86 us  [attention_stats(): pl.pallas_call(stats_kernel, out_shape=jax.ShapeDtypeStruct((3 * tokens,...]
    ppermute x3, waiting for transfers between devices: 4.28 us -> 5.07 us  [cross(): return lax.ppermute(block, 'seq', crossing + [(j, i) for i, j in crossing])]
  transfers between devices with their start and end apart: 20 -> 20, of which waited for: 8 -> 9; matrix products, arithmetic and copies ran while one was open for 0% -> 0% of each run, Pallas kernels for 36% -> 31%
where the time goes in v4:
time: 73.1 us; the launch traced here: 72.9 us
  Pallas kernels  34.9 us (48%)
  starting transfers between devices  26 us (36%)
  waiting for transfers between devices  11.2 us (15%)
  between operations  0.77 us (1%)
    ppermute x13, starting transfers between devices, flip(): return lax.ppermute(block, 'seq', [(i, i ^ bits) for i in range(devices)])  12.1 us
    ppermute x3, starting transfers between devices, cross(): return lax.ppermute(block, 'seq', crossing + [(j, i) for i, j in crossing])  10.6 us
    pallas_call x1, Pallas kernels, local(): pl.pallas_call(functools.partial(main_kernel, places), out_shape=[slots,...  9.08 us
    pallas_call x1, Pallas kernels, attention_grads(): pl.pallas_call(grads_kernel, out_shape=(jax.ShapeDtypeStruct((tokens, D),...  7.01 us
    pallas_call x1, Pallas kernels, local(): pl.pallas_call(weights_kernel, grid=(pieces,), in_specs=[pl.BlockSpec((ro...  6.92 us
    ppermute x3, waiting for transfers between devices, cross(): return lax.ppermute(block, 'seq', crossing + [(j, i) for i, j in crossing])  5.07 us
    pallas_call x1, Pallas kernels, attention_stats(): pl.pallas_call(stats_kernel, out_shape=jax.ShapeDtypeStruct((3 * tokens,...  4.86 us
    ppermute x13, waiting for transfers between devices, flip(): return lax.ppermute(block, 'seq', [(i, i ^ bits) for i in range(devices)])  4.53 us
  transfers between devices with their start and end apart: 20, of which 9 were waited for; matrix products, arithmetic and copies ran while one was open for 0% of the time, Pallas kernels for 31%

profile of v4, /device:TPU:1, one launch (start us, length us, event | category | flops | bytes accessed | tf_op | source)
XLA Modules:
  0.0 72.9 jit_solution(3058206153948797903)
XLA Ops:
  0.6 1.7 %shard_map.163 = (bf16[16,5248]{1,0:T(8,128)(2,1)S(1)}, bf16[16,5248]{1,0:T(8,128)(2,1)S(1)}, bf16[32,4224]{1,0:T(8,128)(2,1)S(1)}) custom-call(s32[1,16]{1,0:T(1,128)} %bitcast.22, s32[1,16]{1,0:T(1,128)} %bitcast.24, bf16[1,16]{1,0:T(2,128)(2,1)} %bitcast.26, bf16[16,4096]{1,0:T(8,128)(2,1)} %input_ref.1, bf16[16,4096]{1,0:T(8,128)(2,1)} %grad_ref.1, ...), custom_call_target="tpu_custom_call" | custom-call | tf_op jit(solution)/shard_map/pallas_call | solution.py:413
  2.3 4.2 %collective-permute-start = (bf16[16,5248]{1,0:T(8,128)(2,1)S(1)}, bf16[16,5248]{1,0:T(8,128)(2,1)S(1)}, u32[]{:S(2)}, u32[]{:S(2)}) collective-permute-start(bf16[16,5248]{1,0:T(8,128)(2,1)S(1)} %get-tuple-element.52), channel_id=1, source_target_pairs={{0,12},{1,13},{2,14},{3,15},{4,8},{5,9},{6,10},{7,11},{8,4},{9,5},... | collective-permute-start | bytes 503816 | tf_op jit(solution)/shard_map/ppermute | solution.py:408
  6.5 4.0 %collective-permute-start.2 = (bf16[32,4224]{1,0:T(8,128)(2,1)S(1)}, bf16[32,4224]{1,0:T(8,128)(2,1)S(1)}, u32[]{:S(2)}, u32[]{:S(2)}) collective-permute-start(bf16[32,4224]{1,0:T(8,128)(2,1)S(1)} %get-tuple-element.53.own_ref), channel_id=1, source_target_pairs={{1,2},{3,4},{5,6},{7,8},{9,10},{11,12},{13,14},{2,1},{4,3},{6,5},{... | collective-permute-start | bytes 811016 | tf_op jit(solution)/shard_map/ppermute | solution.py:322
  10.6 4.0 %shard_map.164 = (bf16[4096,1024]{1,0:T(8,128)(2,1)S(1)}, bf16[128,2,4096]{2,1,0:T(2,128)(2,1)S(1)}) custom-call(bf16[4096,1024]{1,0:T(8,128)(2,1)} %refs_0_.1, bf16[128,2,4096]{2,1,0:T(2,128)(2,1)} %refs_1_.1), custom_call_target="tpu_custom_call" | custom-call | bytes 10485760 | tf_op jit(solution)/shard_map/pallas_call | solution.py:371
  14.6 2.1 %collective-permute-done.2.near_ref = bf16[32,4224]{1,0:T(8,128)(2,1)S(1)} collective-permute-done((bf16[32,4224]{1,0:T(8,128)(2,1)S(1)}, bf16[32,4224]{1,0:T(8,128)(2,1)S(1)}, u32[]{:S(2)}, u32[]{:S(2)}) %collective-permute-start.2) | collective-permute-done | bytes 270368 | tf_op jit(solution)/shard_map/ppermute | solution.py:322
  16.8 1.1 %collective-permute-start.6 = (bf16[32,5248]{1,0:T(8,128)(2,1)S(1)}, bf16[32,5248]{1,0:T(8,128)(2,1)S(1)}, u32[]{:S(2)}, u32[]{:S(2)}) collective-permute-start(bf16[32,5248]{1,0:T(8,128)(2,1)S(1)} %pad_maximum_fusion), channel_id=1, source_target_pairs={{0,6},{1,7},{2,4},{3,5},{4,2},{5,3},{6,0},{7,1},{8,14},{9,15},{10,... | collective-permute-start | bytes 1007624 | tf_op jit(solution)/shard_map/ppermute | solution.py:408
  17.9 1.5 %collective-permute-start.3 = (bf16[32,5248]{1,0:T(8,128)(2,1)S(1)}, bf16[32,5248]{1,0:T(8,128)(2,1)S(1)}, u32[]{:S(2)}, u32[]{:S(2)}) collective-permute-start(bf16[32,5248]{1,0:T(8,128)(2,1)S(1)} %pad_maximum_fusion), channel_id=1, source_target_pairs={{0,2},{1,3},{2,0},{3,1},{4,6},{5,7},{6,4},{7,5},{8,10},{9,11},{10,... | collective-permute-start | bytes 1007624 | tf_op jit(solution)/shard_map/ppermute | solution.py:408
  19.4 4.9 %shard_map.165.st_ref = f32[48,128]{1,0:T(8,128)S(1)} custom-call(bf16[32,4224]{1,0:T(8,128)(2,1)S(1)} %get-tuple-element.53.own_ref, bf16[32,4224]{1,0:T(8,128)(2,1)S(1)} %collective-permute-done.1.sib_ref, bf16[32,4224]{1,0:T(8,128)(2,1)S(1)} %collective-permute-done.2.near_ref, s32[1,128]{1,0:T(1,128)} %bitcast.28, ...), custom_call_target="tpu_custom_call" | custom-call | flops 1000000000 | bytes 16000000 | tf_op jit(solution)/shard_map/pallas_call | solution.py:327
  24.3 1.8 %collective-permute-start.5 = (f32[48,128]{1,0:T(8,128)S(1)}, f32[48,128]{1,0:T(8,128)S(1)}, u32[]{:S(2)}, u32[]{:S(2)}) collective-permute-start(f32[48,128]{1,0:T(8,128)S(1)} %shard_map.165.st_ref), channel_id=1, source_target_pairs={{0,1},{1,0},{2,3},{3,2},{4,5},{5,4},{6,7},{7,6},{8,9},{9,8},{10,11... | collective-permute-start | bytes 73736 | tf_op jit(solution)/shard_map/ppermute | solution.py:317
  26.1 0.8 %collective-permute-done.5.st_sib_ref = f32[48,128]{1,0:T(8,128)S(1)} collective-permute-done((f32[48,128]{1,0:T(8,128)S(1)}, f32[48,128]{1,0:T(8,128)S(1)}, u32[]{:S(2)}, u32[]{:S(2)}) %collective-permute-start.5) | collective-permute-done | bytes 24608 | tf_op jit(solution)/shard_map/ppermute | solution.py:317
  26.9 4.1 %collective-permute-start.7 = (f32[96,128]{1,0:T(8,128)S(1)}, f32[96,128]{1,0:T(8,128)S(1)}, u32[]{:S(2)}, u32[]{:S(2)}) collective-permute-start(f32[96,128]{1,0:T(8,128)S(1)} %pad_maximum_fusion.1), channel_id=1, source_target_pairs={{1,2},{3,4},{5,6},{7,8},{9,10},{11,12},{13,14},{2,1},{4,3},{6,5},{... | collective-permute-start | bytes 147464 | tf_op jit(solution)/shard_map/ppermute | solution.py:322
  31.0 2.9 %collective-permute-done.7.met_ref = f32[96,128]{1,0:T(8,128)S(1)} collective-permute-done((f32[96,128]{1,0:T(8,128)S(1)}, f32[96,128]{1,0:T(8,128)S(1)}, u32[]{:S(2)}, u32[]{:S(2)}) %collective-permute-start.7) | collective-permute-done | bytes 49184 | tf_op jit(solution)/shard_map/ppermute | solution.py:322
  33.9 0.5 collective-permute-start.9
  34.4 0.7 collective-permute-done.8.sib_met_ref
  35.1 0.2 collective-permute-start.12
  35.3 0.4 collective-permute-start.10
  35.8 1.0 %collective-permute-done.12 = bf16[32,5248]{1,0:T(8,128)(2,1)S(1)} collective-permute-done((bf16[32,5248]{1,0:T(8,128)(2,1)S(1)}, bf16[32,5248]{1,0:T(8,128)(2,1)S(1)}, u32[]{:S(2)}, u32[]{:S(2)}) %collective-permute-start.12) | collective-permute-done | bytes 335904 | tf_op jit(solution)/shard_map/ppermute | solution.py:408
  36.8 0.5 collective-permute-done.10
  37.3 0.5 collective-permute-done.11
  37.8 9.1 %shard_map.166 = (bf16[160,4096]{1,0:T(8,128)(2,1)S(1)}, bf16[160,4096]{1,0:T(8,128)(2,1)S(1)}, bf16[160,1024]{1,0:T(8,128)(2,1)S(1)}, bf16[160,1024]{1,0:T(8,12...) custom-call(bf16[1,32,5248]{2,1,0:T(8,128)(2,1)S(1)} %bitcast.14, ...), custom_call_target="tpu_custom_call" | custom-call | flops 4026531840 | bytes 16777216 | tf_op jit(solution)/shard_map/pallas_call | solution.py:453
  46.9 0.2 collective-permute-start.13
  47.1 2.0 %collective-permute-done.13.got_ref = bf16[4,16,5248]{2,1,0:T(8,128)(2,1)S(1)} collective-permute-done((bf16[4,16,5248]{2,1,0:T(8,128)(2,1)S(1)}, bf16[4,16,5248]{2,1,0:T(8,128)(2,1)S(1)}, u32[]{:S(2)}, u32[]{:S(2)}) %collective-permute-start.13) | collective-permute-done | bytes 671776 | tf_op jit(solution)/shard_map/ppermute | solution.py:408
  49.2 1.8 %collective-permute-start.14 = (bf16[16,5248]{1,0:T(8,128)(2,1)S(1)}, bf16[16,5248]{1,0:T(8,128)(2,1)S(1)}, u32[]{:S(2)}, u32[]{:S(2)}) collective-permute-start(bf16[16,5248]{1,0:T(8,128)(2,1)S(1)} %get-tuple-element.73), channel_id=1, source_target_pairs={{0,2},{1,3},{2,0},{3,1},{4,6},{5,7},{6,4},{7,5},{8,10},{9,11},{10,... | collective-permute-start | bytes 503816 | tf_op jit(solution)/shard_map/ppermute | solution.py:408
  51.0 0.7 collective-permute-start.15
  51.7 0.5 collective-permute-start.16
  52.3 7.0 %shard_map.168 = (f32[16,4096]{1,0:T(8,128)S(1)}, bf16[16,4096]{1,0:T(8,128)(2,1)S(1)}, bf16[16,4096]{1,0:T(8,128)(2,1)S(1)}, bf16[128,2,4096]{2,1,0:T(2,128)(2,1)}) custom-call(bf16[32,4224]{1,0:T(8,128)(2,1)S(1)} %get-tuple-element.53.own_ref, bf16[32,4224]{1,0:T(8,128)(2,1)S(1)} %collective-permute-done.1.sib_ref, ...), custom_call_target="tpu_custom_call" | custom-call | flops 1000000000 | bytes 32000000 | tf_op jit(solution)/shard_map/pallas_call | solution.py:338
  59.3 0.6 collective-permute-done.16.refs_3_
  60.0 0.8 %collective-permute-start.17 = (bf16[8,5248]{1,0:T(8,128)(2,1)S(1)}, bf16[8,5248]{1,0:T(8,128)(2,1)S(1)}, u32[]{:S(2)}, u32[]{:S(2)}) collective-permute-start(bf16[8,5248]{1,0:T(8,128)(2,1)S(1)} %get-tuple-element.77), channel_id=1, source_target_pairs={{0,12},{1,13},{2,14},{3,15},{4,8},{5,9},{6,10},{7,11},{8,4},{9,5},... | collective-permute-start | bytes 251912 | tf_op jit(solution)/shard_map/ppermute | solution.py:408
  60.8 1.5 %collective-permute-start.18 = (bf16[16,4096]{1,0:T(8,128)(2,1)S(1)}, bf16[16,4096]{1,0:T(8,128)(2,1)S(1)}, u32[]{:S(2)}, u32[]{:S(2)}) collective-permute-start(bf16[16,4096]{1,0:T(8,128)(2,1)S(1)} %get-tuple-element.80), channel_id=1, source_target_pairs={{0,1},{1,0},{2,3},{3,2},{4,5},{5,4},{6,7},{7,6},{8,9},{9,8},{10,11... | collective-permute-start | bytes 393224 | tf_op jit(solution)/shard_map/ppermute | solution.py:317
  62.2 2.6 %collective-permute-start.19 = (bf16[16,4096]{1,0:T(8,128)(2,1)S(1)}, bf16[16,4096]{1,0:T(8,128)(2,1)S(1)}, u32[]{:S(2)}, u32[]{:S(2)}) collective-permute-start(bf16[16,4096]{1,0:T(8,128)(2,1)S(1)} %get-tuple-element.81), channel_id=1, source_target_pairs={{1,2},{3,4},{5,6},{7,8},{9,10},{11,12},{13,14},{2,1},{4,3},{6,5},{... | collective-permute-start | bytes 393224 | tf_op jit(solution)/shard_map/ppermute | solution.py:322
  64.8 6.9 %shard_map.171 = (bf16[4096,1024]{1,0:T(8,128)(2,1)}, bf16[1024,4096]{1,0:T(8,128)(2,1)}) custom-call(bf16[160,4096]{1,0:T(8,128)(2,1)S(1)} %get-tuple-element.90.x_ref, bf16[160,1024]{1,0:T(8,128)(2,1)S(1)} %get-tuple-element.91.hidden_ref, bf16[160,1024]{1,0:T(8,128)(2,1)S(1)} %get-tuple-element.92.scaled_ref, bf16[160,4096]{1,0:T(8,128)(2,1)S(1)} %get-tuple-element.93.g_ref), custom_call_target="tpu_custom_call" | custom-call | flops 2684354560 | bytes 16777216 | tf_op jit(solution)/shard_map/pallas_call | solution.py:497
  71.8 1.1 %shard_map.170 = (bf16[16,4096]{1,0:T(8,128)(2,1)}, f32[1,16]{1,0:T(1,128)}, bf16[16,4096]{1,0:T(8,128)(2,1)}) custom-call(s32[1,16]{1,0:T(1,128)S(1)} %bitcast.23, s32[1,16]{1,0:T(1,128)S(1)} %bitcast.25, f32[16,5248]{1,0:T(8,128)S(1)} %get-tuple-element.76.own_ref, bf16[8,5248]{1,0:T(8,128)(2,1)S(1)} %collective-permute-done.17.got_ref, ...), custom_call_target="tpu_custom_call" | custom-call | tf_op jit(solution)/shard_map/pallas_call | solution.py:518
  (23 shorter events, 0.6 us)
Async XLA Ops:
  2.3 12.3 %collective-permute-start = (bf16[16,5248]{1,0:T(8,128)(2,1)S(1)}, bf16[16,5248]{1,0:T(8,128)(2,1)S(1)}, u32[]{:S(2)}, u32[]{:S(2)}) collective-permute-start(bf16[16,5248]{1,0:T(8,128)(2,1)S(1)} %get-tuple-element.52), channel_id=1, source_target_pairs={{0,12},{1,13},{2,14},{3,15},{4,8},{5,9},{6,10},{7,11},{8,4},{9,5},... | collective-permute-start | bytes 503816 | tf_op jit(solution)/shard_map/ppermute | solution.py:408
  6.5 10.3 %collective-permute-start.2 = (bf16[32,4224]{1,0:T(8,128)(2,1)S(1)}, bf16[32,4224]{1,0:T(8,128)(2,1)S(1)}, u32[]{:S(2)}, u32[]{:S(2)}) collective-permute-start(bf16[32,4224]{1,0:T(8,128)(2,1)S(1)} %get-tuple-element.53.own_ref), channel_id=1, source_target_pairs={{1,2},{3,4},{5,6},{7,8},{9,10},{11,12},{13,14},{2,1},{4,3},{6,5},{... | collective-permute-start | bytes 811016 | tf_op jit(solution)/shard_map/ppermute | solution.py:322
  10.5 6.3 %collective-permute-start.1 = (bf16[32,4224]{1,0:T(8,128)(2,1)S(1)}, bf16[32,4224]{1,0:T(8,128)(2,1)S(1)}, u32[]{:S(2)}, u32[]{:S(2)}) collective-permute-start(bf16[32,4224]{1,0:T(8,128)(2,1)S(1)} %get-tuple-element.53.own_ref), channel_id=1, source_target_pairs={{0,1},{1,0},{2,3},{3,2},{4,5},{5,4},{6,7},{7,6},{8,9},{9,8},{10,11... | collective-permute-start | bytes 811016 | tf_op jit(solution)/shard_map/ppermute | solution.py:317
  16.8 18.4 %collective-permute-start.6 = (bf16[32,5248]{1,0:T(8,128)(2,1)S(1)}, bf16[32,5248]{1,0:T(8,128)(2,1)S(1)}, u32[]{:S(2)}, u32[]{:S(2)}) collective-permute-start(bf16[32,5248]{1,0:T(8,128)(2,1)S(1)} %pad_maximum_fusion), channel_id=1, source_target_pairs={{0,6},{1,7},{2,4},{3,5},{4,2},{5,3},{6,0},{7,1},{8,14},{9,15},{10,... | collective-permute-start | bytes 1007624 | tf_op jit(solution)/shard_map/ppermute | solution.py:408
  17.9 17.4 %collective-permute-start.4 = (bf16[32,5248]{1,0:T(8,128)(2,1)S(1)}, bf16[32,5248]{1,0:T(8,128)(2,1)S(1)}, u32[]{:S(2)}, u32[]{:S(2)}) collective-permute-start(bf16[32,5248]{1,0:T(8,128)(2,1)S(1)} %pad_maximum_fusion), channel_id=1, source_target_pairs={{0,4},{1,5},{2,6},{3,7},{4,0},{5,1},{6,2},{7,3},{8,12},{9,13},{10,... | collective-permute-start | bytes 1007624 | tf_op jit(solution)/shard_map/ppermute | solution.py:408
  17.9 17.4 %collective-permute-start.3 = (bf16[32,5248]{1,0:T(8,128)(2,1)S(1)}, bf16[32,5248]{1,0:T(8,128)(2,1)S(1)}, u32[]{:S(2)}, u32[]{:S(2)}) collective-permute-start(bf16[32,5248]{1,0:T(8,128)(2,1)S(1)} %pad_maximum_fusion), channel_id=1, source_target_pairs={{0,2},{1,3},{2,0},{3,1},{4,6},{5,7},{6,4},{7,5},{8,10},{9,11},{10,... | collective-permute-start | bytes 1007624 | tf_op jit(solution)/shard_map/ppermute | solution.py:408
  24.3 2.6 %collective-permute-start.5 = (f32[48,128]{1,0:T(8,128)S(1)}, f32[48,128]{1,0:T(8,128)S(1)}, u32[]{:S(2)}, u32[]{:S(2)}) collective-permute-start(f32[48,128]{1,0:T(8,128)S(1)} %shard_map.165.st_ref), channel_id=1, source_target_pairs={{0,1},{1,0},{2,3},{3,2},{4,5},{5,4},{6,7},{7,6},{8,9},{9,8},{10,11... | collective-permute-start | bytes 73736 | tf_op jit(solution)/shard_map/ppermute | solution.py:317
  26.9 7.0 %collective-permute-start.7 = (f32[96,128]{1,0:T(8,128)S(1)}, f32[96,128]{1,0:T(8,128)S(1)}, u32[]{:S(2)}, u32[]{:S(2)}) collective-permute-start(f32[96,128]{1,0:T(8,128)S(1)} %pad_maximum_fusion.1), channel_id=1, source_target_pairs={{1,2},{3,4},{5,6},{7,8},{9,10},{11,12},{13,14},{2,1},{4,3},{6,5},{... | collective-permute-start | bytes 147464 | tf_op jit(solution)/shard_map/ppermute | solution.py:322
  33.9 1.2 %collective-permute-start.8 = (f32[96,128]{1,0:T(8,128)S(1)}, f32[96,128]{1,0:T(8,128)S(1)}, u32[]{:S(2)}, u32[]{:S(2)}) collective-permute-start(f32[96,128]{1,0:T(8,128)S(1)} %collective-permute-done.7.met_ref), channel_id=1, source_target_pairs={{0,1},{1,0},{2,3},{3,2},{4,5},{5,4},{6,7},{7,6},{8,9},{9,8},{10,11... | collective-permute-start | bytes 147464 | tf_op jit(solution)/shard_map/ppermute | solution.py:317
  33.9 1.9 %collective-permute-start.9 = (bf16[32,5248]{1,0:T(8,128)(2,1)S(1)}, bf16[32,5248]{1,0:T(8,128)(2,1)S(1)}, u32[]{:S(2)}, u32[]{:S(2)}) collective-permute-start(bf16[32,5248]{1,0:T(8,128)(2,1)S(1)} %pad_maximum_fusion), channel_id=1, source_target_pairs={{0,1},{1,0},{2,3},{3,2},{4,5},{5,4},{6,7},{7,6},{8,9},{9,8},{10,11... | collective-permute-start | bytes 1007624 | tf_op jit(solution)/shard_map/ppermute | solution.py:408
  35.1 1.6 %collective-permute-start.12 = (bf16[32,5248]{1,0:T(8,128)(2,1)S(1)}, bf16[32,5248]{1,0:T(8,128)(2,1)S(1)}, u32[]{:S(2)}, u32[]{:S(2)}) collective-permute-start(bf16[32,5248]{1,0:T(8,128)(2,1)S(1)} %collective-permute-done.6), channel_id=1, source_target_pairs={{0,1},{1,0},{2,3},{3,2},{4,5},{5,4},{6,7},{7,6},{8,9},{9,8},{10,11... | collective-permute-start | bytes 1007624 | tf_op jit(solution)/shard_map/ppermute | solution.py:408
  35.3 2.0 %collective-permute-start.10 = (bf16[32,5248]{1,0:T(8,128)(2,1)S(1)}, bf16[32,5248]{1,0:T(8,128)(2,1)S(1)}, u32[]{:S(2)}, u32[]{:S(2)}) collective-permute-start(bf16[32,5248]{1,0:T(8,128)(2,1)S(1)} %collective-permute-done.3), channel_id=1, source_target_pairs={{0,1},{1,0},{2,3},{3,2},{4,5},{5,4},{6,7},{7,6},{8,9},{9,8},{10,11... | collective-permute-start | bytes 1007624 | tf_op jit(solution)/shard_map/ppermute | solution.py:408
  35.7 2.1 %collective-permute-start.11 = (bf16[32,5248]{1,0:T(8,128)(2,1)S(1)}, bf16[32,5248]{1,0:T(8,128)(2,1)S(1)}, u32[]{:S(2)}, u32[]{:S(2)}) collective-permute-start(bf16[32,5248]{1,0:T(8,128)(2,1)S(1)} %collective-permute-done.4), channel_id=1, source_target_pairs={{0,1},{1,0},{2,3},{3,2},{4,5},{5,4},{6,7},{7,6},{8,9},{9,8},{10,11... | collective-permute-start | bytes 1007624 | tf_op jit(solution)/shard_map/ppermute | solution.py:408
  46.8 24.9 %copy-start = (s32[16]{0:T(128)S(1)}, s32[16]{0:T(128)}, u32[]{:S(2)}) copy-start(s32[16]{0:T(128)} %param.20) | copy-start | bytes 196
  46.9 24.9 %copy-start.1 = (s32[16]{0:T(128)S(1)}, s32[16]{0:T(128)}, u32[]{:S(2)}) copy-start(s32[16]{0:T(128)} %param.21) | copy-start | bytes 196
  46.9 2.2 %collective-permute-start.13 = (bf16[4,16,5248]{2,1,0:T(8,128)(2,1)S(1)}, bf16[4,16,5248]{2,1,0:T(8,128)(2,1)S(1)}, u32[]{:S(2)}, u32[]{:S(2)}) collective-permute-start(bf16[4,16,5248]{2,1,0:T(8,128)(2,1)S(1)} %get-tuple-element.61), channel_id=1, source_target_pairs={{0,1},{1,0},{2,3},{3,2},{4,5},{5,4},{6,7},{7,6},{8,9},{9,8},{10,11... | collective-permute-start | bytes 2015240 | tf_op jit(solution)/shard_map/ppermute | solution.py:408
  49.2 10.1 %collective-permute-start.14 = (bf16[16,5248]{1,0:T(8,128)(2,1)S(1)}, bf16[16,5248]{1,0:T(8,128)(2,1)S(1)}, u32[]{:S(2)}, u32[]{:S(2)}) collective-permute-start(bf16[16,5248]{1,0:T(8,128)(2,1)S(1)} %get-tuple-element.73), channel_id=1, source_target_pairs={{0,2},{1,3},{2,0},{3,1},{4,6},{5,7},{6,4},{7,5},{8,10},{9,11},{10,... | collective-permute-start | bytes 503816 | tf_op jit(solution)/shard_map/ppermute | solution.py:408
  51.0 8.3 %collective-permute-start.15 = (bf16[16,5248]{1,0:T(8,128)(2,1)S(1)}, bf16[16,5248]{1,0:T(8,128)(2,1)S(1)}, u32[]{:S(2)}, u32[]{:S(2)}) collective-permute-start(bf16[16,5248]{1,0:T(8,128)(2,1)S(1)} %get-tuple-element.74), channel_id=1, source_target_pairs={{0,4},{1,5},{2,6},{3,7},{4,0},{5,1},{6,2},{7,3},{8,12},{9,13},{10,... | collective-permute-start | bytes 503816 | tf_op jit(solution)/shard_map/ppermute | solution.py:408
  51.7 8.2 %collective-permute-start.16 = (bf16[16,5248]{1,0:T(8,128)(2,1)S(1)}, bf16[16,5248]{1,0:T(8,128)(2,1)S(1)}, u32[]{:S(2)}, u32[]{:S(2)}) collective-permute-start(bf16[16,5248]{1,0:T(8,128)(2,1)S(1)} %get-tuple-element.75), channel_id=1, source_target_pairs={{0,6},{1,7},{2,4},{3,5},{4,2},{5,3},{6,0},{7,1},{8,14},{9,15},{10,... | collective-permute-start | bytes 503816 | tf_op jit(solution)/shard_map/ppermute | solution.py:408
  60.0 11.8 %collective-permute-start.17 = (bf16[8,5248]{1,0:T(8,128)(2,1)S(1)}, bf16[8,5248]{1,0:T(8,128)(2,1)S(1)}, u32[]{:S(2)}, u32[]{:S(2)}) collective-permute-start(bf16[8,5248]{1,0:T(8,128)(2,1)S(1)} %get-tuple-element.77), channel_id=1, source_target_pairs={{0,12},{1,13},{2,14},{3,15},{4,8},{5,9},{6,10},{7,11},{8,4},{9,5},... | collective-permute-start | bytes 251912 | tf_op jit(solution)/shard_map/ppermute | solution.py:408
  60.8 11.0 %collective-permute-start.18 = (bf16[16,4096]{1,0:T(8,128)(2,1)S(1)}, bf16[16,4096]{1,0:T(8,128)(2,1)S(1)}, u32[]{:S(2)}, u32[]{:S(2)}) collective-permute-start(bf16[16,4096]{1,0:T(8,128)(2,1)S(1)} %get-tuple-element.80), channel_id=1, source_target_pairs={{0,1},{1,0},{2,3},{3,2},{4,5},{5,4},{6,7},{7,6},{8,9},{9,8},{10,11... | collective-permute-start | bytes 393224 | tf_op jit(solution)/shard_map/ppermute | solution.py:317
  62.2 9.5 %collective-permute-start.19 = (bf16[16,4096]{1,0:T(8,128)(2,1)S(1)}, bf16[16,4096]{1,0:T(8,128)(2,1)S(1)}, u32[]{:S(2)}, u32[]{:S(2)}) collective-permute-start(bf16[16,4096]{1,0:T(8,128)(2,1)S(1)} %get-tuple-element.81), channel_id=1, source_target_pairs={{1,2},{3,4},{5,6},{7,8},{9,10},{11,12},{13,14},{2,1},{4,3},{6,5},{... | collective-permute-start | bytes 393224 | tf_op jit(solution)/shard_map/ppermute | solution.py:322

commit v5 on v4

--- a/solution.py
+++ b/solution.py
@@ -434,8 +434,10 @@
         pair = after(pair, held[1], held[2], near_kv)
         near = [pair, flip(pair, 2), flip(pair, 4), flip(pair, 6)]
         beside = flip(pair, 1)
-        near[1:3] = after(near[1:3], stats_sib)
-        near[3], all_stats = lax.optimization_barrier((near[3], all_stats))
+        near[2:] = after(near[2:], stats_sib)
+        near[1], met = lax.optimization_barrier((near[1], met))
+        all_stats = (stats, stats_sib, met, core(met))
+        beside, all_stats = lax.optimization_barrier((beside, all_stats))
         blocks = [b[None] for b in near + [beside] + [flip(b, 1) for b in near[1:]]]
     else:
         halves = [list(range(e * shards, (e + 1) * shards)) for e in range(EXPERTS)]

time: 73.1 us -> 71 us (0.971)
  waiting for transfers between devices: 11.2 us -> 7.69 us
  starting transfers between devices: 26 us -> 27.3 us
    ppermute x3, waiting for transfers between devices: 5.07 us -> 2.26 us  [cross(): return lax.ppermute(block, 'seq', crossing + [(j, i) for i, j in crossing])]
    ppermute x13, waiting for transfers between devices: 4.53 us -> 2.91 us  [flip(): return lax.ppermute(block, 'seq', [(i, i ^ bits) for i in range(devices)])]
    ppermute x13, starting transfers between devices: 12.1 us -> 13.3 us  [flip(): return lax.ppermute(block, 'seq', [(i, i ^ bits) for i in range(devices)])]
    ppermute x4, waiting for transfers between devices: 1.57 us -> 2.52 us  [core(): lax.ppermute(block, 'seq', [(i, i ^ 1) for i in range(lax.axis_size('seq'...]
  transfers between devices with their start and end apart: 20 -> 20, of which waited for: 9 -> 7; matrix products, arithmetic and copies ran while one was open for 0% -> 0% of each run, Pallas kernels for 31% -> 32%
where the time goes in v5:
time: 71 us; the launch traced here: 70.8 us
  Pallas kernels  34.9 us (49%)
  starting transfers between devices  27.3 us (38%)
  waiting for transfers between devices  7.69 us (11%)
  between operations  0.78 us (1%)
    ppermute x13, starting transfers between devices, flip(): return lax.ppermute(block, 'seq', [(i, i ^ bits) for i in range(devices)])  13.3 us
    ppermute x3, starting transfers between devices, cross(): return lax.ppermute(block, 'seq', crossing + [(j, i) for i, j in crossing])  10.6 us
    pallas_call x1, Pallas kernels, local(): pl.pallas_call(functools.partial(main_kernel, places), out_shape=[slots,...  9.08 us
    pallas_call x1, Pallas kernels, attention_grads(): pl.pallas_call(grads_kernel, out_shape=(jax.ShapeDtypeStruct((tokens, D),...  7.01 us
    pallas_call x1, Pallas kernels, local(): pl.pallas_call(weights_kernel, grid=(pieces,), in_specs=[pl.BlockSpec((ro...  6.92 us
    pallas_call x1, Pallas kernels, attention_stats(): pl.pallas_call(stats_kernel, out_shape=jax.ShapeDtypeStruct((3 * tokens,...  4.88 us
    pallas_call x1, Pallas kernels, fetch(): pl.pallas_call(functools.partial(fetch_kernel, len(arrays)), in_specs=[pl...  4 us
    ppermute x4, starting transfers between devices, core(): lax.ppermute(block, 'seq', [(i, i ^ 1) for i in range(lax.axis_size('seq'...  3.42 us
  transfers between devices with their start and end apart: 20, of which 7 were waited for; matrix products, arithmetic and copies ran while one was open for 0% of the time, Pallas kernels for 32%

profile of v5, /device:TPU:1, one launch (start us, length us, event | category | flops | bytes accessed | tf_op | source)
XLA Modules:
  0.0 70.8 jit_solution(3129463069199417903)
XLA Ops:
  0.6 1.7 %shard_map.163 = (bf16[16,5248]{1,0:T(8,128)(2,1)S(1)}, bf16[16,5248]{1,0:T(8,128)(2,1)S(1)}, bf16[32,4224]{1,0:T(8,128)(2,1)S(1)}) custom-call(s32[1,16]{1,0:T(1,128)} %bitcast.22, s32[1,16]{1,0:T(1,128)} %bitcast.24, bf16[1,16]{1,0:T(2,128)(2,1)} %bitcast.26, bf16[16,4096]{1,0:T(8,128)(2,1)} %input_ref.1, bf16[16,4096]{1,0:T(8,128)(2,1)} %grad_ref.1, ...), custom_call_target="tpu_custom_call" | custom-call | tf_op jit(solution)/shard_map/pallas_call | solution.py:413
  2.3 4.2 %collective-permute-start = (bf16[16,5248]{1,0:T(8,128)(2,1)S(1)}, bf16[16,5248]{1,0:T(8,128)(2,1)S(1)}, u32[]{:S(2)}, u32[]{:S(2)}) collective-permute-start(bf16[16,5248]{1,0:T(8,128)(2,1)S(1)} %get-tuple-element.54), channel_id=1, source_target_pairs={{0,12},{1,13},{2,14},{3,15},{4,8},{5,9},{6,10},{7,11},{8,4},{9,5},... | collective-permute-start | bytes 503816 | tf_op jit(solution)/shard_map/ppermute | solution.py:408
  6.5 4.0 %collective-permute-start.2 = (bf16[32,4224]{1,0:T(8,128)(2,1)S(1)}, bf16[32,4224]{1,0:T(8,128)(2,1)S(1)}, u32[]{:S(2)}, u32[]{:S(2)}) collective-permute-start(bf16[32,4224]{1,0:T(8,128)(2,1)S(1)} %get-tuple-element.55.own_ref), channel_id=1, source_target_pairs={{1,2},{3,4},{5,6},{7,8},{9,10},{11,12},{13,14},{2,1},{4,3},{6,5},{... | collective-permute-start | bytes 811016 | tf_op jit(solution)/shard_map/ppermute | solution.py:322
  10.6 4.0 %shard_map.164 = (bf16[4096,1024]{1,0:T(8,128)(2,1)S(1)}, bf16[128,2,4096]{2,1,0:T(2,128)(2,1)S(1)}) custom-call(bf16[4096,1024]{1,0:T(8,128)(2,1)} %refs_0_.1, bf16[128,2,4096]{2,1,0:T(2,128)(2,1)} %refs_1_.1), custom_call_target="tpu_custom_call" | custom-call | bytes 10485760 | tf_op jit(solution)/shard_map/pallas_call | solution.py:371
  14.6 2.1 %collective-permute-done.2.near_ref = bf16[32,4224]{1,0:T(8,128)(2,1)S(1)} collective-permute-done((bf16[32,4224]{1,0:T(8,128)(2,1)S(1)}, bf16[32,4224]{1,0:T(8,128)(2,1)S(1)}, u32[]{:S(2)}, u32[]{:S(2)}) %collective-permute-start.2) | collective-permute-done | bytes 270368 | tf_op jit(solution)/shard_map/ppermute | solution.py:322
  16.8 1.1 %collective-permute-start.7 = (bf16[32,5248]{1,0:T(8,128)(2,1)S(1)}, bf16[32,5248]{1,0:T(8,128)(2,1)S(1)}, u32[]{:S(2)}, u32[]{:S(2)}) collective-permute-start(bf16[32,5248]{1,0:T(8,128)(2,1)S(1)} %pad_maximum_fusion), channel_id=1, source_target_pairs={{0,6},{1,7},{2,4},{3,5},{4,2},{5,3},{6,0},{7,1},{8,14},{9,15},{10,... | collective-permute-start | bytes 1007624 | tf_op jit(solution)/shard_map/ppermute | solution.py:408
  17.9 1.5 %collective-permute-start.3 = (bf16[32,5248]{1,0:T(8,128)(2,1)S(1)}, bf16[32,5248]{1,0:T(8,128)(2,1)S(1)}, u32[]{:S(2)}, u32[]{:S(2)}) collective-permute-start(bf16[32,5248]{1,0:T(8,128)(2,1)S(1)} %pad_maximum_fusion), channel_id=1, source_target_pairs={{0,2},{1,3},{2,0},{3,1},{4,6},{5,7},{6,4},{7,5},{8,10},{9,11},{10,... | collective-permute-start | bytes 1007624 | tf_op jit(solution)/shard_map/ppermute | solution.py:408
  19.4 4.9 %shard_map.165.st_ref = f32[48,128]{1,0:T(8,128)S(1)} custom-call(bf16[32,4224]{1,0:T(8,128)(2,1)S(1)} %get-tuple-element.55.own_ref, bf16[32,4224]{1,0:T(8,128)(2,1)S(1)} %collective-permute-done.1.sib_ref, bf16[32,4224]{1,0:T(8,128)(2,1)S(1)} %collective-permute-done.2.near_ref, s32[1,128]{1,0:T(1,128)} %bitcast.28, ...), custom_call_target="tpu_custom_call" | custom-call | flops 1000000000 | bytes 16000000 | tf_op jit(solution)/shard_map/pallas_call | solution.py:327
  24.3 1.8 %collective-permute-start.4 = (f32[48,128]{1,0:T(8,128)S(1)}, f32[48,128]{1,0:T(8,128)S(1)}, u32[]{:S(2)}, u32[]{:S(2)}) collective-permute-start(f32[48,128]{1,0:T(8,128)S(1)} %shard_map.165.st_ref), channel_id=1, source_target_pairs={{0,1},{1,0},{2,3},{3,2},{4,5},{5,4},{6,7},{7,6},{8,9},{9,8},{10,11... | collective-permute-start | bytes 73736 | tf_op jit(solution)/shard_map/ppermute | solution.py:317
  26.1 0.8 %collective-permute-done.4.st_sib_ref = f32[48,128]{1,0:T(8,128)S(1)} collective-permute-done((f32[48,128]{1,0:T(8,128)S(1)}, f32[48,128]{1,0:T(8,128)S(1)}, u32[]{:S(2)}, u32[]{:S(2)}) %collective-permute-start.4) | collective-permute-done | bytes 24608 | tf_op jit(solution)/shard_map/ppermute | solution.py:317
  26.9 4.0 %collective-permute-start.5 = (f32[96,128]{1,0:T(8,128)S(1)}, f32[96,128]{1,0:T(8,128)S(1)}, u32[]{:S(2)}, u32[]{:S(2)}) collective-permute-start(f32[96,128]{1,0:T(8,128)S(1)} %pad_maximum_fusion.1), channel_id=1, source_target_pairs={{1,2},{3,4},{5,6},{7,8},{9,10},{11,12},{13,14},{2,1},{4,3},{6,5},{... | collective-permute-start | bytes 147464 | tf_op jit(solution)/shard_map/ppermute | solution.py:322
  31.1 0.8 %collective-permute-done.6 = bf16[32,5248]{1,0:T(8,128)(2,1)S(1)} collective-permute-done((bf16[32,5248]{1,0:T(8,128)(2,1)S(1)}, bf16[32,5248]{1,0:T(8,128)(2,1)S(1)}, u32[]{:S(2)}, u32[]{:S(2)}) %collective-permute-start.6) | collective-permute-done | bytes 335904 | tf_op jit(solution)/shard_map/ppermute | solution.py:408
  31.9 1.9 %collective-permute-start.11 = (bf16[32,5248]{1,0:T(8,128)(2,1)S(1)}, bf16[32,5248]{1,0:T(8,128)(2,1)S(1)}, u32[]{:S(2)}, u32[]{:S(2)}) collective-permute-start(bf16[32,5248]{1,0:T(8,128)(2,1)S(1)} %collective-permute-done.6), channel_id=1, source_target_pairs={{0,1},{1,0},{2,3},{3,2},{4,5},{5,4},{6,7},{7,6},{8,9},{9,8},{10,11... | collective-permute-start | bytes 1007624 | tf_op jit(solution)/shard_map/ppermute | solution.py:408
  33.8 0.1 collective-permute-done.5.met_ref
  33.9 0.4 collective-permute-start.10
  34.3 0.1 collective-permute-start.9
  34.4 1.7 %collective-permute-done.9.sib_met_ref = f32[96,128]{1,0:T(8,128)S(1)} collective-permute-done((f32[96,128]{1,0:T(8,128)S(1)}, f32[96,128]{1,0:T(8,128)S(1)}, u32[]{:S(2)}, u32[]{:S(2)}) %collective-permute-start.9) | collective-permute-done | bytes 49184 | tf_op jit(solution)/shard_map/ppermute | solution.py:317
  36.1 9.1 %shard_map.166 = (bf16[160,4096]{1,0:T(8,128)(2,1)S(1)}, bf16[160,4096]{1,0:T(8,128)(2,1)S(1)}, bf16[160,1024]{1,0:T(8,128)(2,1)S(1)}, bf16[160,1024]{1,0:T(8,12...) custom-call(bf16[1,32,5248]{2,1,0:T(8,128)(2,1)S(1)} %bitcast.14, ...), custom_call_target="tpu_custom_call" | custom-call | flops 4026531840 | bytes 16777216 | tf_op jit(solution)/shard_map/pallas_call | solution.py:455
  45.2 0.4 collective-permute-start.13
  45.7 1.8 %collective-permute-done.13.got_ref = bf16[4,16,5248]{2,1,0:T(8,128)(2,1)S(1)} collective-permute-done((bf16[4,16,5248]{2,1,0:T(8,128)(2,1)S(1)}, bf16[4,16,5248]{2,1,0:T(8,128)(2,1)S(1)}, u32[]{:S(2)}, u32[]{:S(2)}) %collective-permute-start.13) | collective-permute-done | bytes 671776 | tf_op jit(solution)/shard_map/ppermute | solution.py:408
  47.4 0.1 shard_map.167
  47.6 1.3 %collective-permute-start.14 = (bf16[16,5248]{1,0:T(8,128)(2,1)S(1)}, bf16[16,5248]{1,0:T(8,128)(2,1)S(1)}, u32[]{:S(2)}, u32[]{:S(2)}) collective-permute-start(bf16[16,5248]{1,0:T(8,128)(2,1)S(1)} %get-tuple-element.77), channel_id=1, source_target_pairs={{0,2},{1,3},{2,0},{3,1},{4,6},{5,7},{6,4},{7,5},{8,10},{9,11},{10,... | collective-permute-start | bytes 503816 | tf_op jit(solution)/shard_map/ppermute | solution.py:408
  48.9 1.0 %collective-permute-start.15 = (bf16[16,5248]{1,0:T(8,128)(2,1)S(1)}, bf16[16,5248]{1,0:T(8,128)(2,1)S(1)}, u32[]{:S(2)}, u32[]{:S(2)}) collective-permute-start(bf16[16,5248]{1,0:T(8,128)(2,1)S(1)} %get-tuple-element.78), channel_id=1, source_target_pairs={{0,4},{1,5},{2,6},{3,7},{4,0},{5,1},{6,2},{7,3},{8,12},{9,13},{10,... | collective-permute-start | bytes 503816 | tf_op jit(solution)/shard_map/ppermute | solution.py:408
  49.9 0.4 collective-permute-start.16
  50.3 7.0 %shard_map.168 = (f32[16,4096]{1,0:T(8,128)S(1)}, bf16[16,4096]{1,0:T(8,128)(2,1)S(1)}, bf16[16,4096]{1,0:T(8,128)(2,1)S(1)}, bf16[128,2,4096]{2,1,0:T(2,128)(2,1)}) custom-call(bf16[32,4224]{1,0:T(8,128)(2,1)S(1)} %get-tuple-element.55.own_ref, bf16[32,4224]{1,0:T(8,128)(2,1)S(1)} %collective-permute-done.1.sib_ref, ...), custom_call_target="tpu_custom_call" | custom-call | flops 1000000000 | bytes 32000000 | tf_op jit(solution)/shard_map/pallas_call | solution.py:338
  57.3 0.3 collective-permute-done.16.refs_3_
  57.6 0.1 shard_map.169
  57.7 1.0 %collective-permute-start.17 = (bf16[8,5248]{1,0:T(8,128)(2,1)S(1)}, bf16[8,5248]{1,0:T(8,128)(2,1)S(1)}, u32[]{:S(2)}, u32[]{:S(2)}) collective-permute-start(bf16[8,5248]{1,0:T(8,128)(2,1)S(1)} %get-tuple-element.81), channel_id=1, source_target_pairs={{0,12},{1,13},{2,14},{3,15},{4,8},{5,9},{6,10},{7,11},{8,4},{9,5},... | collective-permute-start | bytes 251912 | tf_op jit(solution)/shard_map/ppermute | solution.py:408
  58.6 1.5 %collective-permute-start.18 = (bf16[16,4096]{1,0:T(8,128)(2,1)S(1)}, bf16[16,4096]{1,0:T(8,128)(2,1)S(1)}, u32[]{:S(2)}, u32[]{:S(2)}) collective-permute-start(bf16[16,4096]{1,0:T(8,128)(2,1)S(1)} %get-tuple-element.84), channel_id=1, source_target_pairs={{0,1},{1,0},{2,3},{3,2},{4,5},{5,4},{6,7},{7,6},{8,9},{9,8},{10,11... | collective-permute-start | bytes 393224 | tf_op jit(solution)/shard_map/ppermute | solution.py:317
  60.1 2.6 %collective-permute-start.19 = (bf16[16,4096]{1,0:T(8,128)(2,1)S(1)}, bf16[16,4096]{1,0:T(8,128)(2,1)S(1)}, u32[]{:S(2)}, u32[]{:S(2)}) collective-permute-start(bf16[16,4096]{1,0:T(8,128)(2,1)S(1)} %get-tuple-element.85), channel_id=1, source_target_pairs={{1,2},{3,4},{5,6},{7,8},{9,10},{11,12},{13,14},{2,1},{4,3},{6,5},{... | collective-permute-start | bytes 393224 | tf_op jit(solution)/shard_map/ppermute | solution.py:322
  62.7 6.9 %shard_map.171 = (bf16[4096,1024]{1,0:T(8,128)(2,1)}, bf16[1024,4096]{1,0:T(8,128)(2,1)}) custom-call(bf16[160,4096]{1,0:T(8,128)(2,1)S(1)} %get-tuple-element.94.x_ref, bf16[160,1024]{1,0:T(8,128)(2,1)S(1)} %get-tuple-element.95.hidden_ref, bf16[160,1024]{1,0:T(8,128)(2,1)S(1)} %get-tuple-element.96.scaled_ref, bf16[160,4096]{1,0:T(8,128)(2,1)S(1)} %get-tuple-element.97.g_ref), custom_call_target="tpu_custom_call" | custom-call | flops 2684354560 | bytes 16777216 | tf_op jit(solution)/shard_map/pallas_call | solution.py:499
  69.7 1.1 %shard_map.170 = (bf16[16,4096]{1,0:T(8,128)(2,1)}, f32[1,16]{1,0:T(1,128)}, bf16[16,4096]{1,0:T(8,128)(2,1)}) custom-call(s32[1,16]{1,0:T(1,128)S(1)} %bitcast.23, s32[1,16]{1,0:T(1,128)S(1)} %bitcast.25, f32[16,5248]{1,0:T(8,128)S(1)} %get-tuple-element.80.own_ref, bf16[8,5248]{1,0:T(8,128)(2,1)S(1)} %collective-permute-done.17.got_ref, ...), custom_call_target="tpu_custom_call" | custom-call | tf_op jit(solution)/shard_map/pallas_call | solution.py:520
  (23 shorter events, 0.2 us)
Async XLA Ops:
  2.3 12.3 %collective-permute-start = (bf16[16,5248]{1,0:T(8,128)(2,1)S(1)}, bf16[16,5248]{1,0:T(8,128)(2,1)S(1)}, u32[]{:S(2)}, u32[]{:S(2)}) collective-permute-start(bf16[16,5248]{1,0:T(8,128)(2,1)S(1)} %get-tuple-element.54), channel_id=1, source_target_pairs={{0,12},{1,13},{2,14},{3,15},{4,8},{5,9},{6,10},{7,11},{8,4},{9,5},... | collective-permute-start | bytes 503816 | tf_op jit(solution)/shard_map/ppermute | solution.py:408
  6.5 10.3 %collective-permute-start.2 = (bf16[32,4224]{1,0:T(8,128)(2,1)S(1)}, bf16[32,4224]{1,0:T(8,128)(2,1)S(1)}, u32[]{:S(2)}, u32[]{:S(2)}) collective-permute-start(bf16[32,4224]{1,0:T(8,128)(2,1)S(1)} %get-tuple-element.55.own_ref), channel_id=1, source_target_pairs={{1,2},{3,4},{5,6},{7,8},{9,10},{11,12},{13,14},{2,1},{4,3},{6,5},{... | collective-permute-start | bytes 811016 | tf_op jit(solution)/shard_map/ppermute | solution.py:322
  10.5 6.3 %collective-permute-start.1 = (bf16[32,4224]{1,0:T(8,128)(2,1)S(1)}, bf16[32,4224]{1,0:T(8,128)(2,1)S(1)}, u32[]{:S(2)}, u32[]{:S(2)}) collective-permute-start(bf16[32,4224]{1,0:T(8,128)(2,1)S(1)} %get-tuple-element.55.own_ref), channel_id=1, source_target_pairs={{0,1},{1,0},{2,3},{3,2},{4,5},{5,4},{6,7},{7,6},{8,9},{9,8},{10,11... | collective-permute-start | bytes 811016 | tf_op jit(solution)/shard_map/ppermute | solution.py:317
  16.8 14.3 %collective-permute-start.7 = (bf16[32,5248]{1,0:T(8,128)(2,1)S(1)}, bf16[32,5248]{1,0:T(8,128)(2,1)S(1)}, u32[]{:S(2)}, u32[]{:S(2)}) collective-permute-start(bf16[32,5248]{1,0:T(8,128)(2,1)S(1)} %pad_maximum_fusion), channel_id=1, source_target_pairs={{0,6},{1,7},{2,4},{3,5},{4,2},{5,3},{6,0},{7,1},{8,14},{9,15},{10,... | collective-permute-start | bytes 1007624 | tf_op jit(solution)/shard_map/ppermute | solution.py:408
  17.9 14.0 %collective-permute-start.6 = (bf16[32,5248]{1,0:T(8,128)(2,1)S(1)}, bf16[32,5248]{1,0:T(8,128)(2,1)S(1)}, u32[]{:S(2)}, u32[]{:S(2)}) collective-permute-start(bf16[32,5248]{1,0:T(8,128)(2,1)S(1)} %pad_maximum_fusion), channel_id=1, source_target_pairs={{0,4},{1,5},{2,6},{3,7},{4,0},{5,1},{6,2},{7,3},{8,12},{9,13},{10,... | collective-permute-start | bytes 1007624 | tf_op jit(solution)/shard_map/ppermute | solution.py:408
  17.9 16.0 %collective-permute-start.3 = (bf16[32,5248]{1,0:T(8,128)(2,1)S(1)}, bf16[32,5248]{1,0:T(8,128)(2,1)S(1)}, u32[]{:S(2)}, u32[]{:S(2)}) collective-permute-start(bf16[32,5248]{1,0:T(8,128)(2,1)S(1)} %pad_maximum_fusion), channel_id=1, source_target_pairs={{0,2},{1,3},{2,0},{3,1},{4,6},{5,7},{6,4},{7,5},{8,10},{9,11},{10,... | collective-permute-start | bytes 1007624 | tf_op jit(solution)/shard_map/ppermute | solution.py:408
  24.3 2.6 %collective-permute-start.4 = (f32[48,128]{1,0:T(8,128)S(1)}, f32[48,128]{1,0:T(8,128)S(1)}, u32[]{:S(2)}, u32[]{:S(2)}) collective-permute-start(f32[48,128]{1,0:T(8,128)S(1)} %shard_map.165.st_ref), channel_id=1, source_target_pairs={{0,1},{1,0},{2,3},{3,2},{4,5},{5,4},{6,7},{7,6},{8,9},{9,8},{10,11... | collective-permute-start | bytes 73736 | tf_op jit(solution)/shard_map/ppermute | solution.py:317
  26.9 7.0 %collective-permute-start.5 = (f32[96,128]{1,0:T(8,128)S(1)}, f32[96,128]{1,0:T(8,128)S(1)}, u32[]{:S(2)}, u32[]{:S(2)}) collective-permute-start(f32[96,128]{1,0:T(8,128)S(1)} %pad_maximum_fusion.1), channel_id=1, source_target_pairs={{1,2},{3,4},{5,6},{7,8},{9,10},{11,12},{13,14},{2,1},{4,3},{6,5},{... | collective-permute-start | bytes 147464 | tf_op jit(solution)/shard_map/ppermute | solution.py:322
  31.0 3.4 %collective-permute-start.8 = (bf16[32,5248]{1,0:T(8,128)(2,1)S(1)}, bf16[32,5248]{1,0:T(8,128)(2,1)S(1)}, u32[]{:S(2)}, u32[]{:S(2)}) collective-permute-start(bf16[32,5248]{1,0:T(8,128)(2,1)S(1)} %pad_maximum_fusion), channel_id=1, source_target_pairs={{0,1},{1,0},{2,3},{3,2},{4,5},{5,4},{6,7},{7,6},{8,9},{9,8},{10,11... | collective-permute-start | bytes 1007624 | tf_op jit(solution)/shard_map/ppermute | solution.py:408
  31.9 4.2 %collective-permute-start.11 = (bf16[32,5248]{1,0:T(8,128)(2,1)S(1)}, bf16[32,5248]{1,0:T(8,128)(2,1)S(1)}, u32[]{:S(2)}, u32[]{:S(2)}) collective-permute-start(bf16[32,5248]{1,0:T(8,128)(2,1)S(1)} %collective-permute-done.6), channel_id=1, source_target_pairs={{0,1},{1,0},{2,3},{3,2},{4,5},{5,4},{6,7},{7,6},{8,9},{9,8},{10,11... | collective-permute-start | bytes 1007624 | tf_op jit(solution)/shard_map/ppermute | solution.py:408
  33.8 2.3 %collective-permute-start.12 = (bf16[32,5248]{1,0:T(8,128)(2,1)S(1)}, bf16[32,5248]{1,0:T(8,128)(2,1)S(1)}, u32[]{:S(2)}, u32[]{:S(2)}) collective-permute-start(bf16[32,5248]{1,0:T(8,128)(2,1)S(1)} %collective-permute-done.7), channel_id=1, source_target_pairs={{0,1},{1,0},{2,3},{3,2},{4,5},{5,4},{6,7},{7,6},{8,9},{9,8},{10,11... | collective-permute-start | bytes 1007624 | tf_op jit(solution)/shard_map/ppermute | solution.py:408
  33.9 2.2 %collective-permute-start.10 = (bf16[32,5248]{1,0:T(8,128)(2,1)S(1)}, bf16[32,5248]{1,0:T(8,128)(2,1)S(1)}, u32[]{:S(2)}, u32[]{:S(2)}) collective-permute-start(bf16[32,5248]{1,0:T(8,128)(2,1)S(1)} %collective-permute-done.3), channel_id=1, source_target_pairs={{0,1},{1,0},{2,3},{3,2},{4,5},{5,4},{6,7},{7,6},{8,9},{9,8},{10,11... | collective-permute-start | bytes 1007624 | tf_op jit(solution)/shard_map/ppermute | solution.py:408
  34.3 1.8 %collective-permute-start.9 = (f32[96,128]{1,0:T(8,128)S(1)}, f32[96,128]{1,0:T(8,128)S(1)}, u32[]{:S(2)}, u32[]{:S(2)}) collective-permute-start(f32[96,128]{1,0:T(8,128)S(1)} %collective-permute-done.5.met_ref), channel_id=1, source_target_pairs={{0,1},{1,0},{2,3},{3,2},{4,5},{5,4},{6,7},{7,6},{8,9},{9,8},{10,11... | collective-permute-start | bytes 147464 | tf_op jit(solution)/shard_map/ppermute | solution.py:317
  45.2 24.5 %copy-start = (s32[16]{0:T(128)S(1)}, s32[16]{0:T(128)}, u32[]{:S(2)}) copy-start(s32[16]{0:T(128)} %param.20) | copy-start | bytes 196
  45.2 24.5 %copy-start.1 = (s32[16]{0:T(128)S(1)}, s32[16]{0:T(128)}, u32[]{:S(2)}) copy-start(s32[16]{0:T(128)} %param.21) | copy-start | bytes 196
  45.2 2.2 %collective-permute-start.13 = (bf16[4,16,5248]{2,1,0:T(8,128)(2,1)S(1)}, bf16[4,16,5248]{2,1,0:T(8,128)(2,1)S(1)}, u32[]{:S(2)}, u32[]{:S(2)}) collective-permute-start(bf16[4,16,5248]{2,1,0:T(8,128)(2,1)S(1)} %get-tuple-element.65), channel_id=1, source_target_pairs={{0,1},{1,0},{2,3},{3,2},{4,5},{5,4},{6,7},{7,6},{8,9},{9,8},{10,11... | collective-permute-start | bytes 2015240 | tf_op jit(solution)/shard_map/ppermute | solution.py:408
  47.6 9.7 %collective-permute-start.14 = (bf16[16,5248]{1,0:T(8,128)(2,1)S(1)}, bf16[16,5248]{1,0:T(8,128)(2,1)S(1)}, u32[]{:S(2)}, u32[]{:S(2)}) collective-permute-start(bf16[16,5248]{1,0:T(8,128)(2,1)S(1)} %get-tuple-element.77), channel_id=1, source_target_pairs={{0,2},{1,3},{2,0},{3,1},{4,6},{5,7},{6,4},{7,5},{8,10},{9,11},{10,... | collective-permute-start | bytes 503816 | tf_op jit(solution)/shard_map/ppermute | solution.py:408
  48.9 8.4 %collective-permute-start.15 = (bf16[16,5248]{1,0:T(8,128)(2,1)S(1)}, bf16[16,5248]{1,0:T(8,128)(2,1)S(1)}, u32[]{:S(2)}, u32[]{:S(2)}) collective-permute-start(bf16[16,5248]{1,0:T(8,128)(2,1)S(1)} %get-tuple-element.78), channel_id=1, source_target_pairs={{0,4},{1,5},{2,6},{3,7},{4,0},{5,1},{6,2},{7,3},{8,12},{9,13},{10,... | collective-permute-start | bytes 503816 | tf_op jit(solution)/shard_map/ppermute | solution.py:408
  49.9 7.7 %collective-permute-start.16 = (bf16[16,5248]{1,0:T(8,128)(2,1)S(1)}, bf16[16,5248]{1,0:T(8,128)(2,1)S(1)}, u32[]{:S(2)}, u32[]{:S(2)}) collective-permute-start(bf16[16,5248]{1,0:T(8,128)(2,1)S(1)} %get-tuple-element.79), channel_id=1, source_target_pairs={{0,6},{1,7},{2,4},{3,5},{4,2},{5,3},{6,0},{7,1},{8,14},{9,15},{10,... | collective-permute-start | bytes 503816 | tf_op jit(solution)/shard_map/ppermute | solution.py:408
  57.7 12.0 %collective-permute-start.17 = (bf16[8,5248]{1,0:T(8,128)(2,1)S(1)}, bf16[8,5248]{1,0:T(8,128)(2,1)S(1)}, u32[]{:S(2)}, u32[]{:S(2)}) collective-permute-start(bf16[8,5248]{1,0:T(8,128)(2,1)S(1)} %get-tuple-element.81), channel_id=1, source_target_pairs={{0,12},{1,13},{2,14},{3,15},{4,8},{5,9},{6,10},{7,11},{8,4},{9,5},... | collective-permute-start | bytes 251912 | tf_op jit(solution)/shard_map/ppermute | solution.py:408
  58.6 11.0 %collective-permute-start.18 = (bf16[16,4096]{1,0:T(8,128)(2,1)S(1)}, bf16[16,4096]{1,0:T(8,128)(2,1)S(1)}, u32[]{:S(2)}, u32[]{:S(2)}) collective-permute-start(bf16[16,4096]{1,0:T(8,128)(2,1)S(1)} %get-tuple-element.84), channel_id=1, source_target_pairs={{0,1},{1,0},{2,3},{3,2},{4,5},{5,4},{6,7},{7,6},{8,9},{9,8},{10,11... | collective-permute-start | bytes 393224 | tf_op jit(solution)/shard_map/ppermute | solution.py:317
  60.1 9.5 %collective-permute-start.19 = (bf16[16,4096]{1,0:T(8,128)(2,1)S(1)}, bf16[16,4096]{1,0:T(8,128)(2,1)S(1)}, u32[]{:S(2)}, u32[]{:S(2)}) collective-permute-start(bf16[16,4096]{1,0:T(8,128)(2,1)S(1)} %get-tuple-element.85), channel_id=1, source_target_pairs={{1,2},{3,4},{5,6},{7,8},{9,10},{11,12},{13,14},{2,1},{4,3},{6,5},{... | collective-permute-start | bytes 393224 | tf_op jit(solution)/shard_map/ppermute | solution.py:322
